TPU v7x, 32 devices: a whole 2x2x4 slice. The times are simulated.
32 devices in a mesh: dp: 16 (over z, y, x), tensor: 2 (over core).
Axes of the slice: x: 2, y: 2, z: 4, core: 2. Of those that a mesh axis runs over, the one named last changes fastest.
Arguments:
- tokens: bfloat16 [32768, 512], P(('dp', 'tensor')), may hold values from -6 to 6
- segment_ids: int32 [32, 1024], P('dp'), may hold values from 0 to 15, never falling along the last dimension, each value on 1 to 512 neighbouring positions
- padding: int32 [32, 1024], P('dp'), may hold values from 0 to 1, as said below
- mixer_gain: float32 [512], replicated, may hold values from 0.25 to 1.75
- query_weight: float32 [512, 512], P('dp', 'tensor'), may hold values from -0.75 to 0.75
- key_weight: float32 [512, 512], P('dp', 'tensor'), may hold values from -0.75 to 0.75
- value_weight: float32 [512, 512], P('dp', 'tensor'), may hold values from -0.25 to 0.25
- slot_weight: float32 [512, 512], P('dp', 'tensor'), may hold values from -0.5 to 0.5
- out_weight: float32 [512, 512], P('tensor', 'dp'), may hold values from -0.5 to 0.5
- feed_gain: float32 [512], replicated, may hold values from 0.25 to 1.75
- up_weight: float32 [512, 2048], P('dp', 'tensor'), may hold values from -0.25 to 0.25
- up_bias: float32 [2048], replicated, may hold values from -3 to 3
- down_weight: float32 [2048, 512], P('tensor', 'dp'), may hold values from -0.1875 to 0.1875
- down_bias: float32 [512], replicated, may hold values from -2 to 2
- cotangent: bfloat16 [32768, 512], P(('dp', 'tensor')), may hold values from -6 to 6
Outputs:
- layer_output: bfloat16 [32768, 512], P(('dp', 'tensor'))
- input_grad: bfloat16 [32768, 512], P(('dp', 'tensor'))
- mixer_gain_grad: float32 [512], replicated
- query_grad: float32 [512, 512], P('dp', 'tensor')
- key_grad: float32 [512, 512], P('dp', 'tensor')
- value_grad: float32 [512, 512], P('dp', 'tensor')
- slot_grad: float32 [512, 512], P('dp', 'tensor')
- out_grad: float32 [512, 512], P('tensor', 'dp')
- feed_gain_grad: float32 [512], replicated
- up_grad: float32 [512, 2048], P('dp', 'tensor')
- up_bias_grad: float32 [2048], replicated
- down_grad: float32 [2048, 512], P('tensor', 'dp')
- down_bias_grad: float32 [512], replicated
Inputs may be any that keep to these rules, and one draw needn't show every extreme that they name: `segment_ids`: within each sequence the ids never fall; each document holds 1 to 512 positions, one of them exactly that many. `padding`: in each sequence the ones form a tail, possibly empty.
All inputs are finite; a program needn't handle non-finite values.
Results may differ from a plain program's by a relative error of at most 0.04.
The roundings to bfloat16 on the way count: a program that leaves them out, or rounds other values in their place, can miss the bound.
Values may be sent and summed in bfloat16 or wider, within the bound.
A program may use at most 128 MiB of HBM per device.

v0:
```python
import math

import jax
import jax.numpy as jnp
from jax import lax
from jax.sharding import PartitionSpec as P

HEAD_DIM = 64
SLOTS = 64


highest = lax.Precision.HIGHEST


def smooth_unit(linear):
    return (
        0.5
        * linear
        * (1.0 + jnp.tanh(0.7978845608 * (linear + 0.044715 * linear * linear * linear)))
    )


def layer_norm(token_rows, gain_vec):
    row_mean = jnp.mean(token_rows, axis=-1, keepdims=True)
    centred = token_rows - row_mean
    variance = jnp.mean(centred * centred, axis=-1, keepdims=True)
    return centred * lax.rsqrt(variance + 1e-05) * gain_vec


def mixer_head(queries, key_rows, values, logits, segment, padding):
    length = queries.shape[0]
    places = jnp.arange(length)
    allowed = jnp.logical_and(
        places[None, :] <= places[:, None], segment[None, :] == segment[:, None]
    ).astype(jnp.float32)
    keep_mask = 1.0 - padding.astype(jnp.float32)
    writes = jnp.exp(logits) * keep_mask[:, None]
    pairs = jnp.dot(queries, key_rows.T, precision=highest) * allowed
    totals = jnp.dot(allowed, writes, precision=highest) + (1.0 - keep_mask)[:, None]
    scores = jnp.dot(pairs, writes, precision=highest) / (totals * math.sqrt(queries.shape[1]))
    shifted = scores - jnp.max(scores, axis=1, keepdims=True)
    powers = jnp.exp(shifted)
    chances = powers / jnp.sum(powers, axis=1, keepdims=True)
    mixing = jnp.dot(chances / totals, writes.T, precision=highest) * allowed
    return jnp.dot(mixing, values, precision=highest) * keep_mask[:, None]


def heads_first(matrix, groups, width):
    length = matrix.shape[0] // groups
    return (
        matrix.reshape(groups, length, -1, width).transpose(0, 2, 1, 3).reshape(-1, length, width)
    )


def mixer_all(queries, key_rows, values, logits, segment_ids, padding):
    groups = segment_ids.shape[0]
    length = segment_ids.shape[1]
    head_count = queries.shape[1] // HEAD_DIM
    stacked = (
        heads_first(queries, groups, HEAD_DIM),
        heads_first(key_rows, groups, HEAD_DIM),
        heads_first(values, groups, HEAD_DIM),
        heads_first(logits, groups, SLOTS),
        jnp.repeat(segment_ids, head_count, axis=0),
        jnp.repeat(padding, head_count, axis=0),
    )

    def per_head(member):
        return jax.checkpoint(mixer_head)(
            member[0], member[1], member[2], member[3], member[4], member[5]
        )

    result = lax.map(per_head, stacked)
    return (
        result.reshape(groups, head_count, length, HEAD_DIM)
        .transpose(0, 2, 1, 3)
        .reshape(groups * length, head_count * HEAD_DIM)
    )


def matmul(left, right):
    return jnp.dot(left, right, preferred_element_type=jnp.float32)


def across_rows(left, right):
    return lax.dot_general(
        left, right, (((0,), (0,)), ((), ())), preferred_element_type=jnp.float32
    )


def against(left, right):
    return lax.dot_general(
        left, right, (((1,), (1,)), ((), ())), preferred_element_type=jnp.float32
    )


def per_device(
    tokens,
    segment_ids,
    padding,
    mixer_gain,
    query_weight,
    key_weight,
    value_weight,
    slot_weight,
    out_weight,
    feed_gain,
    up_weight,
    up_bias,
    down_weight,
    down_bias,
    cotangent,
):
    query_full, key_full, value_full, slot_full, out_full = (
        lax.all_gather(query_weight.astype(jnp.bfloat16), "dp", axis=0, tiled=True),
        lax.all_gather(key_weight.astype(jnp.bfloat16), "dp", axis=0, tiled=True),
        lax.all_gather(value_weight.astype(jnp.bfloat16), "dp", axis=0, tiled=True),
        lax.all_gather(slot_weight.astype(jnp.bfloat16), "dp", axis=0, tiled=True),
        lax.all_gather(out_weight.astype(jnp.bfloat16), "dp", axis=1, tiled=True),
    )
    up_full, down_full = (
        lax.all_gather(up_weight.astype(jnp.bfloat16), "dp", axis=0, tiled=True),
        lax.all_gather(down_weight.astype(jnp.bfloat16), "dp", axis=1, tiled=True),
    )
    half_units = up_full.shape[1]
    offset = lax.axis_index("tensor") * half_units
    bias_half = lax.dynamic_slice_in_dim(up_bias, offset, half_units, 0)
    token_rows = tokens.astype(jnp.float32)
    normed_one, norm_back_one = jax.vjp(layer_norm, token_rows, mixer_gain)
    mixer_input = lax.all_gather(normed_one.astype(jnp.bfloat16), "tensor", axis=0, tiled=True)
    queries = matmul(mixer_input, query_full).astype(jnp.bfloat16)
    key_rows = matmul(mixer_input, key_full).astype(jnp.bfloat16)
    values = matmul(mixer_input, value_full).astype(jnp.bfloat16)
    logits = matmul(mixer_input, slot_full)

    def mixer_local(query_in, key_in, value_in, logit_in):
        return mixer_all(query_in, key_in, value_in, logit_in, segment_ids, padding)

    mixed, mixer_back = jax.vjp(
        mixer_local,
        queries.astype(jnp.float32),
        key_rows.astype(jnp.float32),
        values.astype(jnp.float32),
        logits,
    )
    mixed_low = mixed.astype(jnp.bfloat16)
    branch = lax.psum_scatter(
        matmul(mixed_low, out_full).astype(jnp.bfloat16), "tensor", scatter_dimension=0, tiled=True
    ).astype(jnp.float32)
    hidden = token_rows + branch
    normed_two, norm_back_two = jax.vjp(layer_norm, hidden, feed_gain)
    feed_input = lax.all_gather(normed_two.astype(jnp.bfloat16), "tensor", axis=0, tiled=True)
    linear = matmul(feed_input, up_full) + bias_half
    active_full, unit_back = jax.vjp(smooth_unit, linear)
    active = active_full.astype(jnp.bfloat16)
    feed_out = lax.psum_scatter(
        matmul(active, down_full).astype(jnp.bfloat16), "tensor", scatter_dimension=0, tiled=True
    ).astype(jnp.float32)
    layer_output = (hidden + feed_out + down_bias).astype(jnp.bfloat16)
    query_full, key_full, value_full, slot_full, out_full, up_full, down_full = (
        lax.all_gather(query_weight.astype(jnp.bfloat16), "dp", axis=0, tiled=True),
        lax.all_gather(key_weight.astype(jnp.bfloat16), "dp", axis=0, tiled=True),
        lax.all_gather(value_weight.astype(jnp.bfloat16), "dp", axis=0, tiled=True),
        lax.all_gather(slot_weight.astype(jnp.bfloat16), "dp", axis=0, tiled=True),
        lax.all_gather(out_weight.astype(jnp.bfloat16), "dp", axis=1, tiled=True),
        lax.all_gather(up_weight.astype(jnp.bfloat16), "dp", axis=0, tiled=True),
        lax.all_gather(down_weight.astype(jnp.bfloat16), "dp", axis=1, tiled=True),
    )
    grad_rows = lax.all_gather(cotangent, "tensor", axis=0, tiled=True)
    grad_active = against(grad_rows, down_full)
    grad_linear = unit_back(grad_active)[0].astype(jnp.bfloat16)
    down_local = across_rows(active, grad_rows)
    up_local = across_rows(feed_input, grad_linear)
    bias_local = jnp.sum(grad_linear.astype(jnp.float32), axis=0)
    grad_normed_two = lax.psum_scatter(
        against(grad_linear, up_full).astype(jnp.bfloat16),
        "tensor",
        scatter_dimension=0,
        tiled=True,
    ).astype(jnp.float32)
    hidden_from_norm, feed_gain_local = norm_back_two(grad_normed_two)
    grad_hidden = cotangent.astype(jnp.float32) + hidden_from_norm
    branch_grad = lax.all_gather(grad_hidden.astype(jnp.bfloat16), "tensor", axis=0, tiled=True)
    grad_mixed = against(branch_grad, out_full)
    out_local = across_rows(mixed_low, branch_grad)
    mixer_grads = mixer_back(grad_mixed)
    grad_query = mixer_grads[0].astype(jnp.bfloat16)
    grad_key = mixer_grads[1].astype(jnp.bfloat16)
    grad_value = mixer_grads[2].astype(jnp.bfloat16)
    grad_logit = mixer_grads[3].astype(jnp.bfloat16)
    query_local = across_rows(mixer_input, grad_query)
    key_local = across_rows(mixer_input, grad_key)
    value_local = across_rows(mixer_input, grad_value)
    slot_local = across_rows(mixer_input, grad_logit)
    normed_part = (
        against(grad_query, query_full)
        + against(grad_key, key_full)
        + against(grad_value, value_full)
        + against(grad_logit, slot_full)
    )
    grad_normed_one = lax.psum_scatter(
        normed_part.astype(jnp.bfloat16), "tensor", scatter_dimension=0, tiled=True
    ).astype(jnp.float32)
    up_grad, down_grad = (
        lax.psum_scatter(up_local, "dp", scatter_dimension=0, tiled=True),
        lax.psum_scatter(down_local, "dp", scatter_dimension=1, tiled=True),
    )
    query_grad, key_grad, value_grad, slot_grad, out_grad = (
        lax.psum_scatter(query_local, "dp", scatter_dimension=0, tiled=True),
        lax.psum_scatter(key_local, "dp", scatter_dimension=0, tiled=True),
        lax.psum_scatter(value_local, "dp", scatter_dimension=0, tiled=True),
        lax.psum_scatter(slot_local, "dp", scatter_dimension=0, tiled=True),
        lax.psum_scatter(out_local, "dp", scatter_dimension=1, tiled=True),
    )
    tokens_from_norm, mixer_gain_local = norm_back_one(grad_normed_one)
    input_grad = (grad_hidden + tokens_from_norm).astype(jnp.bfloat16)
    bias_full = lax.dynamic_update_slice_in_dim(
        jnp.zeros((up_bias.shape[0],), jnp.float32), bias_local, offset, 0
    )
    down_bias_local = jnp.sum(cotangent.astype(jnp.float32), axis=0)
    mixer_gain_grad, feed_gain_grad, up_bias_grad, down_bias_grad = lax.psum(
        (mixer_gain_local, feed_gain_local, bias_full, down_bias_local), ("dp", "tensor")
    )
    return (
        layer_output,
        input_grad,
        mixer_gain_grad,
        query_grad,
        key_grad,
        value_grad,
        slot_grad,
        out_grad,
        feed_gain_grad,
        up_grad,
        up_bias_grad,
        down_grad,
        down_bias_grad,
    )


def solution(mesh):
    in_specs = (
        P(("dp", "tensor"), None),
        P("dp", None),
        P("dp", None),
        P(),
        P("dp", "tensor"),
        P("dp", "tensor"),
        P("dp", "tensor"),
        P("dp", "tensor"),
        P("tensor", "dp"),
        P(),
        P("dp", "tensor"),
        P(),
        P("tensor", "dp"),
        P(),
        P(("dp", "tensor"), None),
    )
    out_specs = (
        P(("dp", "tensor"), None),
        P(("dp", "tensor"), None),
        P(),
        P("dp", "tensor"),
        P("dp", "tensor"),
        P("dp", "tensor"),
        P("dp", "tensor"),
        P("tensor", "dp"),
        P(),
        P("dp", "tensor"),
        P(),
        P("tensor", "dp"),
        P(),
    )
    return jax.shard_map(
        per_device, mesh=mesh, in_specs=in_specs, out_specs=out_specs, check_vma=False
    )
```

profile of v0, /device:TPU:1, one launch (start us, length us, event | category | flops | bytes accessed | tf_op | source)
XLA Modules:
  0.0 1569.4 jit_solution(16292875433814318425)
XLA Ops:
  14.3 38.6 %all_gather.41 = bf16[512,256]{1,0:T(8,128)(2,1)} all-gather(bf16[32,256]{1,0:T(8,128)(2,1)S(1)} %convert_element_type.188), channel_id=1, replica_groups=mesh['dp'=16,'tensor'=2] {'dp'}, dimensions={0}, use_global_device_ids=true | all-gather | bytes 278528 | tf_op jit(solution)/shard_map/all_gather | solution.py:115
  52.9 32.3 %all_gather.42 = bf16[512,256]{1,0:T(8,128)(2,1)} all-gather(bf16[32,256]{1,0:T(8,128)(2,1)S(1)} %convert_element_type.190), channel_id=1, replica_groups=mesh['dp'=16,'tensor'=2] {'dp'}, dimensions={0}, use_global_device_ids=true | all-gather | bytes 278528 | tf_op jit(solution)/shard_map/all_gather | solution.py:116
  85.2 34.2 %all_gather.44 = bf16[512,256]{1,0:T(8,128)(2,1)} all-gather(bf16[32,256]{1,0:T(8,128)(2,1)S(1)} %convert_element_type.193), channel_id=1, replica_groups=mesh['dp'=16,'tensor'=2] {'dp'}, dimensions={0}, use_global_device_ids=true | all-gather | bytes 278528 | tf_op jit(solution)/shard_map/all_gather | solution.py:117
  119.4 30.2 %all_gather.43 = bf16[512,256]{1,0:T(8,128)(2,1)S(1)} all-gather(bf16[32,256]{1,0:T(8,128)(2,1)S(1)} %convert_element_type.192), channel_id=1, replica_groups=mesh['dp'=16,'tensor'=2] {'dp'}, dimensions={0}, use_global_device_ids=true | all-gather | bytes 278528 | tf_op jit(solution)/shard_map/all_gather | solution.py:118
  149.7 34.0 %all_gather.45 = bf16[256,512]{0,1:T(8,128)(2,1)} all-gather(bf16[256,32]{0,1:T(8,128)(2,1)S(1)} %convert_element_type.199), channel_id=1, replica_groups=mesh['dp'=16,'tensor'=2] {'dp'}, dimensions={1}, use_global_device_ids=true | all-gather | bytes 278528 | tf_op jit(solution)/shard_map/all_gather | solution.py:119
  235.5 142.7 %while.32 = (s32[]{:T(128)}, bf16[8,1024,64]{1,2,0:T(8,128)(2,1)}, s32[8,1024]{1,0:T(8,128)S(1)}, f32[8,1024,64]{2,1,0:T(8,128)}, f32[8,1024,64]{2,1,0:T(8,128)}...) while((s32[]{:T(128)}, bf16[8,1024,64]{1,2,0:T(8,128)(2,1)}, ...), condition=%wide.region_5.6_spmd.clone, body=%wide.region_2.5_spmd.clone.sunk | while | flops 4038919168 | bytes 21063792 | solution.py:73
  385.5 40.1 %reduce-scatter.12.cloned.1.call-done = bf16[1024,512]{1,0:T(8,128)(2,1)} async-done(((bf16[2048,512]{1,0:T(8,128)(2,1)}), bf16[1024,512]{1,0:T(8,128)(2,1)}) %reduce-scatter.12.cloned.1.call-update) | async-done | bytes 1048592 | tf_op jit(solution)/shard_map/reduce_scatter | solution.py:147
  430.8 42.7 %all-gather.11.cloned.1.call-done = bf16[512,1024]{1,0:T(8,128)(2,1)} async-done(((bf16[32,1024]{1,0:T(8,128)(2,1)}), bf16[512,1024]{1,0:T(8,128)(2,1)}) %all-gather.11.cloned.1.call-update) | async-done | bytes 1048592 | tf_op jit(solution)/shard_map/all_gather | solution.py:122
  473.5 13.2 all-gather.9.cloned.1.call-done
  486.7 10.4 multiply_convert_fusion
  497.1 48.0 %all-gather.13.cloned.1.call-done = bf16[1024,512]{0,1:T(8,128)(2,1)} async-done(((bf16[1024,32]{0,1:T(8,128)(2,1)}), bf16[1024,512]{0,1:T(8,128)(2,1)}) %all-gather.13.cloned.1.call-update) | async-done | bytes 1048592 | tf_op jit(solution)/shard_map/all_gather | solution.py:123
  545.1 12.8 all-gather.15.cloned.1.call-done
  557.9 12.3 convert_reduce_fusion.1
  576.0 6.3 convolution_convert_fusion.1
  590.0 9.9 reduce-scatter.14.cloned.1.call-done
  606.0 11.7 all-gather.17.cloned.1.call-done
  628.5 376.4 %while.31 = (s32[]{:T(128)}, bf16[8,1024,64]{1,2,0:T(8,128)(2,1)S(1)}, bf16[8,1024,64]{1,2,0:T(8,128)(2,1)}, bf16[8,1024,64]{1,2,0:T(8,128)(2,1)}, bf16[8,1024,6...) while((s32[]{:T(128)}, ...), condition=%wide.region_19.20_spmd, body=%wide.region_13.19_spmd.sunk | while | flops 10506472448 | bytes 61333680 | solution.py:73
  1054.8 42.3 %all-reduce = (f32[512]{0:T(512)}, f32[512]{0:T(512)}, f32[2048]{0:T(1024)}, f32[512]{0:T(512)}) all-reduce(f32[512]{0:T(512)S(1)} %get-tuple-element.353, f32[512]{0:T(512)S(1)} %copy-done.42, f32[2048]{0:T(1024)S(1)} %dynamic_update_slice.43, f32[512]{0:T(512)S(1)} %get-tuple-element.416), channel_id=1, replica_groups=mesh['dp'=16,'tensor'=2] {'dp','tensor'}, use_global_device_ids=true, to_apply=%region_24.25 | all-reduce | flops 3584 | bytes 28672 | tf_op jit(solution)/shard_map/psum | solution.py:221
  1103.0 79.7 %reduce-scatter.32.cloned.1.call-done = f32[1024,32]{0,1:T(8,128)} async-done(((f32[1024,512]{0,1:T(8,128)}), f32[1024,32]{0,1:T(8,128)}) %reduce-scatter.32.cloned.1.call-update) | async-done | bytes 131088 | tf_op jit(solution)/shard_map/reduce_scatter | solution.py:206
  1182.6 76.3 %reduce-scatter.28.cloned.1.call-done = f32[256,32]{0,1:T(8,128)} async-done(((f32[256,512]{0,1:T(8,128)}), f32[256,32]{0,1:T(8,128)}) %reduce-scatter.28.cloned.1.call-update) | async-done | bytes 32784 | tf_op jit(solution)/shard_map/reduce_scatter | solution.py:213
  1259.0 76.1 %reduce-scatter.20.cloned.1.call-done = f32[32,256]{1,0:T(8,128)} async-done(((f32[512,256]{1,0:T(8,128)}), f32[32,256]{1,0:T(8,128)}) %reduce-scatter.20.cloned.1.call-update) | async-done | bytes 32784 | tf_op jit(solution)/shard_map/reduce_scatter | solution.py:209
  1335.0 75.4 %reduce-scatter.22.cloned.1.call-done = f32[32,256]{1,0:T(8,128)} async-done(((f32[512,256]{1,0:T(8,128)}), f32[32,256]{1,0:T(8,128)}) %reduce-scatter.22.cloned.1.call-update) | async-done | bytes 32784 | tf_op jit(solution)/shard_map/reduce_scatter | solution.py:210
  1410.4 75.8 %reduce-scatter.24.cloned.1.call-done = f32[32,256]{1,0:T(8,128)} async-done(((f32[512,256]{1,0:T(8,128)}), f32[32,256]{1,0:T(8,128)}) %reduce-scatter.24.cloned.1.call-update) | async-done | bytes 32784 | tf_op jit(solution)/shard_map/reduce_scatter | solution.py:211
  1486.2 75.6 %reduce-scatter.26.cloned.1.call-done = f32[32,256]{1,0:T(8,128)} async-done(((f32[512,256]{1,0:T(8,128)}), f32[32,256]{1,0:T(8,128)}) %reduce-scatter.26.cloned.1.call-update) | async-done | bytes 32784 | tf_op jit(solution)/shard_map/reduce_scatter | solution.py:212
  (478 shorter events, 642.9 us)
Async XLA Ops:
  8.0 4.6 copy-start
  8.0 175.7 %all-gather.7.cloned.1.call-start = ((), (), s32[]{:S(2)}) async-start(), calls=%async_computation.11 | async-start | bytes 3145728 | tf_op jit(solution)/shard_map/all_gather | solution.py:130
  14.0 411.5 %reduce-scatter.12.cloned.1.call-start = ((), (), s32[]{:S(2)}) async-start(), calls=%async_computation.12 | async-start | bytes 3145728 | tf_op jit(solution)/shard_map/reduce_scatter | solution.py:147
  149.7 76.4 %copy-start.18 = (bf16[512,256]{1,0:T(8,128)(2,1)}, bf16[512,256]{1,0:T(8,128)(2,1)S(1)}, u32[]{:S(2)}) copy-start(bf16[512,256]{1,0:T(8,128)(2,1)S(1)} %all_gather.43) | copy-start | bytes 786436
  191.8 5.0 copy-start.2
  384.7 88.8 %all-gather.11.cloned.1.call-start = ((), (), s32[]{:S(2)}) async-start(), calls=%async_computation.14 | async-start | bytes 1114112 | tf_op jit(solution)/shard_map/all_gather | solution.py:122
  385.4 42.4 %copy-start.41 = (f32[512]{0:T(512)S(1)}, f32[512]{0:T(512)}, u32[]{:S(2)}) copy-start(f32[512]{0:T(512)} %param.28) | copy-start | bytes 6148
  385.4 101.3 %all-gather.9.cloned.1.call-start = ((), (), s32[]{:S(2)}) async-start(), calls=%async_computation.13 | async-start | bytes 3145728 | tf_op jit(solution)/shard_map/all_gather | solution.py:152
  429.3 115.8 %all-gather.13.cloned.1.call-start = ((), (), s32[]{:S(2)}) async-start(), calls=%async_computation.15 | async-start | bytes 1114112 | tf_op jit(solution)/shard_map/all_gather | solution.py:123
  430.0 127.9 %all-gather.15.cloned.1.call-start = ((), (), s32[]{:S(2)}) async-start(), calls=%async_computation.17 | async-start | bytes 3145728 | tf_op jit(solution)/shard_map/all_gather | solution.py:169
  430.8 156.2 %reduce-scatter.16.cloned.1.call-start = ((), (), s32[]{:S(2)}) async-start(), calls=%async_computation.18 | async-start | bytes 3145728 | tf_op jit(solution)/shard_map/reduce_scatter | solution.py:175
  557.9 14.3 copy-start.50
  576.0 23.9 %reduce-scatter.14.cloned.1.call-start = ((), (), s32[]{:S(2)}) async-start(), calls=%async_computation.16 | async-start | bytes 3145728 | tf_op jit(solution)/shard_map/reduce_scatter | solution.py:156
  582.3 17.6 %copy-start.46 = (f32[512]{0:T(512)S(1)}, f32[512]{0:T(512)}, u32[]{:S(2)}) copy-start(f32[512]{0:T(512)} %param.32) | copy-start | bytes 6148
  582.4 35.3 %all-gather.17.cloned.1.call-start = ((), (), s32[]{:S(2)}) async-start(), calls=%async_computation.19 | async-start | bytes 3145728 | tf_op jit(solution)/shard_map/all_gather | solution.py:183
  590.0 14.6 copy-start.8
  605.9 442.2 %reduce-scatter.18.cloned.1.call-start = ((), (), s32[]{:S(2)}) async-start(), calls=%async_computation.20 | async-start | bytes 3145728 | tf_op jit(solution)/shard_map/reduce_scatter | solution.py:201
  1018.2 84.8 %reduce-scatter.30.cloned.1.call-start = ((), (), s32[]{:S(2)}) async-start(), calls=%async_computation.26 | async-start | bytes 2228224 | tf_op jit(solution)/shard_map/reduce_scatter | solution.py:205
  1025.6 157.0 %reduce-scatter.32.cloned.1.call-start = ((), (), s32[]{:S(2)}) async-start(), calls=%async_computation.27 | async-start | bytes 2228224 | tf_op jit(solution)/shard_map/reduce_scatter | solution.py:206
  1033.5 225.4 %reduce-scatter.28.cloned.1.call-start = ((), (), s32[]{:S(2)}) async-start(), calls=%async_computation.25 | async-start | bytes 557056 | tf_op jit(solution)/shard_map/reduce_scatter | solution.py:213
  1037.4 297.6 %reduce-scatter.20.cloned.1.call-start = ((), (), s32[]{:S(2)}) async-start(), calls=%async_computation.21 | async-start | bytes 557056 | tf_op jit(solution)/shard_map/reduce_scatter | solution.py:209
  1040.3 370.1 %reduce-scatter.22.cloned.1.call-start = ((), (), s32[]{:S(2)}) async-start(), calls=%async_computation.22 | async-start | bytes 557056 | tf_op jit(solution)/shard_map/reduce_scatter | solution.py:210
  1043.2 443.1 %reduce-scatter.24.cloned.1.call-start = ((), (), s32[]{:S(2)}) async-start(), calls=%async_computation.23 | async-start | bytes 557056 | tf_op jit(solution)/shard_map/reduce_scatter | solution.py:211
  1044.8 517.0 %reduce-scatter.26.cloned.1.call-start = ((), (), s32[]{:S(2)}) async-start(), calls=%async_computation.24 | async-start | bytes 557056 | tf_op jit(solution)/shard_map/reduce_scatter | solution.py:212
  (45 other events, 117.6 us)
Sparse Core Ops, SparseCore 0:
  14.1 13.0 all-gather.6
  384.8 40.6 reduce-scatter.11
  576.1 10.8 reduce-scatter.15
  589.1 10.7 reduce-scatter.13
Sparse Core Ops, SparseCore 1:
  388.9 84.6 all-gather.10
  475.6 11.1 all-gather.8
  490.3 54.7 all-gather.12
  546.7 11.1 all-gather.14
  606.0 11.6 all-gather.16
  1018.2 10.7 reduce-scatter.17
  1031.8 71.2 reduce-scatter.29
  1105.7 76.9 reduce-scatter.31
  1185.3 73.6 reduce-scatter.27
  1261.9 73.1 reduce-scatter.19
  1337.7 72.6 reduce-scatter.21
  1413.4 72.8 reduce-scatter.23
  1488.9 72.9 reduce-scatter.25
where the time goes:
time: 1590 us; the launch traced here: 1570 us
  waiting for transfers between devices  649 us (41%)
  matrix products  535 us (34%)
  blocking collectives  212 us (13%)
  local copies, waits for them, and re-layouts  97.6 us (6%)
  loops' own time  32.1 us (2%)
  other arithmetic  26.5 us (2%)
  between operations  16.6 us (1%)
    dot_general x32, matrix products, mixer_head(): pairs = jnp.dot(queries, key_rows.T, precision=highest) * allowed  117 us
    dot_general x32, matrix products, mixer_head(): jnp.dot(pairs, writes, precision=highest)  110 us
    dot_general x32, matrix products, mixer_head(): mixing = jnp.dot(chances / totals, writes.T, precision=highest) * allowed  100 us
    dot_general x24, matrix products, mixer_head(): return jnp.dot(mixing, values, precision=highest) * keep_mask[:, None]  89.6 us
    reduce_scatter x1, waiting for transfers between devices, per_device(): lax.psum_scatter(down_local, 'dp', scatter_dimension=1, tiled=True)  79.7 us
    reduce_scatter x1, waiting for transfers between devices, per_device(): lax.psum_scatter(out_local, 'dp', scatter_dimension=1, tiled=True)  76.3 us
    reduce_scatter x1, waiting for transfers between devices, per_device(): lax.psum_scatter(query_local, 'dp', scatter_dimension=0, tiled=True)  76.1 us
    reduce_scatter x1, waiting for transfers between devices, per_device(): lax.psum_scatter(value_local, 'dp', scatter_dimension=0, tiled=True)  75.8 us
  transfers between devices with their start and end apart: 17, of which 15 were waited for; matrix products, arithmetic and copies ran while one was open for 4% of the time, Pallas kernels for 0%

commit v1 on v0

v1 whole, which is shorter than its diff:
```python
import functools
import math

import jax
import jax.numpy as jnp
from jax import lax
from jax.experimental import pallas as pl
from jax.experimental.pallas import tpu as pltpu
from jax.sharding import PartitionSpec as P

HEAD_DIM = 64
SLOTS = 64
CHUNK = 128
GROUP = 256
TILE = 256

F32 = jnp.float32
BF16 = jnp.bfloat16
MESH = pl.DeviceIdType.MESH


def dot(left, right):
    return lax.dot_general(left, right, (((1,), (0,)), ((), ())), preferred_element_type=F32)


def dot_rt(left, right):
    return lax.dot_general(left, right, (((1,), (1,)), ((), ())), preferred_element_type=F32)


def dot_lt(left, right):
    return lax.dot_general(left, right, (((0,), (0,)), ((), ())), preferred_element_type=F32)


def twice(block):
    return jnp.concatenate([block, block], axis=1)


def four(block):
    return jnp.concatenate([block, block, block, block], axis=1)


def standardise(rows):
    centred = rows - jnp.mean(rows, axis=-1, keepdims=True)
    scale = lax.rsqrt(jnp.mean(centred * centred, axis=-1, keepdims=True) + 1e-05)
    return centred * scale, scale


def head_stack(block):
    lane = lax.broadcasted_iota(jnp.int32, block.shape, 1) // HEAD_DIM
    zero = jnp.zeros_like(block)
    return jnp.concatenate([jnp.where(lane == h, block, zero) for h in range(4)], axis=0)


def head_blocks():
    row = lax.broadcasted_iota(jnp.int32, (GROUP, GROUP), 0) // HEAD_DIM
    column = lax.broadcasted_iota(jnp.int32, (GROUP, GROUP), 1) // HEAD_DIM
    return row == column


def head_sum(block, ones):
    high = block.astype(BF16)
    low = (block - high.astype(F32)).astype(BF16)
    return dot(high, ones) + dot(low, ones)


def head_max(block):
    halves = []
    lane = lax.broadcasted_iota(jnp.int32, (block.shape[0], 128), 1) < HEAD_DIM
    for j in range(block.shape[1] // 128):
        part = block[:, j * 128 : (j + 1) * 128]
        first = jnp.max(jnp.where(lane, part, -jnp.inf), axis=1, keepdims=True)
        second = jnp.max(jnp.where(lane, -jnp.inf, part), axis=1, keepdims=True)
        halves.append(jnp.where(lane, first, second))
    return jnp.concatenate(halves, axis=1)


def rows_to_columns(seg_row, pad_row, segc, keepc, length):
    segc[pl.ds(0, 8), :] = jnp.full((8, 128), -1.0, F32)
    segc[pl.ds(8 + length, 8), :] = jnp.full((8, 128), -2.0, F32)
    for c in range(length // CHUNK):
        here = slice(c * CHUNK, (c + 1) * CHUNK)
        seg = jnp.broadcast_to(seg_row[:, here].astype(F32), (CHUNK, CHUNK))
        pad = jnp.broadcast_to(pad_row[:, here].astype(F32), (CHUNK, CHUNK))
        segc[pl.ds(8 + c * CHUNK, CHUNK), :] = seg.T
        keepc[pl.ds(c * CHUNK, CHUNK), :] = 1.0 - pad.T


def project(r, tok, gain, wa, keepc, n1, q, k, v, w):
    rows = pl.ds(pl.multiple_of(r * TILE, TILE), TILE)
    xhat, _ = standardise(tok[rows, :].astype(F32))
    normed = (xhat * gain[...]).astype(BF16)
    n1[rows, :] = normed
    keep = twice(keepc[rows, :])
    for g in range(2):
        out = dot(normed, wa[g])
        q[g, rows, :] = out[:, 0:256].astype(BF16)
        k[g, rows, :] = out[:, 256:512].astype(BF16)
        v[g, rows, :] = out[:, 512:768].astype(BF16)
        w[g, rows, :] = (jnp.exp(out[:, 768:1024]) * keep).astype(BF16)


def chunk_masks(c, segc):
    base = pl.multiple_of(c * CHUNK, CHUNK)
    seg = segc[pl.ds(base + 8, CHUNK), :]
    across = seg.T
    row = lax.broadcasted_iota(jnp.int32, (CHUNK, CHUNK), 0)
    column = lax.broadcasted_iota(jnp.int32, (CHUNK, CHUNK), 1)
    same = seg == across
    causal = jnp.where(same & (column <= row), 1.0, 0.0)
    anti = jnp.where(same & (row <= column), 1.0, 0.0)
    before = segc[pl.ds(base + 7, 1), :]
    first = segc[pl.ds(base + 8, 1), :]
    last = segc[pl.ds(base + 7 + CHUNK, 1), :]
    after = segc[pl.ds(base + 8 + CHUNK, 1), :]
    one = lambda test: jnp.where(test, 1.0, 0.0)
    return causal, anti, dict(
        from_before=one(seg == before),
        to_after=one(seg == last),
        from_after=one(seg == after),
        to_before=one(seg == first),
        carry_on=one(before == last),
        carry_back=one(after == first),
    )


def mix_forward(c, segc, keepc, q, k, v, w, probs, inv, score, mixed, kw, wv, zsum, kw_all, wv_all):
    rows = pl.ds(pl.multiple_of(c * CHUNK, CHUNK), CHUNK)
    causal, _, edge = chunk_masks(c, segc)
    causal4 = four(causal)
    causal_low = causal.astype(BF16)
    blocks = head_blocks()
    ones = jnp.where(blocks, 1.0, 0.0).astype(BF16)
    keep = twice(keepc[rows, :])
    come = twice(edge["from_before"])
    come_low = come.astype(BF16)
    go_low = twice(edge["to_after"]).astype(BF16)
    carry = twice(edge["carry_on"])
    for g in range(2):
        qc, kc, vc, wc = q[g, rows, :], k[g, rows, :], v[g, rows, :], w[g, rows, :]
        kw_low, wv_low = kw[g].astype(BF16), wv[g].astype(BF16)
        kw_all[c, g] = kw_low
        wv_all[c, g] = wv_low
        ws = head_stack(wc)
        pairs = (dot_rt(qc, head_stack(kc)) * causal4).astype(BF16)
        total = dot(causal_low, wc) + come * zsum[g, 0:1, :] + (1.0 - keep)
        inverse = 1.0 / total
        scores = (dot(pairs, ws) + dot(qc * come_low, kw_low)) * (inverse * (HEAD_DIM**-0.5))
        powers = jnp.exp(scores - head_max(scores))
        chances = powers / head_sum(powers, ones)
        ratio = (chances * inverse).astype(BF16)
        probs[g, rows, :] = chances
        inv[g, rows, :] = inverse
        score[g, rows, :] = scores
        mixing = (dot_rt(ratio, ws) * causal4).astype(BF16)
        out = dot(mixing, head_stack(vc)) + dot(ratio * come_low, wv_low)
        mixed[rows, g * GROUP : (g + 1) * GROUP] = (out * keep).astype(BF16)
        wg = wc * go_low
        kw[g] = kw[g] * carry[0:1, :] + jnp.where(blocks, dot_lt(kc, wg), 0.0)
        wv[g] = wv[g] * carry[0:1, :] + jnp.where(blocks, dot_lt(wg, vc), 0.0)
        added = jnp.sum(wg.astype(F32), axis=0, keepdims=True)
        zsum[g] = zsum[g] * carry[0:1, :] + added


def mix_backward(
    c, segc, keepc, q, k, v, w, probs, inv, score, gm, kw_all, wv_all, rg, uq, zgrad, gy
):
    rows = pl.ds(pl.multiple_of(c * CHUNK, CHUNK), CHUNK)
    causal, anti, edge = chunk_masks(c, segc)
    causal4, anti4 = four(causal), four(anti)
    anti_low = anti.astype(BF16)
    blocks = head_blocks()
    ones = jnp.where(blocks, 1.0, 0.0).astype(BF16)
    come_low = twice(edge["from_before"]).astype(BF16)
    late = twice(edge["from_after"])
    late_low = late.astype(BF16)
    back = twice(edge["to_before"])
    back_low = back.astype(BF16)
    carry = twice(edge["carry_back"])
    for g in range(2):
        qc, kc, vc, wc = q[g, rows, :], k[g, rows, :], v[g, rows, :], w[g, rows, :]
        grad = gm[g, rows, :]
        chances, inverse, scores = probs[g, rows, :], inv[g, rows, :], score[g, rows, :]
        ratio = (chances * inverse).astype(BF16)
        ws, grads, ratios = head_stack(wc), head_stack(grad), head_stack(ratio)
        d_mixing = (dot_rt(grad, head_stack(vc)) * causal4).astype(BF16)
        d_ratio = dot(d_mixing, ws) + dot_rt(grad * come_low, wv_all[c, g])
        d_chance = d_ratio * inverse
        weighted = d_chance * chances
        d_score = chances * d_chance - chances * head_sum(weighted, ones)
        d_pw = (d_score * inverse * (HEAD_DIM**-0.5)).astype(BF16)
        d_total = (weighted + d_score * scores) * inverse
        d_pairs = (dot_rt(d_pw, ws) * causal4).astype(BF16)
        gq = dot(d_pairs, head_stack(kc)) + dot_rt(d_pw * come_low, kw_all[c, g])
        rg_low, uq_low = rg[g].astype(BF16), uq[g].astype(BF16)
        d_pws = head_stack(d_pw)
        mixing_t = (dot_rt(wc, ratios) * anti4).astype(BF16)
        w_late = wc * late_low
        gv = dot(mixing_t, grads) + dot(w_late, rg_low)
        d_pairs_t = (dot_rt(wc, d_pws) * anti4).astype(BF16)
        gk = dot(d_pairs_t, head_stack(qc)) + dot(w_late, uq_low)
        d_mixing_t = (dot_rt(vc, grads) * anti4).astype(BF16)
        pairs_t = (dot_rt(kc, head_stack(qc)) * anti4).astype(BF16)
        z_high = d_total.astype(BF16)
        z_low = (d_total - z_high.astype(F32)).astype(BF16)
        dw = dot(d_mixing_t, ratios) + dot(pairs_t, d_pws)
        dw += dot_rt(vc * late_low, rg_low) + dot_rt(kc * late_low, uq_low)
        dw -= dot(anti_low, z_high) + dot(anti_low, z_low) + late * zgrad[g, 0:1, :]
        gy[g, rows, 0:256] = gq.astype(BF16)
        gy[g, rows, 256:512] = gk.astype(BF16)
        gy[g, rows, 512:768] = gv.astype(BF16)
        gy[g, rows, 768:1024] = (dw * wc.astype(F32)).astype(BF16)
        rg[g] = rg[g] * carry[0:1, :] + jnp.where(blocks, dot_lt(ratio * back_low, grad), 0.0)
        uq[g] = uq[g] * carry[0:1, :] + jnp.where(blocks, dot_lt(d_pw * back_low, qc), 0.0)
        zgrad[g] = zgrad[g] * carry[0:1, :] + jnp.sum(d_total * back, axis=0, keepdims=True)


def feed(
    r, tok, cot, gain, up_bias, down_bias, wb, keepc, mixed, n2, act, lin, xhat, gh, gb, gm, small, out
):
    rows = pl.ds(pl.multiple_of(r * TILE, TILE), TILE)
    hidden = tok[rows, :].astype(F32)
    for g in range(2):
        hidden += dot_rt(mixed[rows, g * GROUP : (g + 1) * GROUP], wb[g, :, 0:256])
    hat, scale = standardise(hidden)
    xhat[...] = hat
    normed = (hat * gain[...]).astype(BF16)
    n2[rows, :] = normed
    grad = cot[rows, :]
    k0 = 0.7978845608
    k1 = k0 * 0.044715
    total = hidden + down_bias[...]
    back = jnp.zeros((TILE, 512), F32)
    for g in range(2):
        for j in range(4):
            here = slice(j * 256, (j + 1) * 256)
            unit = g * 1024 + j * 256
            up = wb[g, :, 256 + j * 256 : 512 + j * 256]
            down = wb[g, :, 1280 + j * 256 : 1536 + j * 256]
            linear = dot(normed, up) + up_bias[:, unit : unit + 256]
            square = linear * linear
            gate = 0.5 * jnp.tanh(linear * (square * k1 + k0)) + 0.5
            active = linear * gate
            slope = gate + active * (1.0 - gate) * (square * (6.0 * k1) + 2.0 * k0)
            active_low = active.astype(BF16)
            grad_low = (dot(grad, down) * slope).astype(BF16)
            act[g, rows, here] = active_low
            lin[g, rows, here] = grad_low
            small[4:5, unit : unit + 256] += jnp.sum(grad_low.astype(F32), axis=0, keepdims=True)
    for g in range(2):
        total += dot_rt(act[g, rows, :], wb[g, :, 1280:2304])
        back += dot_rt(lin[g, rows, :], wb[g, :, 256:1280])
    out[rows, :] = total.astype(BF16)
    hat = xhat[...]
    scaled = back * gain[...]
    inner = scaled - jnp.mean(scaled, axis=-1, keepdims=True)
    inner -= hat * jnp.mean(scaled * hat, axis=-1, keepdims=True)
    grad_f32 = grad.astype(F32)
    grad_hidden = grad_f32 + scale * inner
    gh[rows, :] = grad_hidden
    low = grad_hidden.astype(BF16)
    gb[rows, :] = low
    small[0:1, 0:512] += jnp.sum(back * hat, axis=0, keepdims=True)
    small[2:3, 0:512] += jnp.sum(grad_f32, axis=0, keepdims=True)
    keep = twice(keepc[rows, :])
    for g in range(2):
        gm[g, rows, :] = (dot(low, wb[g, :, 0:256]) * keep).astype(BF16)


def transpose_into(source, target, length):
    for r in range(length // TILE):
        target[:, r * TILE : (r + 1) * TILE] = source[r * TILE : (r + 1) * TILE, :].T


def weight_grad(left_t, right, target, target_column, columns):
    def step(j, carry):
        here = pl.ds(pl.multiple_of(j * 256, 256), 256)
        there = pl.ds(pl.multiple_of(target_column + j * 256, 256), 256)
        target[:, there] = dot(left_t[...], right[:, here]).astype(BF16)
        return carry

    lax.fori_loop(0, columns // 256, step, 0)


def finish(r, tok, gain, wa, gy, gh, small, grad_out):
    rows = pl.ds(pl.multiple_of(r * TILE, TILE), TILE)
    hat, scale = standardise(tok[rows, :].astype(F32))
    back = dot_rt(gy[0, rows, :], wa[0]) + dot_rt(gy[1, rows, :], wa[1])
    scaled = back * gain[...]
    inner = scaled - jnp.mean(scaled, axis=-1, keepdims=True)
    inner -= hat * jnp.mean(scaled * hat, axis=-1, keepdims=True)
    grad_out[rows, :] = (gh[rows, :] + scale * inner).astype(BF16)
    small[1:2, 0:512] += jnp.sum(back * hat, axis=0, keepdims=True)


def layer_kernel(
    length,
    tok,
    cot,
    seg_row,
    pad_row,
    gain_one,
    gain_two,
    up_bias,
    down_bias,
    wa,
    wb,
    out,
    grad_out,
    ga,
    gw,
    small,
    segc,
    keepc,
    n1,
    q,
    k,
    v,
    w,
    probs,
    inv,
    score,
    mixed,
    kw,
    wv,
    zsum,
    kw_all,
    wv_all,
    n2,
    act,
    lin,
    xhat,
    gh,
    gb,
    gm,
    flip,
):
    chunks, tiles = length // CHUNK, length // TILE
    small[...] = jnp.zeros_like(small)
    rows_to_columns(seg_row, pad_row, segc, keepc, length)

    @pl.loop(0, tiles)
    def _(r):
        project(r, tok, gain_one, wa, keepc, n1, q, k, v, w)

    kw[...] = jnp.zeros_like(kw)
    wv[...] = jnp.zeros_like(wv)
    zsum[...] = jnp.zeros_like(zsum)

    @pl.loop(0, chunks)
    def _(c):
        mix_forward(
            c, segc, keepc, q, k, v, w, probs, inv, score, mixed, kw, wv, zsum, kw_all, wv_all
        )

    @pl.loop(0, tiles)
    def _(r):
        feed(
            r, tok, cot, gain_two, up_bias, down_bias, wb, keepc, mixed, n2, act, lin, xhat, gh, gb,
            gm, small, out,
        )

    transpose_into(cot, flip, length)
    for g in range(2):
        weight_grad(flip, act.at[g], gw.at[g], 1280, 1024)
    transpose_into(n2, flip, length)
    for g in range(2):
        weight_grad(flip, lin.at[g], gw.at[g], 256, 1024)
    transpose_into(gb, flip, length)
    for g in range(2):
        gw[g, :, 0:256] = dot(flip[...], mixed[:, g * GROUP : (g + 1) * GROUP]).astype(BF16)

    kw[...] = jnp.zeros_like(kw)
    wv[...] = jnp.zeros_like(wv)
    zsum[...] = jnp.zeros_like(zsum)

    @pl.loop(0, chunks)
    def _(i):
        mix_backward(
            chunks - 1 - i, segc, keepc, q, k, v, w, probs, inv, score, gm, kw_all, wv_all, kw, wv,
            zsum, act,
        )

    transpose_into(n1, flip, length)
    for g in range(2):
        weight_grad(flip, act.at[g], ga.at[g], 0, 1024)

    @pl.loop(0, tiles)
    def _(r):
        finish(r, tok, gain_one, wa, act, gh, small, grad_out)


def layer(tokens, cotangent, seg_row, pad_row, gain_one, gain_two, up_bias, down_bias, wa, wb):
    length, width = tokens.shape
    chunks = length // CHUNK
    shape = jax.ShapeDtypeStruct
    vmem = pltpu.VMEM
    return pl.pallas_call(
        functools.partial(layer_kernel, length),
        out_shape=(
            shape((length, width), BF16),
            shape((length, width), BF16),
            shape(wa.shape, BF16),
            shape(wb.shape, BF16),
            shape((8, 2048), F32),
        ),
        in_specs=[pl.BlockSpec(memory_space=pltpu.VMEM)] * 10,
        out_specs=tuple([pl.BlockSpec(memory_space=pltpu.VMEM)] * 5),
        scratch_shapes=[
            vmem((length + 16, 128), F32),
            vmem((length, 128), F32),
            vmem((length, width), BF16),
            vmem((2, length, GROUP), BF16),
            vmem((2, length, GROUP), BF16),
            vmem((2, length, GROUP), BF16),
            vmem((2, length, GROUP), BF16),
            vmem((2, length, GROUP), F32),
            vmem((2, length, GROUP), F32),
            vmem((2, length, GROUP), F32),
            vmem((length, width), BF16),
            vmem((2, GROUP, GROUP), F32),
            vmem((2, GROUP, GROUP), F32),
            vmem((2, 8, GROUP), F32),
            vmem((chunks, 2, GROUP, GROUP), BF16),
            vmem((chunks, 2, GROUP, GROUP), BF16),
            vmem((length, width), BF16),
            vmem((2, length, 1024), BF16),
            vmem((2, length, 1024), BF16),
            vmem((TILE, width), F32),
            vmem((length, width), F32),
            vmem((length, width), BF16),
            vmem((2, length, GROUP), BF16),
            vmem((width, length), BF16),
        ],
        compiler_params=pltpu.CompilerParams(vmem_limit_bytes=60 * 1024 * 1024),
        name="layer",
    )(tokens, cotangent, seg_row, pad_row, gain_one, gain_two, up_bias, down_bias, wa, wb)


class Place:
    def __init__(self, depth):
        index = lax.axis_index("dp")
        self.depth = depth
        self.x = lax.rem(index, 2)
        self.y = lax.rem(index // 2, 2)
        self.z = index // 4
        self.t = lax.axis_index("tensor")

    def chip(self, z, y, x):
        return {"dp": (z * 2 + y) * 2 + x}

    def above(self, step):
        return lax.rem(self.z + step, self.depth)

    def x_side(self):
        return self.chip(self.z, self.y, 1 - self.x)

    def y_side(self):
        return self.chip(self.z, 1 - self.y, self.x)

    def core(self):
        return {"tensor": 1 - self.t}

    def friends(self):
        others = [self.chip(self.above(s), self.y, self.x) for s in range(1, self.depth)]
        return [self.core(), self.x_side(), self.y_side()] + others

    def greet(self):
        barrier = pltpu.get_barrier_semaphore()
        friends = self.friends()
        for friend in friends:
            pl.semaphore_signal(barrier, inc=1, device_id=friend, device_id_type=MESH)
        pl.semaphore_wait(barrier, len(friends))


def send(source, target, sems, number, device):
    copy = pltpu.make_async_remote_copy(
        src_ref=source,
        dst_ref=target,
        send_sem=sems.at[0, number],
        recv_sem=sems.at[1, number],
        device_id=device,
        device_id_type=MESH,
    )
    copy.start()
    return copy


class Gather:
    COPIES = 16

    def __init__(self, place, full, sems):
        self.p, self.full, self.sems = place, full, sems
        self.copies = []
        self.count = 0

    def push(self, index, device):
        part = self.full.at[index]
        copy = send(part, part, self.sems, self.count, device)
        self.count += 1
        self.copies.append(copy)
        return copy

    def first(self):
        p = self.p
        own = (p.t, p.z, p.y, p.x)
        self.along_z = [self.push(own, p.chip(p.above(s), p.y, p.x)) for s in range(1, p.depth)]

    def second(self):
        p = self.p
        for copy in self.along_z:
            copy.wait_recv()
        every = slice(None)
        self.one = [
            self.push((p.t, every, p.y, p.x, 0), p.x_side()),
            self.push((p.t, every, p.y, p.x, 1), p.y_side()),
        ]
        self.pair = [self.push((p.t, every, p.y, p.x), p.core())]

    def third(self):
        p = self.p
        every = slice(None)
        self.one[0].wait_recv()
        self.two = [self.push((p.t, every, p.y, every, 0), p.y_side())]
        self.one[1].wait_recv()
        self.two += [self.push((p.t, every, every, p.x, 1), p.x_side())]
        self.pair += [
            self.push((p.t, every, p.y, 1 - p.x, 0), p.core()),
            self.push((p.t, every, 1 - p.y, p.x, 1), p.core()),
        ]

    def fourth(self):
        p = self.p
        every = slice(None)
        self.two[0].wait_recv()
        self.pair += [self.push((p.t, every, 1 - p.y, every, 0), p.core())]
        self.two[1].wait_recv()
        self.pair += [self.push((p.t, every, every, 1 - p.x, 1), p.core())]

    def last(self):
        for copy in self.pair:
            copy.wait_recv()
        for copy in self.copies:
            copy.wait_send()


def gather_kernel(depth, own_a, own_b, full_a, full_b, sems_a, sems_b):
    place = Place(depth)
    mine = (place.t, place.z, place.y, place.x)
    full_a[mine] = own_a[...]
    full_b[mine] = own_b[...]
    place.greet()
    one, two = Gather(place, full_a, sems_a), Gather(place, full_b, sems_b)
    one.first()
    two.first()
    one.second()
    two.second()
    one.third()
    two.third()
    one.fourth()
    two.fourth()
    one.last()
    two.last()


def gather(depth, own_a, own_b):
    shape = jax.ShapeDtypeStruct
    halves = lambda own: own.reshape(2, 16, own.shape[1])
    full = lambda own: shape((2, depth, 2, 2, 2, 16, own.shape[1]), BF16)
    full_a, full_b = pl.pallas_call(
        functools.partial(gather_kernel, depth),
        out_shape=(full(own_a), full(own_b)),
        in_specs=[pl.BlockSpec(memory_space=pltpu.VMEM)] * 2,
        out_specs=tuple([pl.BlockSpec(memory_space=pltpu.VMEM)] * 2),
        scratch_shapes=[pltpu.SemaphoreType.DMA((2, Gather.COPIES))] * 2,
        compiler_params=pltpu.CompilerParams(
            collective_id=0, has_side_effects=True, vmem_limit_bytes=32 * 1024 * 1024
        ),
        name="gather",
    )(halves(own_a), halves(own_b))
    flat = lambda full: full.reshape(2, -1, full.shape[-1])
    return flat(full_a), flat(full_b)


class Scatter:
    COPIES = 16

    def __init__(self, place, part, pair_in, one_in, two_in, last_in, sems):
        self.p, self.part, self.sems = place, part, sems
        self.pair_in, self.one_in, self.two_in, self.last_in = pair_in, one_in, two_in, last_in
        self.count = 0
        self.copies = []

    def push(self, source, target, device):
        copy = send(source, target, self.sems, self.count, device)
        self.count += 1
        self.copies.append(copy)
        return copy

    def add(self, index, landed):
        mine = self.part[index].astype(F32)
        self.part[index] = (mine + landed.astype(F32)).astype(BF16)

    def first(self):
        p = self.p
        self.pair = self.push(self.part.at[1 - p.t], self.pair_in, p.core())

    def second(self):
        p = self.p
        self.pair.wait_recv()
        every = slice(None)
        for z in range(p.depth):
            for y in range(2):
                for x in range(2):
                    self.add((p.t, z, y, x), self.pair_in[z, y, x])
        self.one = [
            self.push(self.part.at[p.t, every, 1 - p.y, every, 0], self.one_in.at[0], p.y_side()),
            self.push(self.part.at[p.t, every, every, 1 - p.x, 1], self.one_in.at[1], p.x_side()),
        ]

    def third(self):
        p = self.p
        every = slice(None)
        self.one[0].wait_recv()
        for z in range(p.depth):
            for x in range(2):
                self.add((p.t, z, p.y, x, 0), self.one_in[0, z, x])
        self.one[1].wait_recv()
        for z in range(p.depth):
            for y in range(2):
                self.add((p.t, z, y, p.x, 1), self.one_in[1, z, y])
        self.two = [
            self.push(self.part.at[p.t, every, p.y, 1 - p.x, 0], self.two_in.at[0], p.x_side()),
            self.push(self.part.at[p.t, every, 1 - p.y, p.x, 1], self.two_in.at[1], p.y_side()),
        ]

    def fourth(self):
        p = self.p
        for half in range(2):
            self.two[half].wait_recv()
            for z in range(p.depth):
                self.add((p.t, z, p.y, p.x, half), self.two_in[half, z])
        self.along_z = []
        for s in range(1, p.depth):
            z = p.above(s)
            self.along_z.append(
                self.push(
                    self.part.at[p.t, z, p.y, p.x], self.last_in.at[s - 1], p.chip(z, p.y, p.x)
                )
            )

    def last(self):
        p = self.p
        for copy in self.along_z:
            copy.wait_recv()
        total = self.part[p.t, p.z, p.y, p.x].astype(F32)
        for s in range(1, p.depth):
            total += self.last_in[s - 1].astype(F32)
        for copy in self.copies:
            copy.wait_send()
        return total


def scatter_buffers(depth, columns):
    vmem = pltpu.VMEM
    return [
        vmem((depth, 2, 2, 2, 16, columns), BF16),
        vmem((2, depth, 2, 16, columns), BF16),
        vmem((2, depth, 16, columns), BF16),
        vmem((depth - 1, 2, 16, columns), BF16),
        pltpu.SemaphoreType.DMA((2, Scatter.COPIES)),
    ]


class Reduce:
    COPIES = 8

    def __init__(self, place, total, landing, sems):
        self.p, self.total, self.landing, self.sems = place, total, landing, sems
        self.count = 0

    def swap(self, devices):
        copies = []
        for device in devices:
            n = self.count
            copies.append(send(self.total, self.landing.at[n], self.sems, n, device))
            self.count += 1
        return copies

    def step(self, device):
        n = self.count
        (copy,) = self.swap([device])
        copy.wait()
        self.total[...] += self.landing[n]

    def along_z(self):
        p = self.p
        first = self.count
        copies = self.swap([p.chip(p.above(s), p.y, p.x) for s in range(1, p.depth)])
        for copy in copies:
            copy.wait()
        own = self.total[...]
        total = jnp.zeros_like(own)
        for z in range(p.depth):
            part = jnp.where(p.z == z, own, 0.0)
            for s in range(1, p.depth):
                came = lax.rem(p.z + p.depth - s, p.depth)
                part = jnp.where(came == z, self.landing[first + s - 1], part)
            total += part
        self.total[...] = total


def scatter_kernel(depth, ga, gw, small_in, da, dw, small, *scratch):
    place = Place(depth)
    part_a, part_w = scratch[0], scratch[1]
    one = Scatter(place, part_a, *scratch[2:7])
    two = Scatter(place, part_w, *scratch[7:12])
    landing, sems = scratch[12], scratch[13]
    part_w[...] = gw[...]
    part_a[...] = ga[...]
    small[...] = small_in[...]
    place.greet()
    gains = Reduce(place, small, landing, sems)
    two.first()
    one.first()
    gains.step(place.core())
    two.second()
    one.second()
    gains.step(place.x_side())
    two.third()
    one.third()
    gains.step(place.y_side())
    two.fourth()
    one.fourth()
    gains.along_z()
    dw[...] = two.last()
    da[...] = one.last()


def scatter(depth, ga, gw, small):
    shape = jax.ShapeDtypeStruct
    full = lambda part: part.reshape(2, depth, 2, 2, 2, 16, part.shape[-1])
    columns_a, columns_w = ga.shape[-1], gw.shape[-1]
    da, dw, small = pl.pallas_call(
        functools.partial(scatter_kernel, depth),
        out_shape=(
            shape((2, 16, columns_a), F32),
            shape((2, 16, columns_w), F32),
            shape(small.shape, F32),
        ),
        in_specs=[pl.BlockSpec(memory_space=pltpu.VMEM)] * 3,
        out_specs=tuple([pl.BlockSpec(memory_space=pltpu.VMEM)] * 3),
        scratch_shapes=[
            pltpu.VMEM((2, depth, 2, 2, 2, 16, columns_a), BF16),
            pltpu.VMEM((2, depth, 2, 2, 2, 16, columns_w), BF16),
        ]
        + scatter_buffers(depth, columns_a)
        + scatter_buffers(depth, columns_w)
        + [
            pltpu.VMEM((Reduce.COPIES,) + small.shape, F32),
            pltpu.SemaphoreType.DMA((2, Reduce.COPIES)),
        ],
        compiler_params=pltpu.CompilerParams(
            collective_id=1, has_side_effects=True, vmem_limit_bytes=60 * 1024 * 1024
        ),
        name="scatter",
    )(full(ga), full(gw), small)
    return da.reshape(32, columns_a), dw.reshape(32, columns_w), small


def per_device(
    direct,
    tokens,
    segment_ids,
    padding,
    mixer_gain,
    query_weight,
    key_weight,
    value_weight,
    slot_weight,
    out_weight,
    feed_gain,
    up_weight,
    up_bias,
    down_weight,
    down_bias,
    cotangent,
):
    own_a = jnp.concatenate([query_weight, key_weight, value_weight, slot_weight], 1).astype(BF16)
    own_b = jnp.concatenate([out_weight.T, up_weight, down_weight.T], 1).astype(BF16)
    depth = lax.axis_size("dp") // 4
    if direct:
        wa, wb = gather(depth, own_a, own_b)
    else:
        wa, wb = (
            lax.all_gather(lax.all_gather(own, "dp", axis=0, tiled=True), "tensor")
            for own in (own_a, own_b)
        )
    half = lax.axis_index("tensor")
    pick = lambda rows: lax.dynamic_slice_in_dim(rows, half, 1, 0)
    out, grad_out, ga, gw, small = layer(
        tokens,
        cotangent,
        pick(segment_ids),
        pick(padding),
        mixer_gain[None],
        feed_gain[None],
        up_bias[None],
        down_bias[None],
        wa,
        wb,
    )
    if direct:
        da, dw, small = scatter(depth, ga, gw, small)
    else:
        da, dw = (
            lax.psum_scatter(
                lax.psum_scatter(part.astype(F32), "tensor", scatter_dimension=0),
                "dp",
                scatter_dimension=0,
                tiled=True,
            )
            for part in (ga, gw)
        )
        small = lax.psum(small, ("dp", "tensor"))
    width = mixer_gain.shape[0]
    return (
        out,
        grad_out,
        small[1, :width],
        da[:, 0:256],
        da[:, 256:512],
        da[:, 512:768],
        da[:, 768:1024],
        dw[:, 0:256].T,
        small[0, :width],
        dw[:, 256:1280],
        small[4],
        dw[:, 1280:2304].T,
        small[2, :width],
    )


def solution(mesh):
    in_specs = (
        P(("dp", "tensor"), None),
        P("dp", None),
        P("dp", None),
        P(),
        P("dp", "tensor"),
        P("dp", "tensor"),
        P("dp", "tensor"),
        P("dp", "tensor"),
        P("tensor", "dp"),
        P(),
        P("dp", "tensor"),
        P(),
        P("tensor", "dp"),
        P(),
        P(("dp", "tensor"), None),
    )
    out_specs = (
        P(("dp", "tensor"), None),
        P(("dp", "tensor"), None),
        P(),
        P("dp", "tensor"),
        P("dp", "tensor"),
        P("dp", "tensor"),
        P("dp", "tensor"),
        P("tensor", "dp"),
        P(),
        P("dp", "tensor"),
        P(),
        P("tensor", "dp"),
        P(),
    )
    direct = mesh.shape["dp"] == 16 and mesh.shape["tensor"] == 2
    return jax.shard_map(
        functools.partial(per_device, direct),
        mesh=mesh,
        in_specs=in_specs,
        out_specs=out_specs,
        check_vma=False,
    )
```

time: 1590 us -> 226 us (0.14); the launches traced: 1570 us -> 223 us
  waiting for transfers between devices: 649 us -> 0 us
  matrix products: 535 us -> 0 us
  blocking collectives: 212 us -> 0 us
  Pallas kernels: 0 us -> 204 us
  local copies, waits for them, and re-layouts: 97.6 us -> 12.3 us
  loops' own time: 32.1 us -> 0 us
  other arithmetic: 26.5 us -> 5.65 us
  between operations: 16.6 us -> 0.69 us
    dot_general x165 -> x0, matrix products: 535 us -> none  [the longest x32 117 us: mixer_head(): pairs = jnp.dot(queries, key_rows.T, precision=highest) * allowed]
    reduce_scatter x11 -> x0, waiting for transfers between devices: 519 us -> none  [the longest x1 79.7 us: per_device(): lax.psum_scatter(down_local, 'dp', scatter_dimension=1, tiled=True)]
    pallas_call x0 -> x3, Pallas kernels: none -> 204 us  [the longest x1 81.1 us: layer(): pl.pallas_call(functools.partial(layer_kernel, length), out_shape=(shape(...]
    all_gather x5 -> x0, blocking collectives: 169 us -> none  [the longest x1 38.6 us: per_device(): lax.all_gather(query_weight.astype(jnp.bfloat16), 'dp', axis=0, tiled=True)]
    all_gather x6 -> x0, waiting for transfers between devices: 128 us -> none  [the longest x1 48 us: per_device(): lax.all_gather(down_weight.astype(jnp.bfloat16), 'dp', axis=1, tiled=True)]
    psum x1 -> x0, blocking collectives: 42.3 us -> none  [per_device(): lax.psum((mixer_gain_local, feed_gain_local, bias_full, down_bias_local),...]
    reshape x13 -> x0, local copies, waits for them, and re-layouts: 40.9 us -> none  [the longest x10 38.1 us: heads_first(): matrix.reshape(groups, length, -1, width).transpose(0, 2, 1, 3)]
    another operation x2 -> x0, loops' own time: 32.1 us -> none  [mixer_all(): result = lax.map(per_head, stacked)]
  transfers between devices with their start and end apart: 17 -> 0, of which waited for: 15 -> 0; matrix products, arithmetic and copies ran while one was open for 4% -> 0% of each run, Pallas kernels for 0% -> 0%
where the time goes in v1:
time: 226 us; the launch traced here: 223 us
  Pallas kernels  204 us (90%)
  local copies, waits for them, and re-layouts  12.3 us (5%)
  other arithmetic  5.65 us (2%)
    pallas_call x1, Pallas kernels, layer(): pl.pallas_call(functools.partial(layer_kernel, length), out_shape=(shape(...  81.1 us
    pallas_call x1, Pallas kernels, scatter(): pl.pallas_call(functools.partial(scatter_kernel, depth), out_shape=(shape...  72.9 us
    pallas_call x1, Pallas kernels, gather(): pl.pallas_call(functools.partial(gather_kernel, depth), out_shape=(full(o...  50.2 us
    another operation x7, other arithmetic  5.63 us

profile of v1, /device:TPU:1, one launch (start us, length us, event | category | flops | bytes accessed | tf_op | source)
XLA Modules:
  0.0 222.9 jit_solution(10760520708411504534)
XLA Ops:
  0.6 1.3 constant_dynamic-slice_fusion
  2.0 0.8 convert.30
  2.7 0.8 convert.31
  3.5 0.8 convert.32
  4.3 0.8 convert.33
  5.0 0.8 convert.34
  5.8 0.9 convert.35
  6.7 0.9 convert.36
  7.6 50.2 %gather.1 = (bf16[2,4,2,2,2,16,1024]{6,5,4,3,2,1,0:T(8,128)(2,1)S(1)}, bf16[2,4,2,2,2,16,2304]{6,5,4,3,2,1,0:T(8,128)(2,1)S(1)}) custom-call(bf16[2,16,1024]{2,1,0:T(8,128)(2,1)S(1)} %pad_maximum_fusion.1.own_a, bf16[2,16,2304]{2,1,0:T(8,128)(2,1)S(1)} %pad_maximum_fusion.own_b), custom_call_target="tpu_custom_call" | custom-call | tf_op jit(solution)/shard_map/gather/pallas_call | solution.py:569
  57.8 0.0 copy-start
  57.8 2.2 copy-done
  60.0 0.0 copy-start.1
  60.0 1.4 copy-done.1
  61.4 81.1 %layer.1 = (bf16[1024,512]{1,0:T(8,128)(2,1)}, bf16[1024,512]{1,0:T(8,128)(2,1)}, bf16[2,512,1024]{2,1,0:T(8,128)(2,1)}, bf16[2,512,2304]{2,1,0:T(8,128)(2,1)}, f32[8,2048]{1,0:T(8,128)}) custom-call(bf16[1024,512]{1,0:T(8,128)(2,1)} %tok.1, bf16[1024,512]{1,0:T(8,128)(2,1)} %cot.1, s32[1,1024]{1,0:T(1,128)} %get-tuple-element.43.seg_row, ...), custom_call_target="tpu_custom_call" | custom-call | tf_op jit(solution)/shard_map/layer/pallas_call | solution.py:397
  142.5 72.9 %scatter.1 = (f32[2,16,1024]{2,1,0:T(8,128)}, f32[2,16,2304]{2,1,0:T(8,128)}, f32[8,2048]{1,0:T(8,128)}) custom-call(bf16[2,4,2,2,2,16,1024]{6,5,4,3,2,1,0:T(8,128)(2,1)} %bitcast.32, bf16[2,4,2,2,2,16,2304]{6,5,4,3,2,1,0:T(8,128)(2,1)} %bitcast.31, f32[8,2048]{1,0:T(8,128)} %get-tuple-element.29.small_in), custom_call_target="tpu_custom_call" | custom-call | tf_op jit(solution)/shard_map/scatter/pallas_call | solution.py:743
  215.5 1.5 fusion
  216.9 1.4 fusion.1
  218.4 1.4 slice.41
  219.8 1.4 slice_bitcast_fusion.1
  221.2 1.7 slice_bitcast_fusion
  (2 shorter events, 0.0 us)
Async XLA Ops:
  57.8 2.2 copy-start
  60.0 1.4 copy-start.1

commit v2 on v1

v2 whole, which is shorter than its diff:
```python
import functools
import math

import jax
import jax.numpy as jnp
from jax import lax
from jax.experimental import pallas as pl
from jax.experimental.pallas import tpu as pltpu
from jax.sharding import PartitionSpec as P

HEAD_DIM = 64
SLOTS = 64
CHUNK = 128
GROUP = 256
TILE = 256

F32 = jnp.float32
BF16 = jnp.bfloat16
MESH = pl.DeviceIdType.MESH


def dot(left, right):
    return lax.dot_general(left, right, (((1,), (0,)), ((), ())), preferred_element_type=F32)


def dot_rt(left, right):
    return lax.dot_general(left, right, (((1,), (1,)), ((), ())), preferred_element_type=F32)


def dot_lt(left, right):
    return lax.dot_general(left, right, (((0,), (0,)), ((), ())), preferred_element_type=F32)


def twice(block):
    return jnp.concatenate([block, block], axis=1)


def four(block):
    return jnp.concatenate([block, block, block, block], axis=1)


def standardise(rows):
    centred = rows - jnp.mean(rows, axis=-1, keepdims=True)
    scale = lax.rsqrt(jnp.mean(centred * centred, axis=-1, keepdims=True) + 1e-05)
    return centred * scale, scale


def head_stack(block):
    lane = lax.broadcasted_iota(jnp.int32, block.shape, 1) // HEAD_DIM
    zero = jnp.zeros_like(block)
    return jnp.concatenate([jnp.where(lane == h, block, zero) for h in range(4)], axis=0)


def head_blocks():
    row = lax.broadcasted_iota(jnp.int32, (GROUP, GROUP), 0) // HEAD_DIM
    column = lax.broadcasted_iota(jnp.int32, (GROUP, GROUP), 1) // HEAD_DIM
    return row == column


def head_sum(block, ones):
    high = block.astype(BF16)
    low = (block - high.astype(F32)).astype(BF16)
    return dot(high, ones) + dot(low, ones)


def head_max(block):
    halves = []
    lane = lax.broadcasted_iota(jnp.int32, (block.shape[0], 128), 1) < HEAD_DIM
    for j in range(block.shape[1] // 128):
        part = block[:, j * 128 : (j + 1) * 128]
        first = jnp.max(jnp.where(lane, part, -jnp.inf), axis=1, keepdims=True)
        second = jnp.max(jnp.where(lane, -jnp.inf, part), axis=1, keepdims=True)
        halves.append(jnp.where(lane, first, second))
    return jnp.concatenate(halves, axis=1)


def flat(block):
    return block.reshape(-1, block.shape[-1])


def rows_to_columns(seg_row, pad_row, segc, keepc, length):
    segc[pl.ds(0, 8), :] = jnp.full((8, 128), -1.0, F32)
    segc[pl.ds(8 + length, 8), :] = jnp.full((8, 128), -2.0, F32)
    for c in range(length // CHUNK):
        here = slice(c * CHUNK, (c + 1) * CHUNK)
        seg = jnp.broadcast_to(seg_row[:, here].astype(F32), (CHUNK, CHUNK))
        pad = jnp.broadcast_to(pad_row[:, here].astype(F32), (CHUNK, CHUNK))
        segc[pl.ds(8 + c * CHUNK, CHUNK), :] = seg.T
        keepc[pl.ds(c * CHUNK, CHUNK), :] = 1.0 - pad.T


def normalise(r, tok, gain, n1):
    rows = pl.ds(pl.multiple_of(r * TILE, TILE), TILE)
    xhat, _ = standardise(tok[rows, :].astype(F32))
    n1[rows, :] = (xhat * gain[...]).astype(BF16)


def project(r, wa, keepc, n1, q, k, v, w):
    rows = pl.ds(pl.multiple_of(r * TILE, TILE), TILE)
    normed = n1[rows, :]
    keep = twice(keepc[rows, :])
    for g in range(2):
        out = dot(normed, flat(wa[g]))
        q[g, rows, :] = out[:, 0:256].astype(BF16)
        k[g, rows, :] = out[:, 256:512].astype(BF16)
        v[g, rows, :] = out[:, 512:768].astype(BF16)
        w[g, rows, :] = (jnp.exp(out[:, 768:1024]) * keep).astype(BF16)


def chunk_masks(c, segc):
    base = pl.multiple_of(c * CHUNK, CHUNK)
    seg = segc[pl.ds(base + 8, CHUNK), :]
    across = seg.T
    row = lax.broadcasted_iota(jnp.int32, (CHUNK, CHUNK), 0)
    column = lax.broadcasted_iota(jnp.int32, (CHUNK, CHUNK), 1)
    same = seg == across
    causal = jnp.where(same & (column <= row), 1.0, 0.0)
    anti = jnp.where(same & (row <= column), 1.0, 0.0)
    before = segc[pl.ds(base + 7, 1), :]
    first = segc[pl.ds(base + 8, 1), :]
    last = segc[pl.ds(base + 7 + CHUNK, 1), :]
    after = segc[pl.ds(base + 8 + CHUNK, 1), :]
    one = lambda test: jnp.where(test, 1.0, 0.0)
    return causal, anti, dict(
        from_before=one(seg == before),
        to_after=one(seg == last),
        from_after=one(seg == after),
        to_before=one(seg == first),
        carry_on=one(before == last),
        carry_back=one(after == first),
    )


def mix_forward(c, segc, keepc, q, k, v, w, probs, inv, score, mixed, kw, wv, zsum, kw_all, wv_all):
    rows = pl.ds(pl.multiple_of(c * CHUNK, CHUNK), CHUNK)
    causal, _, edge = chunk_masks(c, segc)
    causal4 = four(causal)
    causal_low = causal.astype(BF16)
    blocks = head_blocks()
    ones = jnp.where(blocks, 1.0, 0.0).astype(BF16)
    keep = twice(keepc[rows, :])
    come = twice(edge["from_before"])
    come_low = come.astype(BF16)
    go_low = twice(edge["to_after"]).astype(BF16)
    carry = twice(edge["carry_on"])
    for g in range(2):
        qc, kc, vc, wc = q[g, rows, :], k[g, rows, :], v[g, rows, :], w[g, rows, :]
        kw_low, wv_low = kw[g].astype(BF16), wv[g].astype(BF16)
        kw_all[c, g] = kw_low
        wv_all[c, g] = wv_low
        ws = head_stack(wc)
        pairs = (dot_rt(qc, head_stack(kc)) * causal4).astype(BF16)
        total = dot(causal_low, wc) + come * zsum[g, 0:1, :] + (1.0 - keep)
        inverse = 1.0 / total
        scores = (dot(pairs, ws) + dot(qc * come_low, kw_low)) * (inverse * (HEAD_DIM**-0.5))
        powers = jnp.exp(scores - head_max(scores))
        chances = powers / head_sum(powers, ones)
        ratio = (chances * inverse).astype(BF16)
        probs[g, rows, :] = chances
        inv[g, rows, :] = inverse
        score[g, rows, :] = scores
        mixing = (dot_rt(ratio, ws) * causal4).astype(BF16)
        out = dot(mixing, head_stack(vc)) + dot(ratio * come_low, wv_low)
        mixed[rows, g * GROUP : (g + 1) * GROUP] = (out * keep).astype(BF16)
        wg = wc * go_low
        kw[g] = kw[g] * carry[0:1, :] + jnp.where(blocks, dot_lt(kc, wg), 0.0)
        wv[g] = wv[g] * carry[0:1, :] + jnp.where(blocks, dot_lt(wg, vc), 0.0)
        added = jnp.sum(wg.astype(F32), axis=0, keepdims=True)
        zsum[g] = zsum[g] * carry[0:1, :] + added


def mix_backward(
    c, segc, keepc, q, k, v, w, probs, inv, score, gm, kw_all, wv_all, rg, uq, zgrad, gy
):
    rows = pl.ds(pl.multiple_of(c * CHUNK, CHUNK), CHUNK)
    causal, anti, edge = chunk_masks(c, segc)
    causal4, anti4 = four(causal), four(anti)
    anti_low = anti.astype(BF16)
    blocks = head_blocks()
    ones = jnp.where(blocks, 1.0, 0.0).astype(BF16)
    come_low = twice(edge["from_before"]).astype(BF16)
    late = twice(edge["from_after"])
    late_low = late.astype(BF16)
    back = twice(edge["to_before"])
    back_low = back.astype(BF16)
    carry = twice(edge["carry_back"])
    for g in range(2):
        qc, kc, vc, wc = q[g, rows, :], k[g, rows, :], v[g, rows, :], w[g, rows, :]
        grad = gm[g, rows, :]
        chances, inverse, scores = probs[g, rows, :], inv[g, rows, :], score[g, rows, :]
        ratio = (chances * inverse).astype(BF16)
        ws, grads, ratios = head_stack(wc), head_stack(grad), head_stack(ratio)
        d_mixing = (dot_rt(grad, head_stack(vc)) * causal4).astype(BF16)
        d_ratio = dot(d_mixing, ws) + dot_rt(grad * come_low, wv_all[c, g])
        d_chance = d_ratio * inverse
        weighted = d_chance * chances
        d_score = chances * d_chance - chances * head_sum(weighted, ones)
        d_pw = (d_score * inverse * (HEAD_DIM**-0.5)).astype(BF16)
        d_total = (weighted + d_score * scores) * inverse
        d_pairs = (dot_rt(d_pw, ws) * causal4).astype(BF16)
        gq = dot(d_pairs, head_stack(kc)) + dot_rt(d_pw * come_low, kw_all[c, g])
        rg_low, uq_low = rg[g].astype(BF16), uq[g].astype(BF16)
        d_pws = head_stack(d_pw)
        mixing_t = (dot_rt(wc, ratios) * anti4).astype(BF16)
        w_late = wc * late_low
        gv = dot(mixing_t, grads) + dot(w_late, rg_low)
        d_pairs_t = (dot_rt(wc, d_pws) * anti4).astype(BF16)
        gk = dot(d_pairs_t, head_stack(qc)) + dot(w_late, uq_low)
        d_mixing_t = (dot_rt(vc, grads) * anti4).astype(BF16)
        pairs_t = (dot_rt(kc, head_stack(qc)) * anti4).astype(BF16)
        z_high = d_total.astype(BF16)
        z_low = (d_total - z_high.astype(F32)).astype(BF16)
        dw = dot(d_mixing_t, ratios) + dot(pairs_t, d_pws)
        dw += dot_rt(vc * late_low, rg_low) + dot_rt(kc * late_low, uq_low)
        dw -= dot(anti_low, z_high) + dot(anti_low, z_low) + late * zgrad[g, 0:1, :]
        gy[g, rows, 0:256] = gq.astype(BF16)
        gy[g, rows, 256:512] = gk.astype(BF16)
        gy[g, rows, 512:768] = gv.astype(BF16)
        gy[g, rows, 768:1024] = (dw * wc.astype(F32)).astype(BF16)
        rg[g] = rg[g] * carry[0:1, :] + jnp.where(blocks, dot_lt(ratio * back_low, grad), 0.0)
        uq[g] = uq[g] * carry[0:1, :] + jnp.where(blocks, dot_lt(d_pw * back_low, qc), 0.0)
        zgrad[g] = zgrad[g] * carry[0:1, :] + jnp.sum(d_total * back, axis=0, keepdims=True)


def feed(
    r, tok, cot, gain, up_bias, down_bias, wb, keepc, mixed, n2, act, lin, xhat, gh, gb, gm, small, out
):
    rows = pl.ds(pl.multiple_of(r * TILE, TILE), TILE)
    hidden = tok[rows, :].astype(F32)
    for g in range(2):
        hidden += dot_rt(mixed[rows, g * GROUP : (g + 1) * GROUP], flat(wb[g, ..., 0:256]))
    hat, scale = standardise(hidden)
    xhat[...] = hat
    normed = (hat * gain[...]).astype(BF16)
    n2[rows, :] = normed
    grad = cot[rows, :]
    k0 = 0.7978845608
    k1 = k0 * 0.044715
    total = hidden + down_bias[...]
    back = jnp.zeros((TILE, 512), F32)
    for g in range(2):
        for j in range(4):
            here = slice(j * 256, (j + 1) * 256)
            unit = g * 1024 + j * 256
            up = flat(wb[g, ..., 256 + j * 256 : 512 + j * 256])
            down = flat(wb[g, ..., 1280 + j * 256 : 1536 + j * 256])
            linear = dot(normed, up) + up_bias[:, unit : unit + 256]
            square = linear * linear
            gate = 0.5 * jnp.tanh(linear * (square * k1 + k0)) + 0.5
            active = linear * gate
            slope = gate + active * (1.0 - gate) * (square * (6.0 * k1) + 2.0 * k0)
            active_low = active.astype(BF16)
            grad_low = (dot(grad, down) * slope).astype(BF16)
            act[g, rows, here] = active_low
            lin[g, rows, here] = grad_low
            row, column = 4 + unit // 512, unit % 512
            small[row : row + 1, column : column + 256] += jnp.sum(
                grad_low.astype(F32), axis=0, keepdims=True
            )
    for g in range(2):
        total += dot_rt(act[g, rows, :], flat(wb[g, ..., 1280:2304]))
        back += dot_rt(lin[g, rows, :], flat(wb[g, ..., 256:1280]))
    out[rows, :] = total.astype(BF16)
    hat = xhat[...]
    scaled = back * gain[...]
    inner = scaled - jnp.mean(scaled, axis=-1, keepdims=True)
    inner -= hat * jnp.mean(scaled * hat, axis=-1, keepdims=True)
    grad_f32 = grad.astype(F32)
    grad_hidden = grad_f32 + scale * inner
    gh[rows, :] = grad_hidden
    low = grad_hidden.astype(BF16)
    gb[rows, :] = low
    small[0:1, :] += jnp.sum(back * hat, axis=0, keepdims=True)
    small[2:3, :] += jnp.sum(grad_f32, axis=0, keepdims=True)
    keep = twice(keepc[rows, :])
    for g in range(2):
        gm[g, rows, :] = (dot(low, flat(wb[g, ..., 0:256])) * keep).astype(BF16)


def transpose_into(source, target, length):
    for r in range(length // TILE):
        target[:, r * TILE : (r + 1) * TILE] = source[r * TILE : (r + 1) * TILE, :].T


def weight_grad(left_t, right, target, g, target_column, columns):
    shape = target.shape[1:-1] + (256,)

    def step(j, carry):
        here = pl.ds(pl.multiple_of(j * 256, 256), 256)
        there = pl.ds(pl.multiple_of(target_column + j * 256, 256), 256)
        target[g, ..., there] = dot(left_t[...], right[:, here]).astype(BF16).reshape(shape)
        return carry

    lax.fori_loop(0, columns // 256, step, 0)


def finish(r, tok, gain, wa, gy, gh, small, grad_out):
    rows = pl.ds(pl.multiple_of(r * TILE, TILE), TILE)
    hat, scale = standardise(tok[rows, :].astype(F32))
    back = dot_rt(gy[0, rows, :], flat(wa[0])) + dot_rt(gy[1, rows, :], flat(wa[1]))
    scaled = back * gain[...]
    inner = scaled - jnp.mean(scaled, axis=-1, keepdims=True)
    inner -= hat * jnp.mean(scaled * hat, axis=-1, keepdims=True)
    grad_out[rows, :] = (gh[rows, :] + scale * inner).astype(BF16)
    small[1:2, :] += jnp.sum(back * hat, axis=0, keepdims=True)


class Quiet:
    def before(self):
        pass

    def weights_a(self):
        pass

    def mixing(self, c):
        pass

    def weights_b(self):
        pass

    def grads_w(self, which):
        pass

    def mixing_back(self, i):
        pass

    def grads_a(self):
        pass

    def after(self):
        pass


LAYER_INPUTS = 8
LAYER_SCRATCH = 24


def layer_body(
    length,
    comm,
    tok,
    cot,
    seg_row,
    pad_row,
    gain_one,
    gain_two,
    up_bias,
    down_bias,
    wa,
    wb,
    out,
    grad_out,
    ga,
    gw,
    small,
    segc,
    keepc,
    n1,
    q,
    k,
    v,
    w,
    probs,
    inv,
    score,
    mixed,
    kw,
    wv,
    zsum,
    kw_all,
    wv_all,
    n2,
    act,
    lin,
    xhat,
    gh,
    gb,
    gm,
    flip,
):
    chunks, tiles = length // CHUNK, length // TILE
    comm.before()
    small[...] = jnp.zeros_like(small)
    rows_to_columns(seg_row, pad_row, segc, keepc, length)

    @pl.loop(0, tiles)
    def _(r):
        normalise(r, tok, gain_one, n1)

    kw[...] = jnp.zeros_like(kw)
    wv[...] = jnp.zeros_like(wv)
    zsum[...] = jnp.zeros_like(zsum)
    comm.weights_a()

    @pl.loop(0, tiles)
    def _(r):
        project(r, wa, keepc, n1, q, k, v, w)

    @pl.loop(0, chunks)
    def _(c):
        comm.mixing(c)
        mix_forward(
            c, segc, keepc, q, k, v, w, probs, inv, score, mixed, kw, wv, zsum, kw_all, wv_all
        )

    comm.weights_b()

    @pl.loop(0, tiles)
    def _(r):
        feed(
            r, tok, cot, gain_two, up_bias, down_bias, wb, keepc, mixed, n2, act, lin, xhat, gh, gb,
            gm, small, out,
        )

    transpose_into(cot, flip, length)
    for g in range(2):
        weight_grad(flip, act.at[g], gw, g, 1280, 1024)
    comm.grads_w(0)
    transpose_into(n2, flip, length)
    for g in range(2):
        weight_grad(flip, lin.at[g], gw, g, 256, 1024)
    transpose_into(gb, flip, length)
    for g in range(2):
        weight_grad(flip, mixed.at[:, g * GROUP : (g + 1) * GROUP], gw, g, 0, GROUP)
    comm.grads_w(1)

    kw[...] = jnp.zeros_like(kw)
    wv[...] = jnp.zeros_like(wv)
    zsum[...] = jnp.zeros_like(zsum)

    @pl.loop(0, chunks)
    def _(i):
        comm.mixing_back(i)
        mix_backward(
            chunks - 1 - i, segc, keepc, q, k, v, w, probs, inv, score, gm, kw_all, wv_all, kw, wv,
            zsum, act,
        )

    transpose_into(n1, flip, length)
    for g in range(2):
        weight_grad(flip, act.at[g], ga, g, 0, 1024)
    comm.grads_a()

    @pl.loop(0, tiles)
    def _(r):
        finish(r, tok, gain_one, wa, act, gh, small, grad_out)

    comm.after()


def layer_scratch(length, width):
    vmem = pltpu.VMEM
    chunks = length // CHUNK
    return [
        vmem((length + 16, 128), F32),
        vmem((length, 128), F32),
        vmem((length, width), BF16),
        vmem((2, length, GROUP), BF16),
        vmem((2, length, GROUP), BF16),
        vmem((2, length, GROUP), BF16),
        vmem((2, length, GROUP), BF16),
        vmem((2, length, GROUP), F32),
        vmem((2, length, GROUP), F32),
        vmem((2, length, GROUP), F32),
        vmem((length, width), BF16),
        vmem((2, GROUP, GROUP), F32),
        vmem((2, GROUP, GROUP), F32),
        vmem((2, 8, GROUP), F32),
        vmem((chunks, 2, GROUP, GROUP), BF16),
        vmem((chunks, 2, GROUP, GROUP), BF16),
        vmem((length, width), BF16),
        vmem((2, length, 1024), BF16),
        vmem((2, length, 1024), BF16),
        vmem((TILE, width), F32),
        vmem((length, width), F32),
        vmem((length, width), BF16),
        vmem((2, length, GROUP), BF16),
        vmem((width, length), BF16),
    ]


def layer_kernel(length, *refs):
    layer_body(length, Quiet(), *refs)


def layer(tokens, cotangent, seg_row, pad_row, gain_one, gain_two, up_bias, down_bias, wa, wb):
    length, width = tokens.shape
    shape = jax.ShapeDtypeStruct
    cut = lambda full: full.reshape(2, -1, 2, 2, 2, 16, full.shape[-1])
    wa, wb = cut(wa), cut(wb)
    space = pl.BlockSpec(memory_space=pltpu.VMEM)
    out, grad_out, ga, gw, small = pl.pallas_call(
        functools.partial(layer_kernel, length),
        out_shape=(
            shape((length, width), BF16),
            shape((length, width), BF16),
            shape(wa.shape, BF16),
            shape(wb.shape, BF16),
            shape((8, width), F32),
        ),
        in_specs=[space] * 10,
        out_specs=tuple([space] * 5),
        scratch_shapes=layer_scratch(length, width),
        compiler_params=pltpu.CompilerParams(vmem_limit_bytes=60 * 1024 * 1024),
        name="layer",
    )(tokens, cotangent, seg_row, pad_row, gain_one, gain_two, up_bias, down_bias, wa, wb)
    whole = lambda full: full.reshape(2, width, full.shape[-1])
    return out, grad_out, whole(ga), whole(gw), small


class Place:
    def __init__(self, depth):
        index = lax.axis_index("dp")
        t = lax.axis_index("tensor")
        x, y, z = lax.rem(index, 2), lax.rem(index // 2, 2), index // 4
        self.depth = depth
        self.x, self.y, self.z, self.t, self.other = x, y, z, t, 1 - t
        self.near = (y + t * (1 - 2 * y), x + (1 - t) * (1 - 2 * x))
        self.next = (y + (1 - t) * (1 - 2 * y), x + t * (1 - 2 * x))
        self.far = (1 - y, 1 - x)
        chip = lambda z, y, x: (z * 2 + y) * 2 + x
        self.levels = [lax.rem(z + s, depth) for s in range(depth)]
        self.chips_z = [chip(level, y, x) for level in self.levels]
        self.to_near = {"dp": chip(z, *self.near)}
        self.to_next = {"dp": chip(z, *self.next)}
        self.to_pair = {"tensor": self.other}
        self.to_x = {"dp": chip(z, y, 1 - x)}
        self.to_y = {"dp": chip(z, 1 - y, x)}

    def along_z(self, step, core):
        return {"dp": self.chips_z[step], "tensor": core}

    def greet(self):
        barrier = pltpu.get_barrier_semaphore()
        friends = [self.to_pair, self.to_x, self.to_y]
        friends += [self.along_z(s, core) for s in range(1, self.depth) for core in range(2)]
        for friend in friends:
            pl.semaphore_signal(barrier, inc=1, device_id=friend, device_id_type=MESH)
        pl.semaphore_wait(barrier, len(friends))


class Copies:
    def __init__(self, sems):
        self.sems = sems
        self.started = []

    def build(self, source, target, device, out_sem, in_sem):
        return pltpu.make_async_remote_copy(
            src_ref=source,
            dst_ref=target,
            send_sem=self.sems.at[0, out_sem],
            recv_sem=self.sems.at[1, in_sem],
            device_id=device,
            device_id_type=MESH,
        )

    def start(self, source, target, device, number, in_sem=None):
        copy = self.build(source(), target, device, number, number if in_sem is None else in_sem)
        copy.start()
        self.started.append((source, number))

    def landed(self, target, number):
        self.build(target, target, {"tensor": 0}, number, number).wait_recv()

    def left(self):
        for source, number in self.started:
            part = source()
            self.build(part, part, {"tensor": 0}, number, number).wait_send()


class Gather(Copies):
    COPIES = 14

    def __init__(self, place, own, full, columns, sems):
        super().__init__(sems)
        self.p, self.own, self.full, self.columns = place, own, full, columns

    def at(self, g, z, spot, half):
        return self.full.at[g, z, spot[0], spot[1], half, :, self.columns]

    def block(self, spot, half):
        return self.at(slice(None), slice(None), spot, half)

    def forward(self, spot, device, number):
        block = lambda: self.block(spot, self.p.t)
        self.start(block, block(), device, number)

    def first(self):
        p = self.p
        here = (p.y, p.x)
        for s in range(1, p.depth):
            for core in range(2):
                self.start(
                    lambda core=core: self.own.at[core, :, self.columns],
                    self.at(p.t, p.z, here, core),
                    p.along_z(s, core),
                    2 * (s - 1) + core,
                    2 * (s - 1) + p.t,
                )
        self.start(
            lambda: self.own.at[p.other, :, self.columns],
            self.at(p.t, p.z, here, p.other),
            p.to_pair,
            6,
        )
        self.full[p.t, p.z, p.y, p.x, p.t, :, self.columns] = self.own[p.t, :, self.columns]

    def second(self):
        p = self.p
        here = (p.y, p.x)
        for n in range(7):
            self.landed(self.at(p.t, p.z, here, p.t), n)
        self.forward(here, p.to_near, 7)
        self.forward(here, p.to_next, 8)
        self.forward(here, p.to_pair, 9)

    def third(self):
        p = self.p
        self.landed(self.block(p.near, p.t), 7)
        self.forward(p.near, p.to_next, 10)
        self.forward(p.near, p.to_pair, 11)
        self.landed(self.block(p.next, p.t), 8)
        self.forward(p.next, p.to_pair, 12)

    def fourth(self):
        p = self.p
        self.landed(self.block(p.far, p.t), 10)
        self.forward(p.far, p.to_pair, 13)

    def last(self):
        p = self.p
        for n in (9, 11, 12, 13):
            self.landed(self.block((p.y, p.x), p.other), n)


class Scatter(Copies):
    COPIES = 11

    def __init__(self, place, part, columns, pair_in, near_in, next_in, last_in, sems):
        super().__init__(sems)
        self.p, self.part, self.columns = place, part, columns
        self.pair_in, self.near_in, self.next_in, self.last_in = pair_in, near_in, next_in, last_in

    def at(self, g, z, spot, half):
        return self.part.at[g, z, spot[0], spot[1], half, :, self.columns]

    def block(self, spot, half):
        return self.at(slice(None), slice(None), spot, half)

    def add(self, spot, landed):
        p = self.p
        here = (slice(None), slice(None), spot[0], spot[1], p.t, slice(None), self.columns)
        self.part[here] = (self.part[here].astype(F32) + landed.astype(F32)).astype(BF16)

    def first(self):
        p = self.p
        self.start(
            lambda: self.part.at[:, :, :, :, p.other, :, self.columns], self.pair_in, p.to_pair, 0
        )

    def second(self):
        p = self.p
        self.landed(self.pair_in, 0)
        for spot, number in ((p.far, 1), (p.near, 2)):
            self.add(spot, self.pair_in[:, :, spot[0], spot[1]])
            self.start(
                lambda spot=spot: self.block(spot, p.t),
                self.near_in.at[number - 1],
                p.to_near,
                number,
            )
        for spot in (p.next, (p.y, p.x)):
            self.add(spot, self.pair_in[:, :, spot[0], spot[1]])

    def third(self):
        p = self.p
        self.landed(self.near_in.at[0], 1)
        self.add(p.next, self.near_in[0])
        self.start(lambda: self.block(p.next, p.t), self.next_in, p.to_next, 3)
        self.landed(self.near_in.at[1], 2)
        self.add((p.y, p.x), self.near_in[1])

    def fourth(self):
        p = self.p
        here = (p.y, p.x)
        self.landed(self.next_in, 3)
        self.add(here, self.next_in[...])
        for s in range(1, p.depth):
            for core in range(2):
                self.start(
                    lambda s=s, core=core: self.at(core, p.levels[s], here, p.t),
                    self.last_in.at[2 * (s - 1) + p.t],
                    p.along_z(s, core),
                    4 + 2 * (s - 1) + core,
                    4 + 2 * (s - 1) + p.t,
                )
        self.start(
            lambda: self.at(p.other, p.z, here, p.t),
            self.last_in.at[2 * (p.depth - 1)],
            p.to_pair,
            10,
        )

    def last(self, target):
        p = self.p
        for n in range(7):
            self.landed(self.last_in.at[n], 4 + n)
        mine = self.part[p.t, p.z, p.y, p.x, p.t, :, self.columns].astype(F32)
        rest = self.last_in[2 * (p.depth - 1)].astype(F32)
        for s in range(1, p.depth):
            mine += self.last_in[2 * (s - 1) + p.t].astype(F32)
            rest += self.last_in[2 * (s - 1) + p.other].astype(F32)
        target[p.t] = mine
        target[p.other] = rest


def scatter_scratch(depth, columns):
    vmem = pltpu.VMEM
    return [
        vmem((2, depth, 2, 2, 16, columns), BF16),
        vmem((2, 2, depth, 16, columns), BF16),
        vmem((2, depth, 16, columns), BF16),
        vmem((2 * depth - 1, 16, columns), BF16),
        pltpu.SemaphoreType.DMA((2, Scatter.COPIES)),
    ]


class Reduce(Copies):
    COPIES = 6

    def __init__(self, place, total, landing, sems):
        super().__init__(sems)
        self.p, self.total, self.landing = place, total, landing

    def swap(self, number, device):
        self.start(lambda: self.total.at[number], self.landing.at[number], device, number)
        self.landed(self.landing.at[number], number)
        self.total[number + 1] = self.total[number] + self.landing[number]

    def finish(self):
        p = self.p
        for s in range(1, p.depth):
            self.start(
                lambda: self.total.at[3], self.landing.at[2 + s], {"dp": p.chips_z[s]}, 2 + s
            )
        for s in range(1, p.depth):
            self.landed(self.landing.at[2 + s], 2 + s)
        own = self.total[3]
        total = jnp.zeros_like(own)
        for z in range(p.depth):
            part = jnp.where(p.z == z, own, 0.0)
            for s in range(1, p.depth):
                came = lax.rem(p.z + p.depth - s, p.depth)
                part = jnp.where(came == z, self.landing[2 + s], part)
            total += part
        return total


class Woven:
    def __init__(self, place, owns, own_a, own_b, wa, wb, ga, gw, gains, gathers, scatters, targets):
        self.p = place
        self.owns, self.own_a, self.own_b = owns, own_a, own_b
        self.a = [
            Gather(place, own_a, wa, slice(0, 512), gathers[0]),
            Gather(place, own_a, wa, slice(512, 1024), gathers[1]),
        ]
        self.b = [
            Gather(place, own_b, wb, slice(0, 1280), gathers[2]),
            Gather(place, own_b, wb, slice(1280, 2304), gathers[3]),
        ]
        self.w = [
            Scatter(place, gw, slice(1280, 2304), *scatters[0]),
            Scatter(place, gw, slice(0, 1280), *scatters[1]),
        ]
        self.g = [
            Scatter(place, ga, slice(0, 512), *scatters[2]),
            Scatter(place, ga, slice(512, 1024), *scatters[3]),
        ]
        self.gains = gains
        self.da, self.dw = targets

    def before(self):
        p = self.p
        query, key, value, slot, out_t, up, down_t = self.owns
        halves = lambda ref: ref[...].astype(BF16).reshape(2, 16, ref.shape[1])
        self.own_a[:, :, 0:256] = halves(query)
        self.own_a[:, :, 256:512] = halves(key)
        self.own_a[:, :, 512:768] = halves(value)
        self.own_a[:, :, 768:1024] = halves(slot)
        self.own_b[:, :, 0:256] = halves(out_t)
        self.own_b[:, :, 256:1280] = halves(up)
        self.own_b[:, :, 1280:2304] = halves(down_t)
        p.greet()
        self.a[0].first()
        self.a[1].first()

    def weights_a(self):
        one, two = self.a
        one.second()
        two.second()
        self.b[0].first()
        one.third()
        two.third()
        one.fourth()
        two.fourth()
        self.b[1].first()
        one.last()
        two.last()

    def mixing(self, c):
        one, two = self.b
        for i, step in enumerate((one.second, one.third, one.fourth, two.second, two.third)):
            pl.when(c == i + 1)(step)

    def weights_b(self):
        one, two = self.b
        two.fourth()
        one.last()
        two.last()

    def grads_w(self, which):
        self.w[which].first()
        if which == 1:
            self.w[0].second()

    def mixing_back(self, i):
        one, two = self.w
        steps = (one.third, two.second, one.fourth, two.third, None, two.fourth)
        for n, step in enumerate(steps):
            if step is not None:
                pl.when(i == n + 1)(step)

    def grads_a(self):
        self.g[0].first()
        self.g[1].first()
        self.w[0].last(self.dw.at[:, :, 1280:2304])
        self.w[1].last(self.dw.at[:, :, 0:1280])
        self.g[0].second()
        self.g[1].second()

    def after(self):
        p = self.p
        one, two = self.g
        self.gains.swap(0, p.to_pair)
        one.third()
        two.third()
        self.gains.swap(1, p.to_x)
        one.fourth()
        two.fourth()
        self.gains.swap(2, p.to_y)
        one.last(self.da.at[:, :, 0:512])
        two.last(self.da.at[:, :, 512:1024])
        self.total = self.gains.finish()
        for copies in self.a + self.b + self.w + self.g + [self.gains]:
            copies.left()


def woven_kernel(length, depth, *refs):
    refs = list(refs)
    take = lambda n: [refs.pop(0) for _ in range(n)]
    tok, cot, seg_rows, pad_rows, gain_one, gain_two, up_bias, down_bias = take(LAYER_INPUTS)
    owns = take(7)
    out, grad_out, da, dw, small_out = take(5)
    own_a, own_b, wa, wb, ga, gw, seg_row, pad_row = take(8)
    small, landing, gain_sems = take(3)
    gathers = take(4)
    scatters = [take(5) for _ in range(4)]
    place = Place(depth)
    gains = Reduce(place, small, landing, gain_sems)
    comm = Woven(place, owns, own_a, own_b, wa, wb, ga, gw, gains, gathers, scatters, (da, dw))
    first = (lax.axis_index("tensor") == 0)
    for rows, row in ((seg_rows, seg_row), (pad_rows, pad_row)):
        row[...] = jnp.where(first, rows[0:1, :], rows[1:2, :])
    layer_body(
        length, comm, tok, cot, seg_row, pad_row, gain_one, gain_two, up_bias, down_bias, wa, wb,
        out, grad_out, ga, gw, small.at[0], *refs,
    )
    small_out[...] = comm.total


def woven(depth, tokens, cotangent, segments, padding, gains, biases, owns):
    length, width = tokens.shape
    shape = jax.ShapeDtypeStruct
    space = pl.BlockSpec(memory_space=pltpu.VMEM)
    vmem = pltpu.VMEM
    dma = pltpu.SemaphoreType.DMA
    full = lambda columns: vmem((2, depth, 2, 2, 2, 16, columns), BF16)
    out, grad_out, da, dw, small = pl.pallas_call(
        functools.partial(woven_kernel, length, depth),
        out_shape=(
            shape((length, width), BF16),
            shape((length, width), BF16),
            shape((2, 16, 1024), F32),
            shape((2, 16, 2304), F32),
            shape((8, width), F32),
        ),
        in_specs=[space] * (LAYER_INPUTS + 7),
        out_specs=tuple([space] * 5),
        scratch_shapes=[
            vmem((2, 16, 1024), BF16),
            vmem((2, 16, 2304), BF16),
            full(1024),
            full(2304),
            full(1024),
            full(2304),
            vmem((1, length), jnp.int32),
            vmem((1, length), jnp.int32),
            vmem((4, 8, width), F32),
            vmem((Reduce.COPIES, 8, width), F32),
            dma((2, Reduce.COPIES)),
        ]
        + [dma((2, Gather.COPIES))] * 4
        + scatter_scratch(depth, 1024)
        + scatter_scratch(depth, 1280)
        + scatter_scratch(depth, 512)
        + scatter_scratch(depth, 512)
        + layer_scratch(length, width),
        compiler_params=pltpu.CompilerParams(
            collective_id=0, has_side_effects=True, vmem_limit_bytes=62 * 1024 * 1024
        ),
        name="woven",
    )(tokens, cotangent, segments, padding, *gains, *biases, *owns)
    return out, grad_out, da.reshape(32, 1024), dw.reshape(32, 2304), small


def per_device(
    direct,
    tokens,
    segment_ids,
    padding,
    mixer_gain,
    query_weight,
    key_weight,
    value_weight,
    slot_weight,
    out_weight,
    feed_gain,
    up_weight,
    up_bias,
    down_weight,
    down_bias,
    cotangent,
):
    gains = (mixer_gain[None], feed_gain[None])
    biases = (up_bias[None], down_bias[None])
    if direct:
        owns = (
            query_weight, key_weight, value_weight, slot_weight, out_weight.T, up_weight,
            down_weight.T,
        )
        depth = lax.axis_size("dp") // 4
        out, grad_out, da, dw, small = woven(
            depth, tokens, cotangent, segment_ids, padding, gains, biases, owns
        )
    else:
        own_a = jnp.concatenate([query_weight, key_weight, value_weight, slot_weight], 1)
        own_b = jnp.concatenate([out_weight.T, up_weight, down_weight.T], 1)
        wa, wb = (
            lax.all_gather(
                lax.all_gather(own.astype(BF16), "dp", axis=0, tiled=True), "tensor"
            )
            for own in (own_a, own_b)
        )
        half = lax.axis_index("tensor")
        pick = lambda rows: lax.dynamic_slice_in_dim(rows, half, 1, 0)
        out, grad_out, ga, gw, small = layer(
            tokens, cotangent, pick(segment_ids), pick(padding), *gains, *biases, wa, wb
        )
        da, dw = (
            lax.psum_scatter(
                lax.psum_scatter(part.astype(F32), "tensor", scatter_dimension=0),
                "dp",
                scatter_dimension=0,
                tiled=True,
            )
            for part in (ga, gw)
        )
        small = lax.psum(small, ("dp", "tensor"))
    return (
        out,
        grad_out,
        small[1],
        da[:, 0:256],
        da[:, 256:512],
        da[:, 512:768],
        da[:, 768:1024],
        dw[:, 0:256].T,
        small[0],
        dw[:, 256:1280],
        small[4:8].reshape(-1),
        dw[:, 1280:2304].T,
        small[2],
    )


def solution(mesh):
    in_specs = (
        P(("dp", "tensor"), None),
        P("dp", None),
        P("dp", None),
        P(),
        P("dp", "tensor"),
        P("dp", "tensor"),
        P("dp", "tensor"),
        P("dp", "tensor"),
        P("tensor", "dp"),
        P(),
        P("dp", "tensor"),
        P(),
        P("tensor", "dp"),
        P(),
        P(("dp", "tensor"), None),
    )
    out_specs = (
        P(("dp", "tensor"), None),
        P(("dp", "tensor"), None),
        P(),
        P("dp", "tensor"),
        P("dp", "tensor"),
        P("dp", "tensor"),
        P("dp", "tensor"),
        P("tensor", "dp"),
        P(),
        P("dp", "tensor"),
        P(),
        P("tensor", "dp"),
        P(),
    )
    direct = mesh.shape["dp"] == 16 and mesh.shape["tensor"] == 2
    return jax.shard_map(
        functools.partial(per_device, direct),
        mesh=mesh,
        in_specs=in_specs,
        out_specs=out_specs,
        check_vma=False,
    )
```

time: 226 us -> 158 us (0.70)
  Pallas kernels: 204 us -> 149 us
  other arithmetic: 5.65 us -> 0 us
  local copies, waits for them, and re-layouts: 12.3 us -> 6.78 us
    pallas_call x3 -> x1, Pallas kernels: 204 us -> 149 us  [woven(): pl.pallas_call(functools.partial(woven_kernel, length, depth), out_shape=...]
    another operation x7 -> x0, other arithmetic: 5.63 us -> none
    slice x2 -> x1, local copies, waits for them, and re-layouts: 2.89 us -> 0.59 us  [per_device(): small[2]]
where the time goes in v2:
time: 158 us; the launch traced here: 156 us
  Pallas kernels  149 us (94%)
  local copies, waits for them, and re-layouts  6.78 us (4%)
    pallas_call x1, Pallas kernels, woven(): pl.pallas_call(functools.partial(woven_kernel, length, depth), out_shape=...  149 us
    unnamed x10, local copies, waits for them, and re-layouts  3.94 us

profile of v2, /device:TPU:1, one launch (start us, length us, event | category | flops | bytes accessed | tf_op | source)
XLA Modules:
  0.0 156.2 jit_solution(5414120423431179733)
XLA Ops:
  0.7 148.8 %woven.1 = (bf16[1024,512]{1,0:T(8,128)(2,1)}, bf16[1024,512]{1,0:T(8,128)(2,1)}, f32[2,16,1024]{2,1,0:T(8,128)}, f32[2,16,2304]{2,1,0:T(8,128)}, f32[8,512]{1,0:T(8,128)}) custom-call(bf16[1024,512]{1,0:T(8,128)(2,1)} %refs_0_.1, bf16[1024,512]{1,0:T(8,128)(2,1)} %refs_1_.1, s32[2,1024]{1,0:T(2,128)} %refs_2_.1, s32[2,1024]{1,0:T(2,128)} %refs_3_.1, ...), custom_call_target="tpu_custom_call" | custom-call | tf_op jit(solution)/shard_map/woven/pallas_call | solution.py:888
  149.4 0.0 copy-start.1
  149.5 0.0 copy-start.2
  149.5 1.5 fusion
  151.0 0.0 copy-done.2
  151.0 0.6 fusion.1
  151.6 0.0 copy-done.1
  151.6 0.7 slice_bitcast_fusion
  152.3 0.6 copy.28
  152.9 0.0 copy-start
  152.9 2.4 %copy.31 = bf16[1024,512]{1,0:T(8,128)(2,1)} copy(bf16[1024,512]{1,0:T(8,128)(2,1)} %get-tuple-element.46) | data formatting | bytes 2097152
  155.3 0.0 copy-done
  155.3 1.0 copy.32
  (1 shorter events, 0.0 us)
Async XLA Ops:
  149.4 2.1 %copy-start.1 = (f32[2,16,2304]{2,1,0:T(8,128)S(1)}, f32[2,16,2304]{2,1,0:T(8,128)}, u32[]{:S(2)}) copy-start(f32[2,16,2304]{2,1,0:T(8,128)} %get-tuple-element.22) | copy-start | bytes 884740
  149.5 1.5 copy-start.2
  152.9 2.4 %copy-start = (bf16[1024,512]{1,0:T(8,128)(2,1)S(1)}, bf16[1024,512]{1,0:T(8,128)(2,1)}, u32[]{:S(2)}) copy-start(bf16[1024,512]{1,0:T(8,128)(2,1)} %get-tuple-element.47) | copy-start | bytes 3145732

commit v3 on v2

v3 whole, which is shorter than its diff:
```python
import functools
import math

import jax
import jax.numpy as jnp
from jax import lax
from jax.experimental import pallas as pl
from jax.experimental.pallas import tpu as pltpu
from jax.sharding import PartitionSpec as P

HEAD_DIM = 64
SLOTS = 64
CHUNK = 128
GROUP = 256
TILE = 256

F32 = jnp.float32
BF16 = jnp.bfloat16
MESH = pl.DeviceIdType.MESH


def dot(left, right):
    return lax.dot_general(left, right, (((1,), (0,)), ((), ())), preferred_element_type=F32)


def dot_rt(left, right):
    return lax.dot_general(left, right, (((1,), (1,)), ((), ())), preferred_element_type=F32)


def dot_lt(left, right):
    return lax.dot_general(left, right, (((0,), (0,)), ((), ())), preferred_element_type=F32)


def twice(block):
    return jnp.concatenate([block, block], axis=1)


def four(block):
    return jnp.concatenate([block, block, block, block], axis=1)


def standardise(rows):
    centred = rows - jnp.mean(rows, axis=-1, keepdims=True)
    scale = lax.rsqrt(jnp.mean(centred * centred, axis=-1, keepdims=True) + 1e-05)
    return centred * scale, scale


def head_stack(block):
    lane = lax.broadcasted_iota(jnp.int32, block.shape, 1) // HEAD_DIM
    zero = jnp.zeros_like(block)
    return jnp.concatenate([jnp.where(lane == h, block, zero) for h in range(4)], axis=0)


def head_blocks():
    row = lax.broadcasted_iota(jnp.int32, (GROUP, GROUP), 0) // HEAD_DIM
    column = lax.broadcasted_iota(jnp.int32, (GROUP, GROUP), 1) // HEAD_DIM
    return row == column


def head_sum(block, ones):
    high = block.astype(BF16)
    low = (block - high.astype(F32)).astype(BF16)
    return dot(high, ones) + dot(low, ones)


def head_max(block):
    halves = []
    lane = lax.broadcasted_iota(jnp.int32, (block.shape[0], 128), 1) < HEAD_DIM
    for j in range(block.shape[1] // 128):
        part = block[:, j * 128 : (j + 1) * 128]
        first = jnp.max(jnp.where(lane, part, -jnp.inf), axis=1, keepdims=True)
        second = jnp.max(jnp.where(lane, -jnp.inf, part), axis=1, keepdims=True)
        halves.append(jnp.where(lane, first, second))
    return jnp.concatenate(halves, axis=1)


def flat(block):
    return block.reshape(-1, block.shape[-1])


def rows_to_columns(seg_row, pad_row, segc, keepc, length):
    segc[pl.ds(0, 8), :] = jnp.full((8, 128), -1.0, F32)
    segc[pl.ds(8 + length, 8), :] = jnp.full((8, 128), -2.0, F32)
    for c in range(length // CHUNK):
        here = slice(c * CHUNK, (c + 1) * CHUNK)
        seg = jnp.broadcast_to(seg_row[:, here].astype(F32), (CHUNK, CHUNK))
        pad = jnp.broadcast_to(pad_row[:, here].astype(F32), (CHUNK, CHUNK))
        segc[pl.ds(8 + c * CHUNK, CHUNK), :] = seg.T
        keepc[pl.ds(c * CHUNK, CHUNK), :] = 1.0 - pad.T


def normalise(r, tok, gain, n1):
    rows = pl.ds(pl.multiple_of(r * TILE, TILE), TILE)
    xhat, _ = standardise(tok[rows, :].astype(F32))
    n1[rows, :] = (xhat * gain[...]).astype(BF16)


def project(g, r, wa, keepc, n1, q, k, v, w):
    rows = pl.ds(pl.multiple_of(r * TILE, TILE), TILE)
    out = dot(n1[rows, :], flat(wa[g]))
    q[g, rows, :] = out[:, 0:256].astype(BF16)
    k[g, rows, :] = out[:, 256:512].astype(BF16)
    v[g, rows, :] = out[:, 512:768].astype(BF16)
    w[g, rows, :] = (jnp.exp(out[:, 768:1024]) * twice(keepc[rows, :])).astype(BF16)


def chunk_masks(c, segc):
    base = pl.multiple_of(c * CHUNK, CHUNK)
    seg = segc[pl.ds(base + 8, CHUNK), :]
    across = seg.T
    row = lax.broadcasted_iota(jnp.int32, (CHUNK, CHUNK), 0)
    column = lax.broadcasted_iota(jnp.int32, (CHUNK, CHUNK), 1)
    same = seg == across
    causal = jnp.where(same & (column <= row), 1.0, 0.0)
    anti = jnp.where(same & (row <= column), 1.0, 0.0)
    before = segc[pl.ds(base + 7, 1), :]
    first = segc[pl.ds(base + 8, 1), :]
    last = segc[pl.ds(base + 7 + CHUNK, 1), :]
    after = segc[pl.ds(base + 8 + CHUNK, 1), :]
    one = lambda test: jnp.where(test, 1.0, 0.0)
    return causal, anti, dict(
        from_before=one(seg == before),
        to_after=one(seg == last),
        from_after=one(seg == after),
        to_before=one(seg == first),
        carry_on=one(before == last),
        carry_back=one(after == first),
    )


def mix_forward(
    g, i, segc, keepc, q, k, v, w, probs, inv, score, mixed, kw, wv, zsum, kw_all, wv_all
):
    blocks = head_blocks()
    ones = jnp.where(blocks, 1.0, 0.0).astype(BF16)
    state_k, state_v, state_z = kw[...], wv[...], zsum[0:1, :]
    for n in range(2):
        c = 2 * i + n
        rows = pl.ds(pl.multiple_of(c * CHUNK, CHUNK), CHUNK)
        causal, _, edge = chunk_masks(c, segc)
        causal4 = four(causal)
        keep = twice(keepc[rows, :])
        come = twice(edge["from_before"])
        come_low = come.astype(BF16)
        carry = twice(edge["carry_on"])
        qc, kc, vc, wc = q[g, rows, :], k[g, rows, :], v[g, rows, :], w[g, rows, :]
        kw_low, wv_low = state_k.astype(BF16), state_v.astype(BF16)
        kw_all[g, c] = kw_low
        wv_all[g, c] = wv_low
        ws = head_stack(wc)
        pairs = (dot_rt(qc, head_stack(kc)) * causal4).astype(BF16)
        total = dot(causal.astype(BF16), wc) + come * state_z + (1.0 - keep)
        inverse = 1.0 / total
        scores = (dot(pairs, ws) + dot(qc * come_low, kw_low)) * (inverse * (HEAD_DIM**-0.5))
        powers = jnp.exp(scores - head_max(scores))
        chances = powers / head_sum(powers, ones)
        ratio = (chances * inverse).astype(BF16)
        probs[g, rows, :] = chances
        inv[g, rows, :] = inverse
        score[g, rows, :] = scores
        mixing = (dot_rt(ratio, ws) * causal4).astype(BF16)
        out = dot(mixing, head_stack(vc)) + dot(ratio * come_low, wv_low)
        mixed[g, rows, :] = (out * keep).astype(BF16)
        wg = wc * twice(edge["to_after"]).astype(BF16)
        state_k = state_k * carry + jnp.where(blocks, dot_lt(kc, wg), 0.0)
        state_v = state_v * carry + jnp.where(blocks, dot_lt(wg, vc), 0.0)
        state_z = state_z * carry + jnp.sum(wg.astype(F32), axis=0, keepdims=True)
    kw[...] = state_k
    wv[...] = state_v
    zsum[...] = jnp.broadcast_to(state_z, zsum.shape)


def mix_backward(
    g, i, segc, keepc, q, k, v, w, probs, inv, score, gm, rg, uq, zgrad, kw_all, wv_all, gy
):
    blocks = head_blocks()
    ones = jnp.where(blocks, 1.0, 0.0).astype(BF16)
    state_v, state_k, state_z = rg[...], uq[...], zgrad[0:1, :]
    for n in range(2):
        c = 2 * i + 1 - n
        rows = pl.ds(pl.multiple_of(c * CHUNK, CHUNK), CHUNK)
        causal, anti, edge = chunk_masks(c, segc)
        causal4, anti4 = four(causal), four(anti)
        anti_low = anti.astype(BF16)
        come_low = twice(edge["from_before"]).astype(BF16)
        late = twice(edge["from_after"])
        late_low = late.astype(BF16)
        back = twice(edge["to_before"])
        back_low = back.astype(BF16)
        carry = twice(edge["carry_back"])
        qc, kc, vc, wc = q[g, rows, :], k[g, rows, :], v[g, rows, :], w[g, rows, :]
        grad = gm[g, rows, :]
        chances, inverse, scores = probs[g, rows, :], inv[g, rows, :], score[g, rows, :]
        ratio = (chances * inverse).astype(BF16)
        ws, grads, ratios = head_stack(wc), head_stack(grad), head_stack(ratio)
        d_mixing = (dot_rt(grad, head_stack(vc)) * causal4).astype(BF16)
        d_ratio = dot(d_mixing, ws) + dot_rt(grad * come_low, wv_all[g, c])
        d_chance = d_ratio * inverse
        weighted = d_chance * chances
        d_score = weighted - chances * head_sum(weighted, ones)
        d_pw = (d_score * inverse * (HEAD_DIM**-0.5)).astype(BF16)
        d_total = (weighted + d_score * scores) * inverse
        d_pairs = (dot_rt(d_pw, ws) * causal4).astype(BF16)
        gq = dot(d_pairs, head_stack(kc)) + dot_rt(d_pw * come_low, kw_all[g, c])
        rg_low, uq_low = state_v.astype(BF16), state_k.astype(BF16)
        d_pws, queries = head_stack(d_pw), head_stack(qc)
        mixing_t = (dot_rt(wc, ratios) * anti4).astype(BF16)
        w_late = wc * late_low
        gv = dot(mixing_t, grads) + dot(w_late, rg_low)
        d_pairs_t = (dot_rt(wc, d_pws) * anti4).astype(BF16)
        gk = dot(d_pairs_t, queries) + dot(w_late, uq_low)
        d_mixing_t = (dot_rt(vc, grads) * anti4).astype(BF16)
        pairs_t = (dot_rt(kc, queries) * anti4).astype(BF16)
        z_high = d_total.astype(BF16)
        z_low = (d_total - z_high.astype(F32)).astype(BF16)
        dw = dot(d_mixing_t, ratios) + dot(pairs_t, d_pws)
        dw += dot_rt(vc * late_low, rg_low) + dot_rt(kc * late_low, uq_low)
        dw -= dot(anti_low, z_high) + dot(anti_low, z_low) + late * state_z
        gy[g, rows, 0:256] = gq.astype(BF16)
        gy[g, rows, 256:512] = gk.astype(BF16)
        gy[g, rows, 512:768] = gv.astype(BF16)
        gy[g, rows, 768:1024] = (dw * wc.astype(F32)).astype(BF16)
        state_v = state_v * carry + jnp.where(blocks, dot_lt(ratio * back_low, grad), 0.0)
        state_k = state_k * carry + jnp.where(blocks, dot_lt(d_pw * back_low, qc), 0.0)
        state_z = state_z * carry + jnp.sum(d_total * back, axis=0, keepdims=True)
    rg[...] = state_v
    uq[...] = state_k
    zgrad[...] = jnp.broadcast_to(state_z, zgrad.shape)


def feed_up(r, tok, gain, up_bias, wb, mixed, n2, act, lin, gh):
    rows = pl.ds(pl.multiple_of(r * TILE, TILE), TILE)
    hidden = tok[rows, :].astype(F32)
    for g in range(2):
        hidden += dot_rt(mixed[g, rows, :], flat(wb[g, ..., 0:256]))
    gh[rows, :] = hidden
    hat, _ = standardise(hidden)
    normed = (hat * gain[...]).astype(BF16)
    n2[rows, :] = normed
    k0 = 0.7978845608
    k1 = k0 * 0.044715
    for g in range(2):
        for j in range(4):
            here = slice(j * 256, (j + 1) * 256)
            unit = g * 1024 + j * 256
            up = flat(wb[g, ..., 256 + j * 256 : 512 + j * 256])
            linear = dot(normed, up) + up_bias[:, unit : unit + 256]
            square = linear * linear
            gate = 0.5 * jnp.tanh(linear * (square * k1 + k0)) + 0.5
            active = linear * gate
            slope = gate + active * (1.0 - gate) * (square * (6.0 * k1) + 2.0 * k0)
            act[g, rows, here] = active.astype(BF16)
            lin[g, rows, here] = slope.astype(BF16)


def feed_down(r, cot, gain, down_bias, wb, keepc, act, lin, gh, gb, gm, small, out):
    rows = pl.ds(pl.multiple_of(r * TILE, TILE), TILE)
    grad = cot[rows, :]
    hidden = gh[rows, :]
    total = hidden + down_bias[...]
    back = jnp.zeros((TILE, 512), F32)
    for g in range(2):
        for j in range(4):
            here = slice(j * 256, (j + 1) * 256)
            unit = g * 1024 + j * 256
            down = flat(wb[g, ..., 1280 + j * 256 : 1536 + j * 256])
            grad_low = (dot(grad, down) * lin[g, rows, here].astype(F32)).astype(BF16)
            lin[g, rows, here] = grad_low
            row, column = 4 + unit // 512, unit % 512
            small[row : row + 1, column : column + 256] += jnp.sum(
                grad_low.astype(F32), axis=0, keepdims=True
            )
    for g in range(2):
        total += dot_rt(act[g, rows, :], flat(wb[g, ..., 1280:2304]))
        back += dot_rt(lin[g, rows, :], flat(wb[g, ..., 256:1280]))
    out[rows, :] = total.astype(BF16)
    hat, scale = standardise(hidden)
    scaled = back * gain[...]
    inner = scaled - jnp.mean(scaled, axis=-1, keepdims=True)
    inner -= hat * jnp.mean(scaled * hat, axis=-1, keepdims=True)
    grad_f32 = grad.astype(F32)
    grad_hidden = grad_f32 + scale * inner
    gh[rows, :] = grad_hidden
    low = grad_hidden.astype(BF16)
    gb[rows, :] = low
    small[0:1, :] += jnp.sum(back * hat, axis=0, keepdims=True)
    small[2:3, :] += jnp.sum(grad_f32, axis=0, keepdims=True)
    keep = twice(keepc[rows, :])
    for g in range(2):
        gm[g, rows, :] = (dot(low, flat(wb[g, ..., 0:256])) * keep).astype(BF16)


def transpose_into(source, target, length):
    for r in range(length // TILE):
        target[:, r * TILE : (r + 1) * TILE] = source[r * TILE : (r + 1) * TILE, :].T


def weight_grad(left_t, right, target, g, target_column, columns):
    shape = target.shape[1:-1] + (256,)

    def step(j, carry):
        here = pl.ds(pl.multiple_of(j * 256, 256), 256)
        there = pl.ds(pl.multiple_of(target_column + j * 256, 256), 256)
        target[g, ..., there] = dot(left_t[...], right[:, here]).astype(BF16).reshape(shape)
        return carry

    lax.fori_loop(0, columns // 256, step, 0)


def finish(r, tok, gain, wa, gy, gh, small, grad_out):
    rows = pl.ds(pl.multiple_of(r * TILE, TILE), TILE)
    hat, scale = standardise(tok[rows, :].astype(F32))
    back = dot_rt(gy[0, rows, :], flat(wa[0])) + dot_rt(gy[1, rows, :], flat(wa[1]))
    scaled = back * gain[...]
    inner = scaled - jnp.mean(scaled, axis=-1, keepdims=True)
    inner -= hat * jnp.mean(scaled * hat, axis=-1, keepdims=True)
    grad_out[rows, :] = (gh[rows, :] + scale * inner).astype(BF16)
    small[1:2, :] += jnp.sum(back * hat, axis=0, keepdims=True)


class Quiet:
    def nothing(self, *at):
        pass

    before = weights_a = mixing = weights_up = feeding = weights_down = nothing
    grads_down = grads_up = mixing_back = grads_a = finishing = after = nothing


LAYER_INPUTS = 8


def layer_body(
    length,
    comm,
    tok,
    cot,
    seg_row,
    pad_row,
    gain_one,
    gain_two,
    up_bias,
    down_bias,
    wa,
    wb,
    out,
    grad_out,
    ga,
    gw,
    small,
    segc,
    keepc,
    n1,
    q,
    k,
    v,
    w,
    probs,
    inv,
    score,
    mixed,
    state_k,
    state_v,
    state_z,
    kw_all,
    wv_all,
    n2,
    act,
    lin,
    gh,
    gb,
    gm,
    flip,
):
    pairs, tiles = length // (2 * CHUNK), length // TILE

    def clear():
        state_k[...] = jnp.zeros_like(state_k)
        state_v[...] = jnp.zeros_like(state_v)
        state_z[...] = jnp.zeros_like(state_z)

    comm.before()
    small[...] = jnp.zeros_like(small)
    rows_to_columns(seg_row, pad_row, segc, keepc, length)

    @pl.loop(0, tiles)
    def _(r):
        normalise(r, tok, gain_one, n1)

    @pl.loop(0, 2)
    def _(g):
        comm.weights_a(g)
        clear()

        @pl.loop(0, tiles)
        def _(r):
            project(g, r, wa, keepc, n1, q, k, v, w)

        @pl.loop(0, pairs)
        def _(i):
            comm.mixing(g, i)
            mix_forward(
                g, i, segc, keepc, q, k, v, w, probs, inv, score, mixed, state_k, state_v, state_z,
                kw_all, wv_all,
            )

    comm.weights_up()

    @pl.loop(0, tiles)
    def _(r):
        comm.feeding(r)
        feed_up(r, tok, gain_two, up_bias, wb, mixed, n2, act, lin, gh)

    comm.weights_down()

    @pl.loop(0, tiles)
    def _(r):
        feed_down(r, cot, gain_two, down_bias, wb, keepc, act, lin, gh, gb, gm, small, out)

    transpose_into(cot, flip, length)
    for g in range(2):
        weight_grad(flip, act.at[g], gw, g, 1280, 1024)
    comm.grads_down()
    transpose_into(n2, flip, length)
    for g in range(2):
        weight_grad(flip, lin.at[g], gw, g, 256, 1024)
    transpose_into(gb, flip, length)
    for g in range(2):
        weight_grad(flip, mixed.at[g], gw, g, 0, GROUP)
    comm.grads_up()
    transpose_into(n1, flip, length)

    @pl.loop(0, 2)
    def _(g):
        clear()

        @pl.loop(0, pairs)
        def _(i):
            comm.mixing_back(g, i)
            mix_backward(
                g, pairs - 1 - i, segc, keepc, q, k, v, w, probs, inv, score, gm, state_v, state_k,
                state_z, kw_all, wv_all, act,
            )

        weight_grad(flip, act.at[g], ga, g, 0, 1024)
        comm.grads_a(g)

    @pl.loop(0, tiles)
    def _(r):
        comm.finishing(r)
        finish(r, tok, gain_one, wa, act, gh, small, grad_out)

    comm.after()


def layer_scratch(length, width):
    vmem = pltpu.VMEM
    chunks = length // CHUNK
    return [
        vmem((length + 16, 128), F32),
        vmem((length, 128), F32),
        vmem((length, width), BF16),
        vmem((2, length, GROUP), BF16),
        vmem((2, length, GROUP), BF16),
        vmem((2, length, GROUP), BF16),
        vmem((2, length, GROUP), BF16),
        vmem((2, length, GROUP), F32),
        vmem((2, length, GROUP), F32),
        vmem((2, length, GROUP), F32),
        vmem((2, length, GROUP), BF16),
        vmem((GROUP, GROUP), F32),
        vmem((GROUP, GROUP), F32),
        vmem((8, GROUP), F32),
        vmem((2, chunks, GROUP, GROUP), BF16),
        vmem((2, chunks, GROUP, GROUP), BF16),
        vmem((length, width), BF16),
        vmem((2, length, 1024), BF16),
        vmem((2, length, 1024), BF16),
        vmem((length, width), F32),
        vmem((length, width), BF16),
        vmem((2, length, GROUP), BF16),
        vmem((width, length), BF16),
    ]


def layer_kernel(length, *refs):
    layer_body(length, Quiet(), *refs)


def layer(tokens, cotangent, seg_row, pad_row, gain_one, gain_two, up_bias, down_bias, wa, wb):
    length, width = tokens.shape
    shape = jax.ShapeDtypeStruct
    cut = lambda full: full.reshape(2, -1, 2, 2, 2, 16, full.shape[-1])
    wa, wb = cut(wa), cut(wb)
    space = pl.BlockSpec(memory_space=pltpu.VMEM)
    out, grad_out, ga, gw, small = pl.pallas_call(
        functools.partial(layer_kernel, length),
        out_shape=(
            shape((length, width), BF16),
            shape((length, width), BF16),
            shape(wa.shape, BF16),
            shape(wb.shape, BF16),
            shape((8, width), F32),
        ),
        in_specs=[space] * 10,
        out_specs=tuple([space] * 5),
        scratch_shapes=layer_scratch(length, width),
        compiler_params=pltpu.CompilerParams(vmem_limit_bytes=60 * 1024 * 1024),
        name="layer",
    )(tokens, cotangent, seg_row, pad_row, gain_one, gain_two, up_bias, down_bias, wa, wb)
    whole = lambda full: full.reshape(2, width, full.shape[-1])
    return out, grad_out, whole(ga), whole(gw), small


class Place:
    def __init__(self, depth):
        index = lax.axis_index("dp")
        t = lax.axis_index("tensor")
        x, y, z = lax.rem(index, 2), lax.rem(index // 2, 2), index // 4
        self.depth = depth
        self.x, self.y, self.z, self.t, self.other = x, y, z, t, 1 - t
        self.near = (y + t * (1 - 2 * y), x + (1 - t) * (1 - 2 * x))
        self.next = (y + (1 - t) * (1 - 2 * y), x + t * (1 - 2 * x))
        self.far = (1 - y, 1 - x)
        chip = lambda z, y, x: (z * 2 + y) * 2 + x
        self.levels = [lax.rem(z + s, depth) for s in range(depth)]
        self.chips_z = [chip(level, y, x) for level in self.levels]
        self.to_near = {"dp": chip(z, *self.near)}
        self.to_next = {"dp": chip(z, *self.next)}
        self.to_pair = {"tensor": self.other}
        self.spot = (y * 2 + x) * 2 + t
        flip = lambda value, bit: value + bit * (1 - 2 * value)
        self.level = [
            {
                "dp": chip(z, flip(y, offset // 4), flip(x, offset // 2 % 2)),
                "tensor": flip(t, offset % 2),
            }
            for offset in range(8)
        ]

    def along_z(self, step, core):
        return {"dp": self.chips_z[step], "tensor": core}

    def greet(self):
        barrier = pltpu.get_barrier_semaphore()
        friends = self.level[1:]
        friends += [self.along_z(s, core) for s in range(1, self.depth) for core in range(2)]
        for friend in friends:
            pl.semaphore_signal(barrier, inc=1, device_id=friend, device_id_type=MESH)
        pl.semaphore_wait(barrier, len(friends))


class Copies:
    def __init__(self, sems):
        self.sems = sems
        self.started = []

    def build(self, source, target, device, out_sem, in_sem):
        return pltpu.make_async_remote_copy(
            src_ref=source,
            dst_ref=target,
            send_sem=self.sems.at[0, out_sem],
            recv_sem=self.sems.at[1, in_sem],
            device_id=device,
            device_id_type=MESH,
        )

    def start(self, source, target, device, number, in_sem=None, only=None):
        def begin():
            landing = number if in_sem is None else in_sem
            self.build(source(), target, device, number, landing).start()

        begin() if only is None else pl.when(only)(begin)
        self.started.append((source, number, only))

    def landed(self, target, number, only=None):
        def wait():
            self.build(target, target, {"tensor": 0}, number, number).wait_recv()

        wait() if only is None else pl.when(only)(wait)

    def left(self):
        for source, number, only in self.started:

            def wait(source=source, number=number):
                part = source()
                self.build(part, part, {"tensor": 0}, number, number).wait_send()

            wait() if only is None else pl.when(only)(wait)


class Gather(Copies):
    COPIES = 14

    def __init__(self, place, own, full, group, columns, sems):
        super().__init__(sems)
        self.p, self.own, self.full, self.columns = place, own, full, columns
        self.group = group
        self.groups = slice(None) if group is None else slice(group, group + 1)
        self.mine = None if group is None else place.t == group
        self.pairs = None if group is None else place.t != group

    def at(self, g, z, spot, half):
        return self.full.at[g, z, spot[0], spot[1], half, :, self.columns]

    def block(self, spot, half):
        return self.at(self.groups, slice(None), spot, half)

    def forward(self, spot, device, number):
        block = lambda: self.block(spot, self.p.t)
        self.start(block, block(), device, number)

    def first(self):
        p = self.p
        here = (p.y, p.x)
        for s in range(1, p.depth):
            for core in range(2):
                self.start(
                    lambda core=core: self.own.at[core, :, self.columns],
                    self.at(p.t, p.z, here, core),
                    p.along_z(s, core),
                    2 * (s - 1) + core,
                    2 * (s - 1) + p.t,
                    only=self.mine,
                )
        self.start(
            lambda: self.own.at[p.other, :, self.columns],
            self.at(p.t, p.z, here, p.other),
            p.to_pair,
            6,
            only=self.mine,
        )

        def keep():
            self.full[p.t, p.z, p.y, p.x, p.t, :, self.columns] = self.own[p.t, :, self.columns]

        keep() if self.mine is None else pl.when(self.mine)(keep)

    def second(self):
        p = self.p
        here = (p.y, p.x)
        for n in range(6):
            if self.group is None or n % 2 == self.group:
                self.landed(self.at(p.t, p.z, here, p.t), n)
        self.landed(self.at(p.t, p.z, here, p.t), 6, only=self.pairs)
        self.forward(here, p.to_near, 7)
        self.forward(here, p.to_next, 8)
        self.forward(here, p.to_pair, 9)

    def third(self):
        p = self.p
        self.landed(self.block(p.near, p.t), 7)
        self.forward(p.near, p.to_next, 10)
        self.forward(p.near, p.to_pair, 11)
        self.landed(self.block(p.next, p.t), 8)
        self.forward(p.next, p.to_pair, 12)

    def fourth(self):
        p = self.p
        self.landed(self.block(p.far, p.t), 10)
        self.forward(p.far, p.to_pair, 13)

    def last(self):
        p = self.p
        for n in (9, 11, 12, 13):
            self.landed(self.block((p.y, p.x), p.other), n)


class Scatter(Copies):
    COPIES = 11

    def __init__(self, place, part, group, columns, pair_in, near_in, next_in, last_in, sems):
        super().__init__(sems)
        self.p, self.part, self.columns = place, part, columns
        self.pair_in, self.near_in, self.next_in, self.last_in = pair_in, near_in, next_in, last_in
        self.group = group
        self.groups = slice(None) if group is None else slice(group, group + 1)
        self.mine = None if group is None else place.t == group
        self.pairs = None if group is None else place.t != group

    def at(self, g, z, spot, half):
        return self.part.at[g, z, spot[0], spot[1], half, :, self.columns]

    def block(self, spot, half):
        return self.at(self.groups, slice(None), spot, half)

    def add(self, spot, landed):
        p = self.p
        here = (self.groups, slice(None), spot[0], spot[1], p.t, slice(None), self.columns)
        self.part[here] = (self.part[here].astype(F32) + landed.astype(F32)).astype(BF16)

    def first(self):
        p = self.p
        self.start(
            lambda: self.part.at[self.groups, :, :, :, p.other, :, self.columns],
            self.pair_in,
            p.to_pair,
            0,
        )

    def second(self):
        p = self.p
        self.landed(self.pair_in, 0)
        for spot, number in ((p.far, 1), (p.near, 2)):
            self.add(spot, self.pair_in[:, :, spot[0], spot[1]])
            self.start(
                lambda spot=spot: self.block(spot, p.t),
                self.near_in.at[number - 1],
                p.to_near,
                number,
            )
        for spot in (p.next, (p.y, p.x)):
            self.add(spot, self.pair_in[:, :, spot[0], spot[1]])

    def third(self):
        p = self.p
        self.landed(self.near_in.at[0], 1)
        self.add(p.next, self.near_in[0])
        self.start(lambda: self.block(p.next, p.t), self.next_in, p.to_next, 3)
        self.landed(self.near_in.at[1], 2)
        self.add((p.y, p.x), self.near_in[1])

    def fourth(self):
        p = self.p
        here = (p.y, p.x)
        self.landed(self.next_in, 3)
        self.add(here, self.next_in[...])
        for s in range(1, p.depth):
            for core in range(2) if self.group is None else (self.group,):
                self.start(
                    lambda s=s, core=core: self.at(core, p.levels[s], here, p.t),
                    self.last_in.at[2 * (s - 1) + p.t],
                    p.along_z(s, core),
                    4 + 2 * (s - 1) + core,
                    4 + 2 * (s - 1) + p.t,
                )
        self.start(
            lambda: self.at(p.other, p.z, here, p.t),
            self.last_in.at[2 * (p.depth - 1)],
            p.to_pair,
            10,
            only=self.pairs,
        )

    def last(self, target):
        p = self.p

        def write():
            for n in range(7):
                self.landed(self.last_in.at[n], 4 + n)
            mine = self.part[p.t, p.z, p.y, p.x, p.t, :, self.columns].astype(F32)
            rest = self.last_in[2 * (p.depth - 1)].astype(F32)
            for s in range(1, p.depth):
                mine += self.last_in[2 * (s - 1) + p.t].astype(F32)
                rest += self.last_in[2 * (s - 1) + p.other].astype(F32)
            target[p.t] = mine
            target[p.other] = rest

        write() if self.mine is None else pl.when(self.mine)(write)


def scatter_scratch(groups, depth, columns):
    vmem = pltpu.VMEM
    return [
        vmem((groups, depth, 2, 2, 16, columns), BF16),
        vmem((2, groups, depth, 16, columns), BF16),
        vmem((groups, depth, 16, columns), BF16),
        vmem((2 * depth - 1, 16, columns), BF16),
        pltpu.SemaphoreType.DMA((2, Scatter.COPIES)),
    ]


class Reduce(Copies):
    COPIES = 12

    def __init__(self, place, own, parts, sums, sems):
        super().__init__(sems)
        self.p, self.own, self.parts, self.sums = place, own, parts, sums

    def first(self):
        p = self.p
        self.parts[p.spot] = self.own[...]
        for offset in range(1, 8):
            self.start(
                lambda: self.own, self.parts.at[p.spot], p.level[offset], offset - 1
            )

    def second(self):
        p = self.p
        for n in range(7):
            self.landed(self.own, n)
        total = self.parts[0]
        for spot in range(1, 8):
            total += self.parts[spot]
        self.sums[p.z] = total
        for s in range(1, p.depth):
            self.start(
                lambda: self.sums.at[p.z], self.sums.at[p.z], {"dp": p.chips_z[s]}, 6 + s
            )

    def last(self):
        p = self.p
        for s in range(1, p.depth):
            self.landed(self.own, 6 + s)
        total = self.sums[0]
        for z in range(1, p.depth):
            total += self.sums[z]
        return total


class Woven:
    def __init__(self, place, owns, own_a, own_b, wa, wb, ga, gw, gains, gathers, scatters, targets):
        self.p = place
        self.owns, self.own_a, self.own_b = owns, own_a, own_b
        every, up, down = slice(0, 1024), slice(0, 1280), slice(1280, 2304)
        self.a = [Gather(place, own_a, wa, g, every, gathers[g]) for g in range(2)]
        self.up = Gather(place, own_b, wb, None, up, gathers[2])
        self.down = Gather(place, own_b, wb, None, down, gathers[3])
        self.down_grad = Scatter(place, gw, None, down, *scatters[0])
        self.up_grad = Scatter(place, gw, None, up, *scatters[1])
        self.a_grad = [Scatter(place, ga, g, every, *scatters[2 + g]) for g in range(2)]
        self.gains = gains
        self.da, self.dw = targets

    def before(self):
        query, key, value, slot, out_t, up, down_t = self.owns
        halves = lambda ref: ref[...].astype(BF16).reshape(2, 16, ref.shape[1])
        self.own_a[:, :, 0:256] = halves(query)
        self.own_a[:, :, 256:512] = halves(key)
        self.own_a[:, :, 512:768] = halves(value)
        self.own_a[:, :, 768:1024] = halves(slot)
        self.p.greet()
        self.a[0].first()
        self.a[1].first()
        self.own_b[:, :, 0:256] = halves(out_t)
        self.own_b[:, :, 256:1280] = halves(up)
        self.own_b[:, :, 1280:2304] = halves(down_t)

    def weights_a(self, g):
        one, two = self.a

        @pl.when(g == 0)
        def _():
            one.second()
            two.second()
            self.up.first()
            one.third()
            one.fourth()
            one.last()
            two.third()

        @pl.when(g == 1)
        def _():
            two.last()

    def mixing(self, g, i):
        steps = {
            (0, 0): (self.a[1].fourth, self.up.second, self.down.first),
            (1, 0): (self.up.third, self.down.second),
            (1, 2): (self.up.fourth,),
            (1, 3): (self.down.third,),
        }
        for (group, pair), calls in steps.items():

            @pl.when((g == group) & (i == pair))
            def _(calls=calls):
                for call in calls:
                    call()

    def weights_up(self):
        self.up.last()

    def feeding(self, r):
        pl.when(r == 1)(self.down.fourth)

    def weights_down(self):
        self.down.last()

    def grads_down(self):
        self.down_grad.first()

    def grads_up(self):
        self.up_grad.first()
        self.down_grad.second()

    def mixing_back(self, g, i):
        steps = {
            (0, 1): (self.up_grad.second,),
            (0, 2): (self.down_grad.third,),
            (0, 3): (self.up_grad.third,),
            (1, 0): (self.down_grad.fourth,),
            (1, 1): (self.up_grad.fourth, self.a_grad[0].second),
            (1, 3): (self.a_grad[0].third,),
        }
        for (group, pair), calls in steps.items():

            @pl.when((g == group) & (i == pair))
            def _(calls=calls):
                for call in calls:
                    call()

    def grads_a(self, g):
        for group in range(2):
            pl.when(g == group)(self.a_grad[group].first)

        @pl.when(g == 1)
        def _():
            self.a_grad[0].fourth()
            self.down_grad.last(self.dw.at[:, :, 1280:2304])
            self.up_grad.last(self.dw.at[:, :, 0:1280])

    def finishing(self, r):
        pl.when(r == 1)(self.a_grad[1].second)

    def after(self):
        self.gains.first()
        self.a_grad[1].third()
        self.gains.second()
        self.a_grad[0].last(self.da)
        self.a_grad[1].fourth()
        self.total = self.gains.last()
        self.a_grad[1].last(self.da)
        for copies in (
            *self.a, self.up, self.down, self.down_grad, self.up_grad, *self.a_grad, self.gains
        ):
            copies.left()


def woven_kernel(length, depth, *refs):
    refs = list(refs)
    take = lambda n: [refs.pop(0) for _ in range(n)]
    tok, cot, seg_rows, pad_rows, gain_one, gain_two, up_bias, down_bias = take(LAYER_INPUTS)
    owns = take(7)
    out, grad_out, da, dw, small_out = take(5)
    own_a, own_b, wa, wb, ga, gw, seg_row, pad_row = take(8)
    small, parts, sums, gain_sems = take(4)
    gathers = take(4)
    scatters = [take(5) for _ in range(4)]
    place = Place(depth)
    gains = Reduce(place, small, parts, sums, gain_sems)
    comm = Woven(place, owns, own_a, own_b, wa, wb, ga, gw, gains, gathers, scatters, (da, dw))
    first = lax.axis_index("tensor") == 0
    for rows, row in ((seg_rows, seg_row), (pad_rows, pad_row)):
        row[...] = jnp.where(first, rows[0:1, :], rows[1:2, :])
    layer_body(
        length, comm, tok, cot, seg_row, pad_row, gain_one, gain_two, up_bias, down_bias, wa, wb,
        out, grad_out, ga, gw, small, *refs,
    )
    small_out[...] = comm.total


def write_kernel(out_in, grad_in, da, dw, small, *refs):
    (
        out, grad_out, mixer_gain, query, key, value, slot, out_t, feed_gain, up, up_bias, down_t,
        down_bias, sems,
    ) = refs
    one = pltpu.make_async_copy(out_in, out, sems.at[0])
    two = pltpu.make_async_copy(grad_in, grad_out, sems.at[1])
    one.start()
    two.start()
    rows = lambda part: part.reshape(-1, part.shape[-1])
    query[...] = rows(da[:, :, 0:256])
    key[...] = rows(da[:, :, 256:512])
    value[...] = rows(da[:, :, 512:768])
    slot[...] = rows(da[:, :, 768:1024])
    out_t[...] = rows(dw[:, :, 0:256])
    up[...] = rows(dw[:, :, 256:1280])
    down_t[...] = rows(dw[:, :, 1280:2304])
    feed_gain[...] = small[0:1, :]
    mixer_gain[...] = small[1:2, :]
    down_bias[...] = small[2:3, :]
    for row in range(4):
        up_bias[:, row * 512 : (row + 1) * 512] = small[4 + row : 5 + row, :]
    one.wait()
    two.wait()


def write(out, grad_out, da, dw, small):
    shape = jax.ShapeDtypeStruct
    space = pl.BlockSpec(memory_space=pltpu.VMEM)
    far = pl.BlockSpec(memory_space=pl.ANY)
    width = out.shape[1]
    square, wide = shape((32, 256), F32), shape((32, 1024), F32)
    row = shape((1, width), F32)
    return pl.pallas_call(
        write_kernel,
        out_shape=(
            shape(out.shape, BF16),
            shape(out.shape, BF16),
            row,
            square,
            square,
            square,
            square,
            square,
            row,
            wide,
            shape((1, 4 * width), F32),
            wide,
            row,
        ),
        in_specs=[far, far, space, space, space],
        out_specs=(far, far) + (space,) * 11,
        scratch_shapes=[pltpu.SemaphoreType.DMA((2,))],
        name="write",
    )(out, grad_out, da, dw, small)


def woven(depth, tokens, cotangent, segments, padding, gains, biases, owns):
    length, width = tokens.shape
    shape = jax.ShapeDtypeStruct
    space = pl.BlockSpec(memory_space=pltpu.VMEM)
    vmem = pltpu.VMEM
    dma = pltpu.SemaphoreType.DMA
    full = lambda columns: vmem((2, depth, 2, 2, 2, 16, columns), BF16)
    return pl.pallas_call(
        functools.partial(woven_kernel, length, depth),
        out_shape=(
            shape((length, width), BF16),
            shape((length, width), BF16),
            shape((2, 16, 1024), F32),
            shape((2, 16, 2304), F32),
            shape((8, width), F32),
        ),
        in_specs=[space] * (LAYER_INPUTS + 7),
        out_specs=tuple([space] * 5),
        scratch_shapes=[
            vmem((2, 16, 1024), BF16),
            vmem((2, 16, 2304), BF16),
            full(1024),
            full(2304),
            full(1024),
            full(2304),
            vmem((1, length), jnp.int32),
            vmem((1, length), jnp.int32),
            vmem((8, width), F32),
            vmem((8, 8, width), F32),
            vmem((depth, 8, width), F32),
            dma((2, Reduce.COPIES)),
        ]
        + [dma((2, Gather.COPIES))] * 4
        + scatter_scratch(2, depth, 1024)
        + scatter_scratch(2, depth, 1280)
        + scatter_scratch(1, depth, 1024)
        + scatter_scratch(1, depth, 1024)
        + layer_scratch(length, width),
        compiler_params=pltpu.CompilerParams(
            collective_id=0, has_side_effects=True, vmem_limit_bytes=62 * 1024 * 1024
        ),
        name="woven",
    )(tokens, cotangent, segments, padding, *gains, *biases, *owns)


def per_device(
    direct,
    tokens,
    segment_ids,
    padding,
    mixer_gain,
    query_weight,
    key_weight,
    value_weight,
    slot_weight,
    out_weight,
    feed_gain,
    up_weight,
    up_bias,
    down_weight,
    down_bias,
    cotangent,
):
    gains = (mixer_gain[None], feed_gain[None])
    biases = (up_bias[None], down_bias[None])
    if direct:
        owns = (
            query_weight, key_weight, value_weight, slot_weight, out_weight.T, up_weight,
            down_weight.T,
        )
        depth = lax.axis_size("dp") // 4
        results = write(
            *woven(depth, tokens, cotangent, segment_ids, padding, gains, biases, owns)
        )
        (
            out, grad_out, gain_one, query, key, value, slot, out_t, gain_two, up, bias_one, down_t,
            bias_two,
        ) = results
        return (
            out, grad_out, gain_one[0], query, key, value, slot, out_t.T, gain_two[0], up,
            bias_one[0], down_t.T, bias_two[0],
        )
    own_a = jnp.concatenate([query_weight, key_weight, value_weight, slot_weight], 1)
    own_b = jnp.concatenate([out_weight.T, up_weight, down_weight.T], 1)
    wa, wb = (
        lax.all_gather(lax.all_gather(own.astype(BF16), "dp", axis=0, tiled=True), "tensor")
        for own in (own_a, own_b)
    )
    half = lax.axis_index("tensor")
    pick = lambda rows: lax.dynamic_slice_in_dim(rows, half, 1, 0)
    out, grad_out, ga, gw, small = layer(
        tokens, cotangent, pick(segment_ids), pick(padding), *gains, *biases, wa, wb
    )
    da, dw = (
        lax.psum_scatter(
            lax.psum_scatter(part.astype(F32), "tensor", scatter_dimension=0),
            "dp",
            scatter_dimension=0,
            tiled=True,
        )
        for part in (ga, gw)
    )
    small = lax.psum(small, ("dp", "tensor"))
    return (
        out,
        grad_out,
        small[1],
        da[:, 0:256],
        da[:, 256:512],
        da[:, 512:768],
        da[:, 768:1024],
        dw[:, 0:256].T,
        small[0],
        dw[:, 256:1280],
        small[4:8].reshape(-1),
        dw[:, 1280:2304].T,
        small[2],
    )


def solution(mesh):
    in_specs = (
        P(("dp", "tensor"), None),
        P("dp", None),
        P("dp", None),
        P(),
        P("dp", "tensor"),
        P("dp", "tensor"),
        P("dp", "tensor"),
        P("dp", "tensor"),
        P("tensor", "dp"),
        P(),
        P("dp", "tensor"),
        P(),
        P("tensor", "dp"),
        P(),
        P(("dp", "tensor"), None),
    )
    out_specs = (
        P(("dp", "tensor"), None),
        P(("dp", "tensor"), None),
        P(),
        P("dp", "tensor"),
        P("dp", "tensor"),
        P("dp", "tensor"),
        P("dp", "tensor"),
        P("tensor", "dp"),
        P(),
        P("dp", "tensor"),
        P(),
        P("tensor", "dp"),
        P(),
    )
    direct = mesh.shape["dp"] == 16 and mesh.shape["tensor"] == 2
    return jax.shard_map(
        functools.partial(per_device, direct),
        mesh=mesh,
        in_specs=in_specs,
        out_specs=out_specs,
        check_vma=False,
    )
```

time: 158 us -> 202 us (1.28)
  Pallas kernels: 149 us -> 201 us
  local copies, waits for them, and re-layouts: 6.78 us -> 0 us
    pallas_call x0 -> x1, Pallas kernels: none -> 66.4 us  [write(): pl.pallas_call(write_kernel, out_shape=(shape(out.shape, BF16), shape(out...]
    pallas_call x1, Pallas kernels: 149 us -> 135 us  [woven(): pl.pallas_call(functools.partial(woven_kernel, length, depth), out_shape=...]
    unnamed x10 -> x0, local copies, waits for them, and re-layouts: 3.94 us -> none
    slice x2 -> x0, local copies, waits for them, and re-layouts: 2.12 us -> none  [the longest x1 1.53 us: per_device(): da[:, 768:1024]]
where the time goes in v3:
time: 202 us
  Pallas kernels  201 us (100%)
    pallas_call x1, Pallas kernels, woven(): pl.pallas_call(functools.partial(woven_kernel, length, depth), out_shape=...  135 us
    pallas_call x1, Pallas kernels, write(): pl.pallas_call(write_kernel, out_shape=(shape(out.shape, BF16), shape(out...  66.4 us

profile of v3, /device:TPU:1, one launch (start us, length us, event | category | flops | bytes accessed | tf_op | source)
XLA Modules:
  0.0 202.1 jit_solution(15441582227367566428)
XLA Ops:
  0.7 134.9 %woven.1 = (bf16[1024,512]{1,0:T(8,128)(2,1)}, bf16[1024,512]{1,0:T(8,128)(2,1)}, f32[2,16,1024]{2,1,0:T(8,128)}, f32[2,16,2304]{2,1,0:T(8,128)}, f32[8,512]{1,0:T(8,128)}) custom-call(bf16[1024,512]{1,0:T(8,128)(2,1)} %refs_0_.1, bf16[1024,512]{1,0:T(8,128)(2,1)} %refs_1_.1, s32[2,1024]{1,0:T(2,128)} %refs_2_.1, s32[2,1024]{1,0:T(2,128)} %refs_3_.1, ...), custom_call_target="tpu_custom_call" | custom-call | tf_op jit(solution)/shard_map/woven/pallas_call | solution.py:1015
  135.6 66.4 %write.1 = (bf16[1024,512]{1,0:T(8,128)(2,1)}, bf16[1024,512]{1,0:T(8,128)(2,1)}, f32[1,512]{1,0:T(1,128)}, f32[32,256]{1,0:T(8,128)}, f32[32,256]{1,0:T(8,128)}...) custom-call(bf16[1024,512]{1,0:T(8,128)(2,1)} %get-tuple-element.31., ...), custom_call_target="tpu_custom_call" | custom-call | tf_op jit(solution)/shard_map/write/pallas_call | solution.py:984

commit v4 on v3

--- a/solution.py
+++ b/solution.py
@@ -11,8 +11,10 @@
 HEAD_DIM = 64
 SLOTS = 64
 CHUNK = 128
+UNROLL = 4
 GROUP = 256
-TILE = 256
+TILE = 512
+WIDE = 512
 
 F32 = jnp.float32
 BF16 = jnp.bfloat16
@@ -33,10 +35,6 @@
 
 def twice(block):
     return jnp.concatenate([block, block], axis=1)
-
-
-def four(block):
-    return jnp.concatenate([block, block, block, block], axis=1)
 
 
 def standardise(rows):
@@ -51,27 +49,50 @@
     return jnp.concatenate([jnp.where(lane == h, block, zero) for h in range(4)], axis=0)
 
 
-def head_blocks():
-    row = lax.broadcasted_iota(jnp.int32, (GROUP, GROUP), 0) // HEAD_DIM
-    column = lax.broadcasted_iota(jnp.int32, (GROUP, GROUP), 1) // HEAD_DIM
-    return row == column
-
-
-def head_sum(block, ones):
-    high = block.astype(BF16)
-    low = (block - high.astype(F32)).astype(BF16)
-    return dot(high, ones) + dot(low, ones)
-
-
-def head_max(block):
+def diagonal(product):
+    parts = [product[h * HEAD_DIM : (h + 1) * HEAD_DIM, :] for h in range(4)]
+    lane = lax.broadcasted_iota(jnp.int32, parts[0].shape, 1) // HEAD_DIM
+    kept = parts[3]
+    for h in range(3):
+        kept = jnp.where(lane == h, parts[h], kept)
+    return kept
+
+
+def over_heads(block, reduce, rest):
     halves = []
     lane = lax.broadcasted_iota(jnp.int32, (block.shape[0], 128), 1) < HEAD_DIM
     for j in range(block.shape[1] // 128):
         part = block[:, j * 128 : (j + 1) * 128]
-        first = jnp.max(jnp.where(lane, part, -jnp.inf), axis=1, keepdims=True)
-        second = jnp.max(jnp.where(lane, -jnp.inf, part), axis=1, keepdims=True)
+        first = reduce(jnp.where(lane, part, rest), axis=1, keepdims=True)
+        second = reduce(jnp.where(lane, rest, part), axis=1, keepdims=True)
         halves.append(jnp.where(lane, first, second))
     return jnp.concatenate(halves, axis=1)
+
+
+def head_max(block):
+    return over_heads(block, jnp.max, -jnp.inf)
+
+
+def head_sum(block):
+    return over_heads(block, jnp.sum, 0.0)
+
+
+def head_pairs(product, allowed):
+    parts = [product[h * CHUNK : (h + 1) * CHUNK, :] * allowed for h in range(4)]
+    return jnp.concatenate(parts, axis=1).astype(BF16)
+
+
+def flip_pairs(pairs):
+    parts = [pairs[:, h * CHUNK : (h + 1) * CHUNK].T for h in range(4)]
+    return jnp.concatenate(parts, axis=1)
+
+
+def beside(*blocks):
+    return jnp.concatenate(blocks, axis=1)
+
+
+def above(*blocks):
+    return jnp.concatenate(blocks, axis=0)
 
 
 def flat(block):
@@ -96,7 +117,7 @@
 
 
 def project(g, r, wa, keepc, n1, q, k, v, w):
-    rows = pl.ds(pl.multiple_of(r * TILE, TILE), TILE)
+    rows = pl.ds(pl.multiple_of(r * WIDE, WIDE), WIDE)
     out = dot(n1[rows, :], flat(wa[g]))
     q[g, rows, :] = out[:, 0:256].astype(BF16)
     k[g, rows, :] = out[:, 256:512].astype(BF16)
@@ -112,13 +133,12 @@
     column = lax.broadcasted_iota(jnp.int32, (CHUNK, CHUNK), 1)
     same = seg == across
     causal = jnp.where(same & (column <= row), 1.0, 0.0)
-    anti = jnp.where(same & (row <= column), 1.0, 0.0)
     before = segc[pl.ds(base + 7, 1), :]
     first = segc[pl.ds(base + 8, 1), :]
     last = segc[pl.ds(base + 7 + CHUNK, 1), :]
     after = segc[pl.ds(base + 8 + CHUNK, 1), :]
     one = lambda test: jnp.where(test, 1.0, 0.0)
-    return causal, anti, dict(
+    return causal, dict(
         from_before=one(seg == before),
         to_after=one(seg == last),
         from_after=one(seg == after),
@@ -129,151 +149,205 @@
 
 
 def mix_forward(
-    g, i, segc, keepc, q, k, v, w, probs, inv, score, mixed, kw, wv, zsum, kw_all, wv_all
+    g, i, segc, keepc, q, k, v, w, probs, inv, score, mixed, kw, wv, zsum, kw_all, wv_all, pt_all,
+    mt_all,
 ):
-    blocks = head_blocks()
-    ones = jnp.where(blocks, 1.0, 0.0).astype(BF16)
-    state_k, state_v, state_z = kw[...], wv[...], zsum[0:1, :]
-    for n in range(2):
-        c = 2 * i + n
-        rows = pl.ds(pl.multiple_of(c * CHUNK, CHUNK), CHUNK)
-        causal, _, edge = chunk_masks(c, segc)
-        causal4 = four(causal)
-        keep = twice(keepc[rows, :])
-        come = twice(edge["from_before"])
-        come_low = come.astype(BF16)
-        carry = twice(edge["carry_on"])
-        qc, kc, vc, wc = q[g, rows, :], k[g, rows, :], v[g, rows, :], w[g, rows, :]
-        kw_low, wv_low = state_k.astype(BF16), state_v.astype(BF16)
-        kw_all[g, c] = kw_low
-        wv_all[g, c] = wv_low
-        ws = head_stack(wc)
-        pairs = (dot_rt(qc, head_stack(kc)) * causal4).astype(BF16)
-        total = dot(causal.astype(BF16), wc) + come * state_z + (1.0 - keep)
-        inverse = 1.0 / total
-        scores = (dot(pairs, ws) + dot(qc * come_low, kw_low)) * (inverse * (HEAD_DIM**-0.5))
-        powers = jnp.exp(scores - head_max(scores))
-        chances = powers / head_sum(powers, ones)
-        ratio = (chances * inverse).astype(BF16)
-        probs[g, rows, :] = chances
-        inv[g, rows, :] = inverse
-        score[g, rows, :] = scores
-        mixing = (dot_rt(ratio, ws) * causal4).astype(BF16)
-        out = dot(mixing, head_stack(vc)) + dot(ratio * come_low, wv_low)
-        mixed[g, rows, :] = (out * keep).astype(BF16)
-        wg = wc * twice(edge["to_after"]).astype(BF16)
-        state_k = state_k * carry + jnp.where(blocks, dot_lt(kc, wg), 0.0)
-        state_v = state_v * carry + jnp.where(blocks, dot_lt(wg, vc), 0.0)
-        state_z = state_z * carry + jnp.sum(wg.astype(F32), axis=0, keepdims=True)
-    kw[...] = state_k
-    wv[...] = state_v
-    zsum[...] = jnp.broadcast_to(state_z, zsum.shape)
+    run = range(UNROLL)
+    chunks = [UNROLL * i + n for n in run]
+    rows = [pl.ds(pl.multiple_of(c * CHUNK, CHUNK), CHUNK) for c in chunks]
+    masks = [chunk_masks(c, segc) for c in chunks]
+    keep = [twice(keepc[r, :]) for r in rows]
+    qc, kc, vc, wc = ([ref[g, r, :] for r in rows] for ref in (q, k, v, w))
+    state_k, state_v, state_z = [kw[...]], [wv[...]], [zsum[0:1, :]]
+    causal = [mask for mask, _ in masks]
+    edge = [edges for _, edges in masks]
+    come = [twice(edge[n]["from_before"]) for n in run]
+    come_low = [come[n].astype(BF16) for n in run]
+    pairs = [head_pairs(dot_rt(head_stack(qc[n]), kc[n]), causal[n]) for n in run]
+    for n in run:
+        carry = twice(edge[n]["carry_on"])
+        wg = wc[n] * twice(edge[n]["to_after"]).astype(BF16)
+        state_k.append(state_k[n] * carry + diagonal(dot_lt(kc[n], wg)))
+        state_v.append(state_v[n] * carry + diagonal(dot_lt(wg, vc[n])))
+        state_z.append(state_z[n] * carry + jnp.sum(wg.astype(F32), axis=0, keepdims=True))
+    kw_low = [head_stack(state_k[n].astype(BF16)) for n in run]
+    wv_low = [head_stack(state_v[n].astype(BF16)) for n in run]
+    inverse = [
+        1.0 / (dot(causal[n].astype(BF16), wc[n]) + come[n] * state_z[n] + (1.0 - keep[n]))
+        for n in run
+    ]
+    scores = [
+        dot(beside(pairs[n], qc[n] * come_low[n]), above(head_stack(wc[n]), kw_low[n]))
+        * (inverse[n] * (HEAD_DIM**-0.5))
+        for n in run
+    ]
+    powers = [jnp.exp(scores[n] - head_max(scores[n])) for n in run]
+    chances = [powers[n] / head_sum(powers[n]) for n in run]
+    ratio = [(chances[n] * inverse[n]).astype(BF16) for n in run]
+    mixing = [head_pairs(dot_rt(head_stack(ratio[n]), wc[n]), causal[n]) for n in run]
+    out = [
+        dot(beside(mixing[n], ratio[n] * come_low[n]), above(head_stack(vc[n]), wv_low[n]))
+        for n in run
+    ]
+    for n in run:
+        r = rows[n]
+        kw_all[g, chunks[n]] = diagonal(kw_low[n].T)
+        wv_all[g, chunks[n]] = diagonal(wv_low[n].T)
+        pt_all[g, r, :] = flip_pairs(pairs[n])
+        mt_all[g, r, :] = flip_pairs(mixing[n])
+        inv[g, r, :] = inverse[n]
+        score[g, r, :] = scores[n]
+        probs[g, r, :] = chances[n]
+        mixed[g, r, :] = (out[n] * keep[n]).astype(BF16)
+    kw[...] = state_k[-1]
+    wv[...] = state_v[-1]
+    zsum[...] = jnp.broadcast_to(state_z[-1], zsum.shape)
 
 
 def mix_backward(
-    g, i, segc, keepc, q, k, v, w, probs, inv, score, gm, rg, uq, zgrad, kw_all, wv_all, gy
+    g, i, segc, keepc, q, k, v, w, probs, inv, score, gm, rg, uq, zgrad, kw_all, wv_all, pt_all,
+    mt_all, gy,
 ):
-    blocks = head_blocks()
-    ones = jnp.where(blocks, 1.0, 0.0).astype(BF16)
-    state_v, state_k, state_z = rg[...], uq[...], zgrad[0:1, :]
-    for n in range(2):
-        c = 2 * i + 1 - n
-        rows = pl.ds(pl.multiple_of(c * CHUNK, CHUNK), CHUNK)
-        causal, anti, edge = chunk_masks(c, segc)
-        causal4, anti4 = four(causal), four(anti)
-        anti_low = anti.astype(BF16)
-        come_low = twice(edge["from_before"]).astype(BF16)
-        late = twice(edge["from_after"])
-        late_low = late.astype(BF16)
-        back = twice(edge["to_before"])
-        back_low = back.astype(BF16)
-        carry = twice(edge["carry_back"])
-        qc, kc, vc, wc = q[g, rows, :], k[g, rows, :], v[g, rows, :], w[g, rows, :]
-        grad = gm[g, rows, :]
-        chances, inverse, scores = probs[g, rows, :], inv[g, rows, :], score[g, rows, :]
-        ratio = (chances * inverse).astype(BF16)
-        ws, grads, ratios = head_stack(wc), head_stack(grad), head_stack(ratio)
-        d_mixing = (dot_rt(grad, head_stack(vc)) * causal4).astype(BF16)
-        d_ratio = dot(d_mixing, ws) + dot_rt(grad * come_low, wv_all[g, c])
-        d_chance = d_ratio * inverse
-        weighted = d_chance * chances
-        d_score = weighted - chances * head_sum(weighted, ones)
-        d_pw = (d_score * inverse * (HEAD_DIM**-0.5)).astype(BF16)
-        d_total = (weighted + d_score * scores) * inverse
-        d_pairs = (dot_rt(d_pw, ws) * causal4).astype(BF16)
-        gq = dot(d_pairs, head_stack(kc)) + dot_rt(d_pw * come_low, kw_all[g, c])
-        rg_low, uq_low = state_v.astype(BF16), state_k.astype(BF16)
-        d_pws, queries = head_stack(d_pw), head_stack(qc)
-        mixing_t = (dot_rt(wc, ratios) * anti4).astype(BF16)
-        w_late = wc * late_low
-        gv = dot(mixing_t, grads) + dot(w_late, rg_low)
-        d_pairs_t = (dot_rt(wc, d_pws) * anti4).astype(BF16)
-        gk = dot(d_pairs_t, queries) + dot(w_late, uq_low)
-        d_mixing_t = (dot_rt(vc, grads) * anti4).astype(BF16)
-        pairs_t = (dot_rt(kc, queries) * anti4).astype(BF16)
-        z_high = d_total.astype(BF16)
-        z_low = (d_total - z_high.astype(F32)).astype(BF16)
-        dw = dot(d_mixing_t, ratios) + dot(pairs_t, d_pws)
-        dw += dot_rt(vc * late_low, rg_low) + dot_rt(kc * late_low, uq_low)
-        dw -= dot(anti_low, z_high) + dot(anti_low, z_low) + late * state_z
-        gy[g, rows, 0:256] = gq.astype(BF16)
-        gy[g, rows, 256:512] = gk.astype(BF16)
-        gy[g, rows, 512:768] = gv.astype(BF16)
-        gy[g, rows, 768:1024] = (dw * wc.astype(F32)).astype(BF16)
-        state_v = state_v * carry + jnp.where(blocks, dot_lt(ratio * back_low, grad), 0.0)
-        state_k = state_k * carry + jnp.where(blocks, dot_lt(d_pw * back_low, qc), 0.0)
-        state_z = state_z * carry + jnp.sum(d_total * back, axis=0, keepdims=True)
-    rg[...] = state_v
-    uq[...] = state_k
-    zgrad[...] = jnp.broadcast_to(state_z, zgrad.shape)
-
-
-def feed_up(r, tok, gain, up_bias, wb, mixed, n2, act, lin, gh):
+    run = range(UNROLL)
+    chunks = [UNROLL * i + UNROLL - 1 - n for n in run]
+    rows = [pl.ds(pl.multiple_of(c * CHUNK, CHUNK), CHUNK) for c in chunks]
+    masks = [chunk_masks(c, segc) for c in chunks]
+    qc, kc, vc, wc, grad, chances, inverse, scores, pairs_t, mixing_t = (
+        [ref[g, r, :] for r in rows]
+        for ref in (q, k, v, w, gm, probs, inv, score, pt_all, mt_all)
+    )
+    kw_t, wv_t = ([head_stack(ref[g, c]) for c in chunks] for ref in (kw_all, wv_all))
+    state_v, state_k, state_z = [rg[...]], [uq[...]], [zgrad[0:1, :]]
+    causal = [mask for mask, _ in masks]
+    edge = [edges for _, edges in masks]
+    come_low = [twice(edge[n]["from_before"]).astype(BF16) for n in run]
+    late = [twice(edge[n]["from_after"]) for n in run]
+    late_low = [late[n].astype(BF16) for n in run]
+    back = [twice(edge[n]["to_before"]) for n in run]
+    back_low = [back[n].astype(BF16) for n in run]
+    carry = [twice(edge[n]["carry_back"]) for n in run]
+    grads = [head_stack(grad[n]) for n in run]
+    d_mixing = [head_pairs(dot_rt(grads[n], vc[n]), causal[n]) for n in run]
+    d_chance = [
+        dot(beside(d_mixing[n], grad[n] * come_low[n]), above(head_stack(wc[n]), wv_t[n]))
+        * inverse[n]
+        for n in run
+    ]
+    ratio = [(chances[n] * inverse[n]).astype(BF16) for n in run]
+    ratios = [head_stack(ratio[n]) for n in run]
+    for n in run:
+        added = diagonal(dot_lt(ratio[n] * back_low[n], grad[n]))
+        state_v.append(state_v[n] * carry[n] + added)
+    rg_low = [head_stack(state_v[n].astype(BF16)) for n in run]
+    w_late = [wc[n] * late_low[n] for n in run]
+    gv = [dot(beside(mixing_t[n], w_late[n]), above(grads[n], rg_low[n])) for n in run]
+    weighted = [d_chance[n] * chances[n] for n in run]
+    d_score = [weighted[n] - chances[n] * head_sum(weighted[n]) for n in run]
+    d_pw = [(d_score[n] * inverse[n] * (HEAD_DIM**-0.5)).astype(BF16) for n in run]
+    d_total = [(weighted[n] + d_score[n] * scores[n]) * inverse[n] for n in run]
+    d_pws = [head_stack(d_pw[n]) for n in run]
+    d_pairs = [head_pairs(dot_rt(d_pws[n], wc[n]), causal[n]) for n in run]
+    for n in run:
+        added = diagonal(dot_lt(d_pw[n] * back_low[n], qc[n]))
+        state_k.append(state_k[n] * carry[n] + added)
+        added = jnp.sum(d_total[n] * back[n], axis=0, keepdims=True)
+        state_z.append(state_z[n] * carry[n] + added)
+    uq_low = [head_stack(state_k[n].astype(BF16)) for n in run]
+    dw = []
+    for n in run:
+        z_high = d_total[n].astype(BF16)
+        z_low = (d_total[n] - z_high.astype(F32)).astype(BF16)
+        anti = -causal[n].T.astype(BF16)
+        left = beside(
+            flip_pairs(d_mixing[n]), pairs_t[n], vc[n] * late_low[n], kc[n] * late_low[n], anti, anti
+        )
+        right = above(ratios[n], d_pws[n], rg_low[n].T, uq_low[n].T, z_high, z_low)
+        dw.append(dot(left, right) - late[n] * state_z[n])
+    gq = [
+        dot(beside(d_pairs[n], d_pw[n] * come_low[n]), above(head_stack(kc[n]), kw_t[n]))
+        for n in run
+    ]
+    gk = [
+        dot(beside(flip_pairs(d_pairs[n]), w_late[n]), above(head_stack(qc[n]), uq_low[n]))
+        for n in run
+    ]
+    for n in run:
+        gy[g, rows[n], 512:768] = gv[n].astype(BF16)
+        gy[g, rows[n], 768:1024] = (dw[n] * wc[n].astype(F32)).astype(BF16)
+        gy[g, rows[n], 0:256] = gq[n].astype(BF16)
+        gy[g, rows[n], 256:512] = gk[n].astype(BF16)
+    rg[...] = state_v[-1]
+    uq[...] = state_k[-1]
+    zgrad[...] = jnp.broadcast_to(state_z[-1], zgrad.shape)
+
+
+def units(j):
+    return j // 2 % 2, (j // 4 * 2 + j % 2) * 256
+
+
+def feed_in(r, tok, gain, wb, mixed, n2, gh):
     rows = pl.ds(pl.multiple_of(r * TILE, TILE), TILE)
     hidden = tok[rows, :].astype(F32)
     for g in range(2):
         hidden += dot_rt(mixed[g, rows, :], flat(wb[g, ..., 0:256]))
     gh[rows, :] = hidden
     hat, _ = standardise(hidden)
-    normed = (hat * gain[...]).astype(BF16)
-    n2[rows, :] = normed
+    n2[rows, :] = (hat * gain[...]).astype(BF16)
+
+
+def feed_up(part, r, up_bias, wb, n2, act, lin):
+    rows = pl.ds(pl.multiple_of(r * TILE, TILE), TILE)
+    normed = n2[rows, :]
     k0 = 0.7978845608
     k1 = k0 * 0.044715
-    for g in range(2):
-        for j in range(4):
-            here = slice(j * 256, (j + 1) * 256)
-            unit = g * 1024 + j * 256
-            up = flat(wb[g, ..., 256 + j * 256 : 512 + j * 256])
-            linear = dot(normed, up) + up_bias[:, unit : unit + 256]
-            square = linear * linear
-            gate = 0.5 * jnp.tanh(linear * (square * k1 + k0)) + 0.5
-            active = linear * gate
-            slope = gate + active * (1.0 - gate) * (square * (6.0 * k1) + 2.0 * k0)
-            act[g, rows, here] = active.astype(BF16)
-            lin[g, rows, here] = slope.astype(BF16)
-
-
-def feed_down(r, cot, gain, down_bias, wb, keepc, act, lin, gh, gb, gm, small, out):
+
+    def linear_of(j):
+        g, column = units(j)
+        up = flat(wb[g, ..., 256 + column : 512 + column])
+        bias = up_bias[:, g * 1024 + column : g * 1024 + column + 256]
+        return dot(normed, up) + bias
+
+    after = linear_of(4 * part)
+    for j in range(4 * part, 4 * part + 4):
+        linear = after
+        if j < 4 * part + 3:
+            after = linear_of(j + 1)
+        square = linear * linear
+        gate = 0.5 * jnp.tanh(linear * (square * k1 + k0)) + 0.5
+        active = linear * gate
+        slope = gate + active * (1.0 - gate) * (square * (6.0 * k1) + 2.0 * k0)
+        g, column = units(j)
+        act[g, rows, column : column + 256] = active.astype(BF16)
+        lin[g, rows, column : column + 256] = slope.astype(BF16)
+
+
+def feed_down(r, cot, gain, down_bias, wb, keepc, act, lin, gh, gm, small):
     rows = pl.ds(pl.multiple_of(r * TILE, TILE), TILE)
     grad = cot[rows, :]
     hidden = gh[rows, :]
     total = hidden + down_bias[...]
     back = jnp.zeros((TILE, 512), F32)
-    for g in range(2):
-        for j in range(4):
-            here = slice(j * 256, (j + 1) * 256)
-            unit = g * 1024 + j * 256
-            down = flat(wb[g, ..., 1280 + j * 256 : 1536 + j * 256])
-            grad_low = (dot(grad, down) * lin[g, rows, here].astype(F32)).astype(BF16)
-            lin[g, rows, here] = grad_low
-            row, column = 4 + unit // 512, unit % 512
-            small[row : row + 1, column : column + 256] += jnp.sum(
-                grad_low.astype(F32), axis=0, keepdims=True
-            )
+
+    def grad_of(j):
+        g, column = divmod(j * 256, 1024)
+        down = flat(wb[g, ..., 1280 + column : 1536 + column])
+        return dot(grad, down) * lin[g, rows, column : column + 256].astype(F32)
+
+    after = grad_of(0)
+    for j in range(8):
+        grad_low = after.astype(BF16)
+        if j < 7:
+            after = grad_of(j + 1)
+        g, column = divmod(j * 256, 1024)
+        lin[g, rows, column : column + 256] = grad_low
+        row, column = 4 + j // 2, j % 2 * 256
+        small[row : row + 1, column : column + 256] += jnp.sum(
+            grad_low.astype(F32), axis=0, keepdims=True
+        )
     for g in range(2):
         total += dot_rt(act[g, rows, :], flat(wb[g, ..., 1280:2304]))
         back += dot_rt(lin[g, rows, :], flat(wb[g, ..., 256:1280]))
-    out[rows, :] = total.astype(BF16)
+    cot[rows, :] = total.astype(BF16)
     hat, scale = standardise(hidden)
     scaled = back * gain[...]
     inner = scaled - jnp.mean(scaled, axis=-1, keepdims=True)
@@ -282,7 +356,6 @@
     grad_hidden = grad_f32 + scale * inner
     gh[rows, :] = grad_hidden
     low = grad_hidden.astype(BF16)
-    gb[rows, :] = low
     small[0:1, :] += jnp.sum(back * hat, axis=0, keepdims=True)
     small[2:3, :] += jnp.sum(grad_f32, axis=0, keepdims=True)
     keep = twice(keepc[rows, :])
@@ -291,30 +364,35 @@
 
 
 def transpose_into(source, target, length):
-    for r in range(length // TILE):
-        target[:, r * TILE : (r + 1) * TILE] = source[r * TILE : (r + 1) * TILE, :].T
+    for r in range(length // 256):
+        here = slice(r * 256, (r + 1) * 256)
+        target[:, here] = source[here, :].astype(BF16).T
 
 
 def weight_grad(left_t, right, target, g, target_column, columns):
-    shape = target.shape[1:-1] + (256,)
-
-    def step(j, carry):
-        here = pl.ds(pl.multiple_of(j * 256, 256), 256)
-        there = pl.ds(pl.multiple_of(target_column + j * 256, 256), 256)
-        target[g, ..., there] = dot(left_t[...], right[:, here]).astype(BF16).reshape(shape)
-        return carry
-
-    lax.fori_loop(0, columns // 256, step, 0)
-
-
-def finish(r, tok, gain, wa, gy, gh, small, grad_out):
-    rows = pl.ds(pl.multiple_of(r * TILE, TILE), TILE)
+    shape = target.shape[1:-1]
+    block = min(columns, 512)
+
+    def product(j):
+        return dot(left_t[...], right[:, j * block : (j + 1) * block]).astype(BF16)
+
+    after = product(0)
+    for j in range(columns // block):
+        here = after
+        if (j + 1) * block < columns:
+            after = product(j + 1)
+        there = slice(target_column + j * block, target_column + (j + 1) * block)
+        target[g, ..., there] = here.reshape(shape + (block,))
+
+
+def finish(r, tok, gain, wa, gy, gh, small):
+    rows = pl.ds(pl.multiple_of(r * WIDE, WIDE), WIDE)
     hat, scale = standardise(tok[rows, :].astype(F32))
     back = dot_rt(gy[0, rows, :], flat(wa[0])) + dot_rt(gy[1, rows, :], flat(wa[1]))
     scaled = back * gain[...]
     inner = scaled - jnp.mean(scaled, axis=-1, keepdims=True)
     inner -= hat * jnp.mean(scaled * hat, axis=-1, keepdims=True)
-    grad_out[rows, :] = (gh[rows, :] + scale * inner).astype(BF16)
+    tok[rows, :] = (gh[rows, :] + scale * inner).astype(BF16)
     small[1:2, :] += jnp.sum(back * hat, axis=0, keepdims=True)
 
 
@@ -322,18 +400,17 @@
     def nothing(self, *at):
         pass
 
-    before = weights_a = mixing = weights_up = feeding = weights_down = nothing
-    grads_down = grads_up = mixing_back = grads_a = finishing = after = nothing
-
-
-LAYER_INPUTS = 8
+    before = enter = weights_a = projected = mixing = weights_up = feeding = weights_down = nothing
+    grads_down = feeding_down = layer_out = grads_mid = grads_up = nothing
+    mixing_back = mixed_back = grads_a = finishing = finished = after = nothing
+
+
+LAYER_INPUTS = 6
 
 
 def layer_body(
     length,
     comm,
-    tok,
-    cot,
     seg_row,
     pad_row,
     gain_one,
@@ -342,11 +419,11 @@
     down_bias,
     wa,
     wb,
-    out,
-    grad_out,
     ga,
     gw,
     small,
+    tok,
+    cot,
     segc,
     keepc,
     n1,
@@ -363,15 +440,16 @@
     state_z,
     kw_all,
     wv_all,
+    pt_all,
+    mt_all,
     n2,
     act,
     lin,
     gh,
-    gb,
     gm,
     flip,
 ):
-    pairs, tiles = length // (2 * CHUNK), length // TILE
+    runs, tiles = length // (UNROLL * CHUNK), length // TILE
 
     def clear():
         state_k[...] = jnp.zeros_like(state_k)
@@ -381,49 +459,63 @@
     comm.before()
     small[...] = jnp.zeros_like(small)
     rows_to_columns(seg_row, pad_row, segc, keepc, length)
+    comm.enter()
 
     @pl.loop(0, tiles)
     def _(r):
         normalise(r, tok, gain_one, n1)
+
+    transpose_into(cot, flip, length)
 
     @pl.loop(0, 2)
     def _(g):
         comm.weights_a(g)
         clear()
 
-        @pl.loop(0, tiles)
+        @pl.loop(0, length // WIDE)
         def _(r):
             project(g, r, wa, keepc, n1, q, k, v, w)
 
-        @pl.loop(0, pairs)
+        comm.projected(g)
+
+        @pl.loop(0, runs)
         def _(i):
             comm.mixing(g, i)
             mix_forward(
                 g, i, segc, keepc, q, k, v, w, probs, inv, score, mixed, state_k, state_v, state_z,
-                kw_all, wv_all,
+                kw_all, wv_all, pt_all, mt_all,
             )
 
-    comm.weights_up()
+    comm.weights_up(0)
+
+    @pl.loop(0, tiles)
+    def _(r):
+        feed_in(r, tok, gain_two, wb, mixed, n2, gh)
+        feed_up(0, r, up_bias, wb, n2, act, lin)
+
+    comm.weights_up(1)
 
     @pl.loop(0, tiles)
     def _(r):
         comm.feeding(r)
-        feed_up(r, tok, gain_two, up_bias, wb, mixed, n2, act, lin, gh)
-
-    comm.weights_down()
-
-    @pl.loop(0, tiles)
-    def _(r):
-        feed_down(r, cot, gain_two, down_bias, wb, keepc, act, lin, gh, gb, gm, small, out)
-
-    transpose_into(cot, flip, length)
+        feed_up(1, r, up_bias, wb, n2, act, lin)
+
     for g in range(2):
         weight_grad(flip, act.at[g], gw, g, 1280, 1024)
     comm.grads_down()
+    comm.weights_down()
+
+    @pl.loop(0, tiles)
+    def _(r):
+        comm.feeding_down(r)
+        feed_down(r, cot, gain_two, down_bias, wb, keepc, act, lin, gh, gm, small)
+
+    comm.layer_out()
     transpose_into(n2, flip, length)
-    for g in range(2):
-        weight_grad(flip, lin.at[g], gw, g, 256, 1024)
-    transpose_into(gb, flip, length)
+    weight_grad(flip, lin.at[0], gw, 0, 256, 1024)
+    comm.grads_mid()
+    weight_grad(flip, lin.at[1], gw, 1, 256, 1024)
+    transpose_into(gh, flip, length)
     for g in range(2):
         weight_grad(flip, mixed.at[g], gw, g, 0, GROUP)
     comm.grads_up()
@@ -433,21 +525,23 @@
     def _(g):
         clear()
 
-        @pl.loop(0, pairs)
+        @pl.loop(0, runs)
         def _(i):
             comm.mixing_back(g, i)
             mix_backward(
-                g, pairs - 1 - i, segc, keepc, q, k, v, w, probs, inv, score, gm, state_v, state_k,
-                state_z, kw_all, wv_all, act,
+                g, runs - 1 - i, segc, keepc, q, k, v, w, probs, inv, score, gm, state_v, state_k,
+                state_z, kw_all, wv_all, pt_all, mt_all, act,
             )
 
+        comm.mixed_back(g)
         weight_grad(flip, act.at[g], ga, g, 0, 1024)
         comm.grads_a(g)
 
-    @pl.loop(0, tiles)
+    @pl.loop(0, length // WIDE)
     def _(r):
         comm.finishing(r)
-        finish(r, tok, gain_one, wa, act, gh, small, grad_out)
+        finish(r, tok, gain_one, wa, act, gh, small)
+        comm.finished(r)
 
     comm.after()
 
@@ -467,23 +561,28 @@
         vmem((2, length, GROUP), F32),
         vmem((2, length, GROUP), F32),
         vmem((2, length, GROUP), BF16),
-        vmem((GROUP, GROUP), F32),
-        vmem((GROUP, GROUP), F32),
+        vmem((HEAD_DIM, GROUP), F32),
+        vmem((HEAD_DIM, GROUP), F32),
         vmem((8, GROUP), F32),
-        vmem((2, chunks, GROUP, GROUP), BF16),
-        vmem((2, chunks, GROUP, GROUP), BF16),
+        vmem((2, chunks, HEAD_DIM, GROUP), BF16),
+        vmem((2, chunks, HEAD_DIM, GROUP), BF16),
+        vmem((2, length, 4 * CHUNK), BF16),
+        vmem((2, length, 4 * CHUNK), BF16),
         vmem((length, width), BF16),
         vmem((2, length, 1024), BF16),
         vmem((2, length, 1024), BF16),
         vmem((length, width), F32),
-        vmem((length, width), BF16),
         vmem((2, length, GROUP), BF16),
         vmem((width, length), BF16),
     ]
 
 
-def layer_kernel(length, *refs):
-    layer_body(length, Quiet(), *refs)
+def layer_kernel(length, tokens, cotangent, *refs):
+    inputs, (out, grad_out), rest = refs[: LAYER_INPUTS + 2], refs[8:10], refs[10:]
+    grad_out[...] = tokens[...]
+    out[...] = cotangent[...]
+    ga, gw, small = rest[:3]
+    layer_body(length, Quiet(), *inputs, ga, gw, small, grad_out, out, *rest[3:])
 
 
 def layer(tokens, cotangent, seg_row, pad_row, gain_one, gain_two, up_bias, down_bias, wa, wb):
@@ -504,7 +603,7 @@
         in_specs=[space] * 10,
         out_specs=tuple([space] * 5),
         scratch_shapes=layer_scratch(length, width),
-        compiler_params=pltpu.CompilerParams(vmem_limit_bytes=60 * 1024 * 1024),
+        compiler_params=pltpu.CompilerParams(vmem_limit_bytes=62 * 1024 * 1024),
         name="layer",
     )(tokens, cotangent, seg_row, pad_row, gain_one, gain_two, up_bias, down_bias, wa, wb)
     whole = lambda full: full.reshape(2, width, full.shape[-1])
@@ -540,13 +639,17 @@
     def along_z(self, step, core):
         return {"dp": self.chips_z[step], "tensor": core}
 
-    def greet(self):
+    def friends(self):
+        along = [self.along_z(s, core) for s in range(1, self.depth) for core in range(2)]
+        return self.level[1:] + along
+
+    def knock(self):
         barrier = pltpu.get_barrier_semaphore()
-        friends = self.level[1:]
-        friends += [self.along_z(s, core) for s in range(1, self.depth) for core in range(2)]
-        for friend in friends:
+        for friend in self.friends():
             pl.semaphore_signal(barrier, inc=1, device_id=friend, device_id_type=MESH)
-        pl.semaphore_wait(barrier, len(friends))
+
+    def enter(self):
+        pl.semaphore_wait(pltpu.get_barrier_semaphore(), len(self.friends()))
 
 
 class Copies:
@@ -808,142 +911,191 @@
 
 
 class Woven:
-    def __init__(self, place, owns, own_a, own_b, wa, wb, ga, gw, gains, gathers, scatters, targets):
+    def __init__(
+        self, place, owns, ends, own_a, own_b, wa, wb, ga, gw, gains, gathers, scatters, targets
+    ):
         self.p = place
         self.owns, self.own_a, self.own_b = owns, own_a, own_b
-        every, up, down = slice(0, 1024), slice(0, 1280), slice(1280, 2304)
+        self.tokens, self.cotangent, self.out, self.grad_out, self.tok, self.cot, self.io = ends
+        every = slice(0, 1024)
         self.a = [Gather(place, own_a, wa, g, every, gathers[g]) for g in range(2)]
-        self.up = Gather(place, own_b, wb, None, up, gathers[2])
-        self.down = Gather(place, own_b, wb, None, down, gathers[3])
-        self.down_grad = Scatter(place, gw, None, down, *scatters[0])
-        self.up_grad = Scatter(place, gw, None, up, *scatters[1])
-        self.a_grad = [Scatter(place, ga, g, every, *scatters[2 + g]) for g in range(2)]
+        self.b = [
+            Gather(place, own_b, wb, None, slice(768 * n, 768 * n + 768), gathers[2 + n])
+            for n in range(3)
+        ]
+        self.down_grad = Scatter(place, gw, None, slice(1280, 2304), *scatters[0])
+        self.up_grad = Scatter(place, gw, None, slice(0, 1280), *scatters[1])
+        self.a_grad = [Scatter(place, ga, 0, every, *scatters[2])]
+        self.a_grad += [
+            Scatter(place, ga, 1, slice(512 * n, 512 * n + 512), *scatters[3 + n])
+            for n in range(2)
+        ]
         self.gains = gains
         self.da, self.dw = targets
 
+    def table(self, at, steps):
+        for place, calls in steps.items():
+            here = None
+            for value, wanted in zip(at, place):
+                here = (value == wanted) if here is None else here & (value == wanted)
+
+            @pl.when(here)
+            def _(calls=calls):
+                for call in calls:
+                    call()
+
+    def copy(self, n):
+        here, there = (
+            (self.tokens, self.tok),
+            (self.cotangent, self.cot),
+            (self.cot, self.out),
+        )[n]
+        return pltpu.make_async_copy(here, there, self.io.at[n])
+
+    def copy_grad(self, r):
+        rows = pl.ds(pl.multiple_of(r * WIDE, WIDE), WIDE)
+        return pltpu.make_async_copy(self.tok.at[rows], self.grad_out.at[rows], self.io.at[3 + r])
+
     def before(self):
+        self.p.knock()
+        self.copy(0).start()
+        self.copy(1).start()
         query, key, value, slot, out_t, up, down_t = self.owns
         halves = lambda ref: ref[...].astype(BF16).reshape(2, 16, ref.shape[1])
         self.own_a[:, :, 0:256] = halves(query)
         self.own_a[:, :, 256:512] = halves(key)
         self.own_a[:, :, 512:768] = halves(value)
         self.own_a[:, :, 768:1024] = halves(slot)
-        self.p.greet()
-        self.a[0].first()
-        self.a[1].first()
         self.own_b[:, :, 0:256] = halves(out_t)
         self.own_b[:, :, 256:1280] = halves(up)
         self.own_b[:, :, 1280:2304] = halves(down_t)
 
+    def enter(self):
+        self.p.enter()
+        self.a[0].first()
+        self.a[1].first()
+        self.copy(0).wait()
+        self.copy(1).wait()
+
     def weights_a(self, g):
         one, two = self.a
-
-        @pl.when(g == 0)
-        def _():
-            one.second()
-            two.second()
-            self.up.first()
-            one.third()
-            one.fourth()
-            one.last()
-            two.third()
-
-        @pl.when(g == 1)
-        def _():
-            two.last()
+        b = self.b
+        self.table(
+            (g,),
+            {
+                (0,): (
+                    one.second, b[0].first, two.second, one.third, b[1].first, two.third,
+                    one.fourth, b[0].second, one.last,
+                ),
+                (1,): (two.last, b[0].third),
+            },
+        )
+
+    def projected(self, g):
+        self.table((g,), {(0,): (self.a[1].fourth,)})
 
     def mixing(self, g, i):
-        steps = {
-            (0, 0): (self.a[1].fourth, self.up.second, self.down.first),
-            (1, 0): (self.up.third, self.down.second),
-            (1, 2): (self.up.fourth,),
-            (1, 3): (self.down.third,),
-        }
-        for (group, pair), calls in steps.items():
-
-            @pl.when((g == group) & (i == pair))
-            def _(calls=calls):
-                for call in calls:
-                    call()
-
-    def weights_up(self):
-        self.up.last()
+        b = self.b
+        self.table((g, i), {(0, 1): (b[1].second, b[2].first), (1, 1): (b[0].fourth, b[2].second)})
+
+    def weights_up(self, part):
+        b = self.b
+        if part == 0:
+            b[1].third()
+            b[0].last()
+        else:
+            b[1].fourth()
+            b[1].last()
 
     def feeding(self, r):
-        pl.when(r == 1)(self.down.fourth)
-
-    def weights_down(self):
-        self.down.last()
+        self.table((r,), {(0,): (self.b[2].third,)})
 
     def grads_down(self):
         self.down_grad.first()
+        self.b[2].fourth()
+
+    def weights_down(self):
+        self.b[2].last()
+
+    def feeding_down(self, r):
+        self.table((r,), {(1,): (self.down_grad.second,)})
+
+    def layer_out(self):
+        self.copy(2).start()
+
+    def grads_mid(self):
+        pass
 
     def grads_up(self):
         self.up_grad.first()
-        self.down_grad.second()
+        self.down_grad.third()
 
     def mixing_back(self, g, i):
-        steps = {
-            (0, 1): (self.up_grad.second,),
-            (0, 2): (self.down_grad.third,),
-            (0, 3): (self.up_grad.third,),
-            (1, 0): (self.down_grad.fourth,),
-            (1, 1): (self.up_grad.fourth, self.a_grad[0].second),
-            (1, 3): (self.a_grad[0].third,),
-        }
-        for (group, pair), calls in steps.items():
-
-            @pl.when((g == group) & (i == pair))
-            def _(calls=calls):
-                for call in calls:
-                    call()
+        self.table(
+            (g, i),
+            {(0, 1): (self.up_grad.second,), (1, 1): (self.a_grad[0].second,)},
+        )
+
+    def mixed_back(self, g):
+        self.table((g,), {(0,): (self.down_grad.fourth,), (1,): (self.up_grad.third,)})
 
     def grads_a(self, g):
-        for group in range(2):
-            pl.when(g == group)(self.a_grad[group].first)
-
-        @pl.when(g == 1)
-        def _():
-            self.a_grad[0].fourth()
-            self.down_grad.last(self.dw.at[:, :, 1280:2304])
-            self.up_grad.last(self.dw.at[:, :, 0:1280])
+        one, two, three = self.a_grad
+        self.table((g,), {(0,): (one.first,), (1,): (two.first, three.first)})
 
     def finishing(self, r):
-        pl.when(r == 1)(self.a_grad[1].second)
+        one, two, three = self.a_grad
+        self.table((r,), {(1,): (two.second, one.third)})
+
+    def finished(self, r):
+        self.copy_grad(r).start()
 
     def after(self):
+        one, two, three = self.a_grad
+        three.second()
         self.gains.first()
-        self.a_grad[1].third()
+        self.down_grad.last(self.dw.at[:, :, 1280:2304])
+        self.up_grad.fourth()
+        two.third()
+        one.fourth()
         self.gains.second()
-        self.a_grad[0].last(self.da)
-        self.a_grad[1].fourth()
+        three.third()
+        two.fourth()
+        three.fourth()
+        self.up_grad.last(self.dw.at[:, :, 0:1280])
+        one.last(self.da)
         self.total = self.gains.last()
-        self.a_grad[1].last(self.da)
-        for copies in (
-            *self.a, self.up, self.down, self.down_grad, self.up_grad, *self.a_grad, self.gains
-        ):
+        two.last(self.da.at[:, :, 0:512])
+        three.last(self.da.at[:, :, 512:1024])
+        for copies in (*self.a, *self.b, self.down_grad, self.up_grad, *self.a_grad, self.gains):
             copies.left()
+        self.copy(2).wait()
+        for r in range(2):
+            self.copy_grad(r).wait()
 
 
 def woven_kernel(length, depth, *refs):
     refs = list(refs)
     take = lambda n: [refs.pop(0) for _ in range(n)]
-    tok, cot, seg_rows, pad_rows, gain_one, gain_two, up_bias, down_bias = take(LAYER_INPUTS)
+    tokens, cotangent, seg_rows, pad_rows = take(4)
+    layer_inputs = take(4)
     owns = take(7)
     out, grad_out, da, dw, small_out = take(5)
-    own_a, own_b, wa, wb, ga, gw, seg_row, pad_row = take(8)
+    tok, cot, io, own_a, own_b, wa, wb, ga, gw, seg_row, pad_row = take(11)
     small, parts, sums, gain_sems = take(4)
-    gathers = take(4)
-    scatters = [take(5) for _ in range(4)]
+    gathers = take(5)
+    scatters = [take(5) for _ in range(5)]
     place = Place(depth)
     gains = Reduce(place, small, parts, sums, gain_sems)
-    comm = Woven(place, owns, own_a, own_b, wa, wb, ga, gw, gains, gathers, scatters, (da, dw))
+    ends = (tokens, cotangent, out, grad_out, tok, cot, io)
+    comm = Woven(
+        place, owns, ends, own_a, own_b, wa, wb, ga, gw, gains, gathers, scatters, (da, dw)
+    )
     first = lax.axis_index("tensor") == 0
     for rows, row in ((seg_rows, seg_row), (pad_rows, pad_row)):
         row[...] = jnp.where(first, rows[0:1, :], rows[1:2, :])
     layer_body(
-        length, comm, tok, cot, seg_row, pad_row, gain_one, gain_two, up_bias, down_bias, wa, wb,
-        out, grad_out, ga, gw, small, *refs,
+        length, comm, seg_row, pad_row, *layer_inputs, wa, wb, ga, gw, small, tok, cot, *refs
     )
     small_out[...] = comm.total
 
@@ -951,12 +1103,10 @@
 def write_kernel(out_in, grad_in, da, dw, small, *refs):
     (
         out, grad_out, mixer_gain, query, key, value, slot, out_t, feed_gain, up, up_bias, down_t,
-        down_bias, sems,
+        down_bias,
     ) = refs
-    one = pltpu.make_async_copy(out_in, out, sems.at[0])
-    two = pltpu.make_async_copy(grad_in, grad_out, sems.at[1])
-    one.start()
-    two.start()
+    out[...] = out_in[...]
+    grad_out[...] = grad_in[...]
     rows = lambda part: part.reshape(-1, part.shape[-1])
     query[...] = rows(da[:, :, 0:256])
     key[...] = rows(da[:, :, 256:512])
@@ -970,14 +1120,11 @@
     down_bias[...] = small[2:3, :]
     for row in range(4):
         up_bias[:, row * 512 : (row + 1) * 512] = small[4 + row : 5 + row, :]
-    one.wait()
-    two.wait()
 
 
 def write(out, grad_out, da, dw, small):
     shape = jax.ShapeDtypeStruct
     space = pl.BlockSpec(memory_space=pltpu.VMEM)
-    far = pl.BlockSpec(memory_space=pl.ANY)
     width = out.shape[1]
     square, wide = shape((32, 256), F32), shape((32, 1024), F32)
     row = shape((1, width), F32)
@@ -998,9 +1145,8 @@
             wide,
             row,
         ),
-        in_specs=[far, far, space, space, space],
-        out_specs=(far, far) + (space,) * 11,
-        scratch_shapes=[pltpu.SemaphoreType.DMA((2,))],
+        in_specs=[space] * 5,
+        out_specs=(space,) * 13,
         name="write",
     )(out, grad_out, da, dw, small)
 
@@ -1009,6 +1155,7 @@
     length, width = tokens.shape
     shape = jax.ShapeDtypeStruct
     space = pl.BlockSpec(memory_space=pltpu.VMEM)
+    far = pl.BlockSpec(memory_space=pl.ANY)
     vmem = pltpu.VMEM
     dma = pltpu.SemaphoreType.DMA
     full = lambda columns: vmem((2, depth, 2, 2, 2, 16, columns), BF16)
@@ -1021,9 +1168,12 @@
             shape((2, 16, 2304), F32),
             shape((8, width), F32),
         ),
-        in_specs=[space] * (LAYER_INPUTS + 7),
-        out_specs=tuple([space] * 5),
+        in_specs=[far, far] + [space] * 13,
+        out_specs=(far, far, space, space, space),
         scratch_shapes=[
+            vmem((length, width), BF16),
+            vmem((length, width), BF16),
+            dma((5,)),
             vmem((2, 16, 1024), BF16),
             vmem((2, 16, 2304), BF16),
             full(1024),
@@ -1037,14 +1187,15 @@
             vmem((depth, 8, width), F32),
             dma((2, Reduce.COPIES)),
         ]
-        + [dma((2, Gather.COPIES))] * 4
+        + [dma((2, Gather.COPIES))] * 5
         + scatter_scratch(2, depth, 1024)
         + scatter_scratch(2, depth, 1280)
         + scatter_scratch(1, depth, 1024)
-        + scatter_scratch(1, depth, 1024)
+        + scatter_scratch(1, depth, 512)
+        + scatter_scratch(1, depth, 512)
         + layer_scratch(length, width),
         compiler_params=pltpu.CompilerParams(
-            collective_id=0, has_side_effects=True, vmem_limit_bytes=62 * 1024 * 1024
+            collective_id=0, has_side_effects=True, vmem_limit_bytes=63 * 1024 * 1024
         ),
         name="woven",
     )(tokens, cotangent, segments, padding, *gains, *biases, *owns)

time: 202 us -> 109 us (0.54)
  Pallas kernels: 201 us -> 108 us
    pallas_call x1, Pallas kernels: 66.4 us -> 3.22 us  [write(): pl.pallas_call(write_kernel, out_shape=(shape(out.shape, BF16), shape(out...]
    pallas_call x1, Pallas kernels: 135 us -> 105 us  [woven(): pl.pallas_call(functools.partial(woven_kernel, length, depth), out_shape=...]
where the time goes in v4:
time: 109 us
  Pallas kernels  108 us (99%)
    pallas_call x1, Pallas kernels, woven(): pl.pallas_call(functools.partial(woven_kernel, length, depth), out_shape=...  105 us
    pallas_call x1, Pallas kernels, write(): pl.pallas_call(write_kernel, out_shape=(shape(out.shape, BF16), shape(out...  3.22 us

profile of v4, /device:TPU:1, one launch (start us, length us, event | category | flops | bytes accessed | tf_op | source)
XLA Modules:
  0.0 108.6 jit_solution(13313301370415844458)
XLA Ops:
  0.7 104.6 %woven.1 = (bf16[1024,512]{1,0:T(8,128)(2,1)}, bf16[1024,512]{1,0:T(8,128)(2,1)}, f32[2,16,1024]{2,1,0:T(8,128)}, f32[2,16,2304]{2,1,0:T(8,128)}, f32[8,512]{1,0:T(8,128)}) custom-call(bf16[1024,512]{1,0:T(8,128)(2,1)} %refs_0_.1, bf16[1024,512]{1,0:T(8,128)(2,1)} %refs_1_.1, s32[2,1024]{1,0:T(2,128)} %refs_2_.1, s32[2,1024]{1,0:T(2,128)} %refs_3_.1, ...), custom_call_target="tpu_custom_call" | custom-call | tf_op jit(solution)/shard_map/woven/pallas_call | solution.py:1162
  105.2 3.2 %write.1 = (bf16[1024,512]{1,0:T(8,128)(2,1)}, bf16[1024,512]{1,0:T(8,128)(2,1)}, f32[1,512]{1,0:T(1,128)}, f32[32,256]{1,0:T(8,128)}, f32[32,256]{1,0:T(8,128)}...) custom-call(bf16[1024,512]{1,0:T(8,128)(2,1)} %get-tuple-element.31., ...), custom_call_target="tpu_custom_call" | custom-call | tf_op jit(solution)/shard_map/write/pallas_call | solution.py:1131

commit v5 on v4

--- a/solution.py
+++ b/solution.py
@@ -15,6 +15,7 @@
 GROUP = 256
 TILE = 512
 WIDE = 512
+LAST = 256
 
 F32 = jnp.float32
 BF16 = jnp.bfloat16
@@ -116,13 +117,18 @@
     n1[rows, :] = (xhat * gain[...]).astype(BF16)
 
 
-def project(g, r, wa, keepc, n1, q, k, v, w):
+def project_qk(g, r, wa, n1, q, k):
     rows = pl.ds(pl.multiple_of(r * WIDE, WIDE), WIDE)
-    out = dot(n1[rows, :], flat(wa[g]))
+    out = dot(n1[rows, :], flat(wa[g, ..., 0:512]))
     q[g, rows, :] = out[:, 0:256].astype(BF16)
     k[g, rows, :] = out[:, 256:512].astype(BF16)
-    v[g, rows, :] = out[:, 512:768].astype(BF16)
-    w[g, rows, :] = (jnp.exp(out[:, 768:1024]) * twice(keepc[rows, :])).astype(BF16)
+
+
+def project_vw(g, r, wa, keepc, n1, v, w):
+    rows = pl.ds(pl.multiple_of(r * WIDE, WIDE), WIDE)
+    out = dot(n1[rows, :], flat(wa[g, ..., 512:1024]))
+    v[g, rows, :] = out[:, 0:256].astype(BF16)
+    w[g, rows, :] = (jnp.exp(out[:, 256:512]) * twice(keepc[rows, :])).astype(BF16)
 
 
 def chunk_masks(c, segc):
@@ -206,7 +212,7 @@
 
 def mix_backward(
     g, i, segc, keepc, q, k, v, w, probs, inv, score, gm, rg, uq, zgrad, kw_all, wv_all, pt_all,
-    mt_all, gy,
+    mt_all, gy, between,
 ):
     run = range(UNROLL)
     chunks = [UNROLL * i + UNROLL - 1 - n for n in run]
@@ -253,6 +259,7 @@
         added = jnp.sum(d_total[n] * back[n], axis=0, keepdims=True)
         state_z.append(state_z[n] * carry[n] + added)
     uq_low = [head_stack(state_k[n].astype(BF16)) for n in run]
+    between()
     dw = []
     for n in run:
         z_high = d_total[n].astype(BF16)
@@ -321,11 +328,10 @@
         lin[g, rows, column : column + 256] = slope.astype(BF16)
 
 
-def feed_down(r, cot, gain, down_bias, wb, keepc, act, lin, gh, gm, small):
+def feed_down(r, cot, gain, wb, keepc, lin, gh, gm, small, between):
     rows = pl.ds(pl.multiple_of(r * TILE, TILE), TILE)
     grad = cot[rows, :]
     hidden = gh[rows, :]
-    total = hidden + down_bias[...]
     back = jnp.zeros((TILE, 512), F32)
 
     def grad_of(j):
@@ -344,10 +350,9 @@
         small[row : row + 1, column : column + 256] += jnp.sum(
             grad_low.astype(F32), axis=0, keepdims=True
         )
+    between()
     for g in range(2):
-        total += dot_rt(act[g, rows, :], flat(wb[g, ..., 1280:2304]))
         back += dot_rt(lin[g, rows, :], flat(wb[g, ..., 256:1280]))
-    cot[rows, :] = total.astype(BF16)
     hat, scale = standardise(hidden)
     scaled = back * gain[...]
     inner = scaled - jnp.mean(scaled, axis=-1, keepdims=True)
@@ -363,36 +368,46 @@
         gm[g, rows, :] = (dot(low, flat(wb[g, ..., 0:256])) * keep).astype(BF16)
 
 
+def emit(r, tok, down_bias, wb, mixed, act):
+    rows = pl.ds(pl.multiple_of(r * LAST, LAST), LAST)
+    total = tok[rows, :].astype(F32)
+    for g in range(2):
+        total += dot_rt(mixed[g, rows, :], flat(wb[g, ..., 0:256]))
+    total += down_bias[...]
+    for g in range(2):
+        total += dot_rt(act[g, rows, :], flat(wb[g, ..., 1280:2304]))
+    tok[rows, :] = total.astype(BF16)
+
+
 def transpose_into(source, target, length):
     for r in range(length // 256):
         here = slice(r * 256, (r + 1) * 256)
         target[:, here] = source[here, :].astype(BF16).T
 
 
-def weight_grad(left_t, right, target, g, target_column, columns):
+def weight_grads(left_t, target, jobs):
     shape = target.shape[1:-1]
-    block = min(columns, 512)
-
-    def product(j):
-        return dot(left_t[...], right[:, j * block : (j + 1) * block]).astype(BF16)
-
-    after = product(0)
-    for j in range(columns // block):
+
+    def product(job):
+        _, right, at, _, columns = job
+        return dot(left_t[...], right[:, at : at + columns]).astype(BF16)
+
+    after = product(jobs[0])
+    for n, (g, _, _, to, columns) in enumerate(jobs):
         here = after
-        if (j + 1) * block < columns:
-            after = product(j + 1)
-        there = slice(target_column + j * block, target_column + (j + 1) * block)
-        target[g, ..., there] = here.reshape(shape + (block,))
-
-
-def finish(r, tok, gain, wa, gy, gh, small):
-    rows = pl.ds(pl.multiple_of(r * WIDE, WIDE), WIDE)
+        if n + 1 < len(jobs):
+            after = product(jobs[n + 1])
+        target[g, ..., to : to + columns] = here.reshape(shape + (columns,))
+
+
+def finish(r, tok, cot, gain, wa, gy, gh, small):
+    rows = pl.ds(pl.multiple_of(r * LAST, LAST), LAST)
     hat, scale = standardise(tok[rows, :].astype(F32))
     back = dot_rt(gy[0, rows, :], flat(wa[0])) + dot_rt(gy[1, rows, :], flat(wa[1]))
     scaled = back * gain[...]
     inner = scaled - jnp.mean(scaled, axis=-1, keepdims=True)
     inner -= hat * jnp.mean(scaled * hat, axis=-1, keepdims=True)
-    tok[rows, :] = (gh[rows, :] + scale * inner).astype(BF16)
+    cot[rows, :] = (gh[rows, :] + scale * inner).astype(BF16)
     small[1:2, :] += jnp.sum(back * hat, axis=0, keepdims=True)
 
 
@@ -400,9 +415,9 @@
     def nothing(self, *at):
         pass
 
-    before = enter = weights_a = projected = mixing = weights_up = feeding = weights_down = nothing
-    grads_down = feeding_down = layer_out = grads_mid = grads_up = nothing
-    mixing_back = mixed_back = grads_a = finishing = finished = after = nothing
+    before = enter = normalised = weights_a = projected = mixing = nothing
+    weights_up = feeding = weights_down = grads_down = feeding_down = fed = grads_up = nothing
+    mixing_back = mixed_back = grads_a = finishing = finished = gained = after = nothing
 
 
 LAYER_INPUTS = 6
@@ -465,16 +480,23 @@
     def _(r):
         normalise(r, tok, gain_one, n1)
 
+    comm.normalised()
     transpose_into(cot, flip, length)
 
     @pl.loop(0, 2)
     def _(g):
-        comm.weights_a(g)
+        comm.weights_a(g, 0)
         clear()
 
         @pl.loop(0, length // WIDE)
         def _(r):
-            project(g, r, wa, keepc, n1, q, k, v, w)
+            project_qk(g, r, wa, n1, q, k)
+
+        comm.weights_a(g, 1)
+
+        @pl.loop(0, length // WIDE)
+        def _(r):
+            project_vw(g, r, wa, keepc, n1, v, w)
 
         comm.projected(g)
 
@@ -490,6 +512,7 @@
 
     @pl.loop(0, tiles)
     def _(r):
+        comm.feeding(0, r)
         feed_in(r, tok, gain_two, wb, mixed, n2, gh)
         feed_up(0, r, up_bias, wb, n2, act, lin)
 
@@ -497,28 +520,31 @@
 
     @pl.loop(0, tiles)
     def _(r):
-        comm.feeding(r)
+        comm.feeding(1, r)
         feed_up(1, r, up_bias, wb, n2, act, lin)
 
-    for g in range(2):
-        weight_grad(flip, act.at[g], gw, g, 1280, 1024)
-    comm.grads_down()
+    for part in range(2):
+        at = part * 512
+        weight_grads(flip, gw, [(g, act.at[g], at, 1280 + at, 512) for g in range(2)])
+        comm.grads_down(part)
     comm.weights_down()
 
     @pl.loop(0, tiles)
     def _(r):
-        comm.feeding_down(r)
-        feed_down(r, cot, gain_two, down_bias, wb, keepc, act, lin, gh, gm, small)
-
-    comm.layer_out()
+        comm.feeding_down(r, 0)
+        feed_down(
+            r, cot, gain_two, wb, keepc, lin, gh, gm, small,
+            functools.partial(comm.feeding_down, r, 1),
+        )
+
+    comm.fed()
     transpose_into(n2, flip, length)
-    weight_grad(flip, lin.at[0], gw, 0, 256, 1024)
-    comm.grads_mid()
-    weight_grad(flip, lin.at[1], gw, 1, 256, 1024)
+    weight_grads(flip, gw, [(g, lin.at[g], 512, 768, 512) for g in range(2)])
+    comm.grads_up(0)
+    weight_grads(flip, gw, [(g, lin.at[g], 0, 256, 512) for g in range(2)])
     transpose_into(gh, flip, length)
-    for g in range(2):
-        weight_grad(flip, mixed.at[g], gw, g, 0, GROUP)
-    comm.grads_up()
+    weight_grads(flip, gw, [(g, mixed.at[g], 0, 0, GROUP) for g in range(2)])
+    comm.grads_up(1)
     transpose_into(n1, flip, length)
 
     @pl.loop(0, 2)
@@ -527,21 +553,31 @@
 
         @pl.loop(0, runs)
         def _(i):
-            comm.mixing_back(g, i)
+            comm.mixing_back(g, i, 0)
             mix_backward(
                 g, runs - 1 - i, segc, keepc, q, k, v, w, probs, inv, score, gm, state_v, state_k,
-                state_z, kw_all, wv_all, pt_all, mt_all, act,
+                state_z, kw_all, wv_all, pt_all, mt_all, lin,
+                functools.partial(comm.mixing_back, g, i, 1),
             )
 
         comm.mixed_back(g)
-        weight_grad(flip, act.at[g], ga, g, 0, 1024)
-        comm.grads_a(g)
-
-    @pl.loop(0, length // WIDE)
+        for part in range(2):
+            weight_grads(flip, ga, [(g, lin.at[g], part * 512, part * 512, 512)])
+            comm.grads_a(g, part)
+
+    @pl.loop(0, length // LAST)
     def _(r):
-        comm.finishing(r)
-        finish(r, tok, gain_one, wa, act, gh, small)
-        comm.finished(r)
+        comm.finishing(0, r)
+        finish(r, tok, cot, gain_one, wa, lin, gh, small)
+        comm.finished(0, r)
+
+    comm.gained()
+
+    @pl.loop(0, length // LAST)
+    def _(r):
+        comm.finishing(1, r)
+        emit(r, tok, down_bias, wb, mixed, act)
+        comm.finished(1, r)
 
     comm.after()
 
@@ -579,10 +615,10 @@
 
 def layer_kernel(length, tokens, cotangent, *refs):
     inputs, (out, grad_out), rest = refs[: LAYER_INPUTS + 2], refs[8:10], refs[10:]
-    grad_out[...] = tokens[...]
-    out[...] = cotangent[...]
+    out[...] = tokens[...]
+    grad_out[...] = cotangent[...]
     ga, gw, small = rest[:3]
-    layer_body(length, Quiet(), *inputs, ga, gw, small, grad_out, out, *rest[3:])
+    layer_body(length, Quiet(), *inputs, ga, gw, small, out, grad_out, *rest[3:])
 
 
 def layer(tokens, cotangent, seg_row, pad_row, gain_one, gain_two, up_bias, down_bias, wa, wb):
@@ -655,7 +691,6 @@
 class Copies:
     def __init__(self, sems):
         self.sems = sems
-        self.started = []
 
     def build(self, source, target, device, out_sem, in_sem):
         return pltpu.make_async_remote_copy(
@@ -673,7 +708,6 @@
             self.build(source(), target, device, number, landing).start()
 
         begin() if only is None else pl.when(only)(begin)
-        self.started.append((source, number, only))
 
     def landed(self, target, number, only=None):
         def wait():
@@ -681,14 +715,12 @@
 
         wait() if only is None else pl.when(only)(wait)
 
-    def left(self):
-        for source, number, only in self.started:
-
-            def wait(source=source, number=number):
-                part = source()
-                self.build(part, part, {"tensor": 0}, number, number).wait_send()
-
-            wait() if only is None else pl.when(only)(wait)
+    def sent(self, source, numbers, only=None):
+        def wait():
+            for number in numbers:
+                self.build(source, source, {"tensor": 0}, number, number).wait_send()
+
+        wait() if only is None else pl.when(only)(wait)
 
 
 class Gather(Copies):
@@ -766,6 +798,11 @@
         p = self.p
         for n in (9, 11, 12, 13):
             self.landed(self.block((p.y, p.x), p.other), n)
+
+    def left(self):
+        p = self.p
+        self.sent(self.own.at[0, :, self.columns], range(7), self.mine)
+        self.sent(self.block((p.y, p.x), p.t), range(7, 14))
 
 
 class Scatter(Copies):
@@ -860,6 +897,14 @@
 
         write() if self.mine is None else pl.when(self.mine)(write)
 
+    def left(self):
+        p = self.p
+        self.sent(self.pair_in, (0,))
+        self.sent(self.next_in, (1, 2, 3))
+        for core in range(2) if self.group is None else (self.group,):
+            self.sent(self.last_in.at[0], [4 + 2 * s + core for s in range(p.depth - 1)])
+        self.sent(self.last_in.at[0], (10,), self.pairs)
+
 
 def scatter_scratch(groups, depth, columns):
     vmem = pltpu.VMEM
@@ -868,7 +913,6 @@
         vmem((2, groups, depth, 16, columns), BF16),
         vmem((groups, depth, 16, columns), BF16),
         vmem((2 * depth - 1, 16, columns), BF16),
-        pltpu.SemaphoreType.DMA((2, Scatter.COPIES)),
     ]
 
 
@@ -909,29 +953,33 @@
             total += self.sums[z]
         return total
 
+    def left(self):
+        self.sent(self.own, range(6 + self.p.depth))
+
 
 class Woven:
-    def __init__(
-        self, place, owns, ends, own_a, own_b, wa, wb, ga, gw, gains, gathers, scatters, targets
-    ):
-        self.p = place
-        self.owns, self.own_a, self.own_b = owns, own_a, own_b
-        self.tokens, self.cotangent, self.out, self.grad_out, self.tok, self.cot, self.io = ends
-        every = slice(0, 1024)
-        self.a = [Gather(place, own_a, wa, g, every, gathers[g]) for g in range(2)]
-        self.b = [
-            Gather(place, own_b, wb, None, slice(768 * n, 768 * n + 768), gathers[2 + n])
-            for n in range(3)
+    def __init__(self, place, far, near, own, full, gathers, scatters, gains):
+        self.p, self.far, self.near, self.own = place, far, near, own
+        wa, wb, ga, gw = full
+        own_a, own_b = own
+        ranges = [(own_a, wa, 0, 0, 512), (own_a, wa, 0, 512, 1024), (own_a, wa, 1, 0, 1024)]
+        ranges += [(own_b, wb, None, 768 * n, 768 * n + 768) for n in range(3)]
+        gather = [
+            Gather(place, part, whole, g, slice(first, last), sems)
+            for (part, whole, g, first, last), sems in zip(ranges, gathers)
         ]
-        self.down_grad = Scatter(place, gw, None, slice(1280, 2304), *scatters[0])
-        self.up_grad = Scatter(place, gw, None, slice(0, 1280), *scatters[1])
-        self.a_grad = [Scatter(place, ga, 0, every, *scatters[2])]
-        self.a_grad += [
-            Scatter(place, ga, 1, slice(512 * n, 512 * n + 512), *scatters[3 + n])
-            for n in range(2)
+        self.a0, self.a1, self.b = gather[:2], gather[2], gather[3:]
+        ranges = [(gw, None, 1280, 1792), (gw, None, 1792, 2304)]
+        ranges += [(gw, None, 768, 1280), (gw, None, 0, 768)]
+        ranges += [(ga, 0, 0, 1024), (ga, 1, 0, 512), (ga, 1, 512, 1024)]
+        scatter = [
+            Scatter(place, part, g, slice(first, last), *buffers)
+            for (part, g, first, last), buffers in zip(ranges, scatters)
         ]
+        self.down_grad, self.up_grad = scatter[:2], scatter[2:4]
+        self.a0_grad, self.a1_grad = scatter[4], scatter[5:]
         self.gains = gains
-        self.da, self.dw = targets
+        self.everything = scatter + [gains]
 
     def table(self, at, steps):
         for place, calls in steps.items():
@@ -944,160 +992,216 @@
                 for call in calls:
                     call()
 
-    def copy(self, n):
-        here, there = (
-            (self.tokens, self.tok),
-            (self.cotangent, self.cot),
-            (self.cot, self.out),
-        )[n]
-        return pltpu.make_async_copy(here, there, self.io.at[n])
-
-    def copy_grad(self, r):
-        rows = pl.ds(pl.multiple_of(r * WIDE, WIDE), WIDE)
-        return pltpu.make_async_copy(self.tok.at[rows], self.grad_out.at[rows], self.io.at[3 + r])
+    def fetch(self, n):
+        return pltpu.make_async_copy(self.far[n], self.near[n], self.near["sems"].at[n])
+
+    def put(self, name, n):
+        return pltpu.make_async_copy(self.near[name], self.far[name], self.near["sems"].at[n])
+
+    def put_rows(self, which, r):
+        rows = pl.ds(pl.multiple_of(r * LAST, LAST), LAST)
+        source, target = ((1, "grad_out"), (0, "out"))[which]
+        return pltpu.make_async_copy(
+            self.near[source].at[rows],
+            self.far[target].at[rows],
+            self.near["sems"].at[18 + 4 * which + r],
+        )
 
     def before(self):
         self.p.knock()
-        self.copy(0).start()
-        self.copy(1).start()
-        query, key, value, slot, out_t, up, down_t = self.owns
-        halves = lambda ref: ref[...].astype(BF16).reshape(2, 16, ref.shape[1])
-        self.own_a[:, :, 0:256] = halves(query)
-        self.own_a[:, :, 256:512] = halves(key)
-        self.own_a[:, :, 512:768] = halves(value)
-        self.own_a[:, :, 768:1024] = halves(slot)
-        self.own_b[:, :, 0:256] = halves(out_t)
-        self.own_b[:, :, 256:1280] = halves(up)
-        self.own_b[:, :, 1280:2304] = halves(down_t)
+        for n in range(14, -1, -1):
+            self.fetch(n).start()
+        for n in range(2, 15):
+            self.fetch(n).wait()
+        first = self.p.t == 0
+        for rows, row in ((2, "seg_row"), (3, "pad_row")):
+            rows = self.near[rows]
+            self.near[row][...] = jnp.where(first, rows[0:1, :], rows[1:2, :])
+        own_a, own_b = self.own
+        halves = lambda n: self.near[n][...].astype(BF16).reshape(2, 16, -1)
+        for n in range(4):
+            own_a[:, :, 256 * n : 256 * n + 256] = halves(8 + n)
+        own_b[:, :, 0:256] = halves(12)
+        own_b[:, :, 256:1280] = halves(13)
+        own_b[:, :, 1280:2304] = halves(14)
 
     def enter(self):
         self.p.enter()
-        self.a[0].first()
-        self.a[1].first()
-        self.copy(0).wait()
-        self.copy(1).wait()
-
-    def weights_a(self, g):
-        one, two = self.a
-        b = self.b
+        self.a0[0].first()
+        self.a0[1].first()
+        self.fetch(0).wait()
+        self.fetch(1).wait()
+
+    def normalised(self):
+        pass
+
+    def weights_a(self, g, part):
+        one, two = self.a0
+        a1, b = self.a1, self.b
         self.table(
             (g,),
-            {
-                (0,): (
-                    one.second, b[0].first, two.second, one.third, b[1].first, two.third,
-                    one.fourth, b[0].second, one.last,
-                ),
-                (1,): (two.last, b[0].third),
-            },
+            (
+                {
+                    (0,): (
+                        one.second, a1.first, two.second, b[0].first, one.third, two.third,
+                        one.fourth, a1.second, one.last,
+                    ),
+                    (1,): (a1.fourth, a1.last),
+                },
+                {
+                    (0,): (b[1].first, two.fourth, two.last),
+                    (1,): (b[0].third,),
+                },
+            )[part],
         )
 
     def projected(self, g):
-        self.table((g,), {(0,): (self.a[1].fourth,)})
+        self.table((g,), {(0,): (self.a1.third, self.b[0].second)})
 
     def mixing(self, g, i):
-        b = self.b
-        self.table((g, i), {(0, 1): (b[1].second, b[2].first), (1, 1): (b[0].fourth, b[2].second)})
+        one, two, three = self.b
+        steps = {
+            (0, 1): (two.second, self.a0[0].left, self.a0[1].left, three.first),
+            (1, 1): (three.second, one.fourth, two.third),
+        }
+        self.table((g, i), steps)
 
     def weights_up(self, part):
-        b = self.b
+        one, two, three = self.b
         if part == 0:
-            b[1].third()
-            b[0].last()
+            one.last()
         else:
-            b[1].fourth()
-            b[1].last()
-
-    def feeding(self, r):
-        self.table((r,), {(0,): (self.b[2].third,)})
-
-    def grads_down(self):
-        self.down_grad.first()
-        self.b[2].fourth()
+            three.third()
+            two.fourth()
+            two.last()
+
+    def feeding(self, part, r):
+        pass
+
+    def grads_down(self, part):
+        if part == 0:
+            self.b[2].fourth()
+            self.a1.left()
+            self.b[0].left()
+            self.b[1].left()
+        self.down_grad[part].first()
 
     def weights_down(self):
         self.b[2].last()
-
-    def feeding_down(self, r):
-        self.table((r,), {(1,): (self.down_grad.second,)})
-
-    def layer_out(self):
-        self.copy(2).start()
-
-    def grads_mid(self):
+        self.b[2].left()
+
+    def feeding_down(self, r, part):
+        one, two = self.down_grad
+        if part == 0:
+            self.table((r,), {(1,): (two.second,)})
+        else:
+            self.table((r,), {(0,): (one.second,)})
+
+    def fed(self):
         pass
 
-    def grads_up(self):
-        self.up_grad.first()
-        self.down_grad.third()
-
-    def mixing_back(self, g, i):
-        self.table(
-            (g, i),
-            {(0, 1): (self.up_grad.second,), (1, 1): (self.a_grad[0].second,)},
-        )
+    def grads_up(self, part):
+        one, two = self.down_grad
+        self.up_grad[part].first()
+        if part == 0:
+            one.third()
+        else:
+            two.third()
+            self.up_grad[0].second()
+
+    def mixing_back(self, g, i, part):
+        up, rest = self.up_grad
+        one, two = self.down_grad
+        steps = {
+            (0, 0, 1): (one.fourth,),
+            (0, 1, 0): (rest.second,),
+            (0, 1, 1): (two.fourth, up.third),
+            (1, 0, 1): (rest.third,),
+            (1, 1, 0): (self.a0_grad.second, self.down_last, up.fourth),
+        }
+        self.table((g, i, part), steps)
 
     def mixed_back(self, g):
-        self.table((g,), {(0,): (self.down_grad.fourth,), (1,): (self.up_grad.third,)})
-
-    def grads_a(self, g):
-        one, two, three = self.a_grad
-        self.table((g,), {(0,): (one.first,), (1,): (two.first, three.first)})
-
-    def finishing(self, r):
-        one, two, three = self.a_grad
-        self.table((r,), {(1,): (two.second, one.third)})
-
-    def finished(self, r):
-        self.copy_grad(r).start()
+        self.table((g,), {(1,): (self.up_grad[1].fourth,)})
+
+    def grads_a(self, g, part):
+        one, two = self.a1_grad
+        if part == 0:
+            self.table((g,), {(1,): (one.first,)})
+        else:
+            self.table((g,), {(0,): (self.a0_grad.first,), (1,): (two.first, self.a0_grad.third)})
+
+    def finishing(self, which, r):
+        one, two = self.a1_grad
+        steps = {
+            (0, 1): (one.second,),
+            (0, 2): (two.second,),
+            (0, 3): (self.a0_grad.fourth,),
+            (1, 1): (one.third,),
+            (1, 2): (two.third,),
+            (1, 3): (one.fourth,),
+        }
+        self.table((which, r), steps)
+
+    def down_last(self):
+        dw = self.near["dw"]
+        self.down_grad[0].last(dw.at[:, :, 1280:1792])
+        self.down_grad[1].last(dw.at[:, :, 1792:2304])
+
+    def finished(self, which, r):
+        self.put_rows(which, r).start()
+
+    def gained(self):
+        self.gains.first()
 
     def after(self):
-        one, two, three = self.a_grad
-        three.second()
-        self.gains.first()
-        self.down_grad.last(self.dw.at[:, :, 1280:2304])
-        self.up_grad.fourth()
-        two.third()
-        one.fourth()
+        one, two = self.a1_grad
+        up, rest = self.up_grad
+        da, dw = self.near["da"], self.near["dw"]
         self.gains.second()
-        three.third()
         two.fourth()
-        three.fourth()
-        self.up_grad.last(self.dw.at[:, :, 0:1280])
-        one.last(self.da)
-        self.total = self.gains.last()
-        two.last(self.da.at[:, :, 0:512])
-        three.last(self.da.at[:, :, 512:1024])
-        for copies in (*self.a, *self.b, self.down_grad, self.up_grad, *self.a_grad, self.gains):
+        up.last(dw.at[:, :, 768:1280])
+        rest.last(dw.at[:, :, 0:768])
+        self.put("dw", 15).start()
+        self.near["total"][...] = self.gains.last()
+        self.put("total", 16).start()
+        self.a0_grad.last(da)
+        one.last(da.at[:, :, 0:512])
+        two.last(da.at[:, :, 512:1024])
+        self.put("da", 17).start()
+        self.everything_left()
+
+    def everything_left(self):
+        for copies in self.everything:
             copies.left()
-        self.copy(2).wait()
-        for r in range(2):
-            self.copy_grad(r).wait()
+        for r in range(4):
+            self.put_rows(0, r).wait()
+            self.put_rows(1, r).wait()
+        self.put("dw", 15).wait()
+        self.put("total", 16).wait()
+        self.put("da", 17).wait()
 
 
 def woven_kernel(length, depth, *refs):
     refs = list(refs)
     take = lambda n: [refs.pop(0) for _ in range(n)]
-    tokens, cotangent, seg_rows, pad_rows = take(4)
-    layer_inputs = take(4)
-    owns = take(7)
-    out, grad_out, da, dw, small_out = take(5)
-    tok, cot, io, own_a, own_b, wa, wb, ga, gw, seg_row, pad_row = take(11)
+    far = dict(enumerate(take(15)))
+    far.update(zip(("out", "grad_out", "da", "dw", "total"), take(5)))
+    near = dict(enumerate(take(15)))
+    near.update(zip(("da", "dw", "total", "seg_row", "pad_row", "sems"), take(6)))
+    own, full = take(2), take(4)
     small, parts, sums, gain_sems = take(4)
-    gathers = take(5)
-    scatters = [take(5) for _ in range(5)]
+    gathers = take(6)
+    scatters = [take(4) for _ in range(7)]
+    scatter_sems = gathers[:5] + take(2)
+    scatters = [buffers + [sems] for buffers, sems in zip(scatters, scatter_sems)]
     place = Place(depth)
     gains = Reduce(place, small, parts, sums, gain_sems)
-    ends = (tokens, cotangent, out, grad_out, tok, cot, io)
-    comm = Woven(
-        place, owns, ends, own_a, own_b, wa, wb, ga, gw, gains, gathers, scatters, (da, dw)
+    comm = Woven(place, far, near, own, full, gathers, scatters, gains)
+    layer_body(
+        length, comm, near["seg_row"], near["pad_row"], *[near[n] for n in range(4, 8)], *full,
+        small, near[0], near[1], *refs,
     )
-    first = lax.axis_index("tensor") == 0
-    for rows, row in ((seg_rows, seg_row), (pad_rows, pad_row)):
-        row[...] = jnp.where(first, rows[0:1, :], rows[1:2, :])
-    layer_body(
-        length, comm, seg_row, pad_row, *layer_inputs, wa, wb, ga, gw, small, tok, cot, *refs
-    )
-    small_out[...] = comm.total
 
 
 def write_kernel(out_in, grad_in, da, dw, small, *refs):
@@ -1151,54 +1255,48 @@
     )(out, grad_out, da, dw, small)
 
 
-def woven(depth, tokens, cotangent, segments, padding, gains, biases, owns):
-    length, width = tokens.shape
+def woven(depth, *inputs):
+    length, width = inputs[0].shape
     shape = jax.ShapeDtypeStruct
-    space = pl.BlockSpec(memory_space=pltpu.VMEM)
     far = pl.BlockSpec(memory_space=pl.ANY)
     vmem = pltpu.VMEM
     dma = pltpu.SemaphoreType.DMA
     full = lambda columns: vmem((2, depth, 2, 2, 2, 16, columns), BF16)
+    da, dw, total = shape((2, 16, 1024), F32), shape((2, 16, 2304), F32), shape((8, width), F32)
+    scatters = []
+    for groups, columns in ((2, 512), (2, 512), (2, 512), (2, 768), (1, 1024), (1, 512), (1, 512)):
+        scatters += scatter_scratch(groups, depth, columns)
     return pl.pallas_call(
         functools.partial(woven_kernel, length, depth),
-        out_shape=(
-            shape((length, width), BF16),
-            shape((length, width), BF16),
-            shape((2, 16, 1024), F32),
-            shape((2, 16, 2304), F32),
-            shape((8, width), F32),
-        ),
-        in_specs=[far, far] + [space] * 13,
-        out_specs=(far, far, space, space, space),
-        scratch_shapes=[
-            vmem((length, width), BF16),
-            vmem((length, width), BF16),
-            dma((5,)),
+        out_shape=(shape((length, width), BF16), shape((length, width), BF16), da, dw, total),
+        in_specs=[far] * 15,
+        out_specs=(far,) * 5,
+        scratch_shapes=[vmem(array.shape, array.dtype) for array in inputs]
+        + [vmem(array.shape, array.dtype) for array in (da, dw, total)]
+        + [
+            vmem((1, length), jnp.int32),
+            vmem((1, length), jnp.int32),
+            dma((26,)),
             vmem((2, 16, 1024), BF16),
             vmem((2, 16, 2304), BF16),
             full(1024),
             full(2304),
             full(1024),
             full(2304),
-            vmem((1, length), jnp.int32),
-            vmem((1, length), jnp.int32),
             vmem((8, width), F32),
             vmem((8, 8, width), F32),
             vmem((depth, 8, width), F32),
             dma((2, Reduce.COPIES)),
         ]
-        + [dma((2, Gather.COPIES))] * 5
-        + scatter_scratch(2, depth, 1024)
-        + scatter_scratch(2, depth, 1280)
-        + scatter_scratch(1, depth, 1024)
-        + scatter_scratch(1, depth, 512)
-        + scatter_scratch(1, depth, 512)
+        + [dma((2, Gather.COPIES))] * 6
+        + scatters
+        + [dma((2, Scatter.COPIES))] * 2
         + layer_scratch(length, width),
         compiler_params=pltpu.CompilerParams(
             collective_id=0, has_side_effects=True, vmem_limit_bytes=63 * 1024 * 1024
         ),
         name="woven",
-    )(tokens, cotangent, segments, padding, *gains, *biases, *owns)
+    )(*inputs)
 
 
 def per_device(
@@ -1228,7 +1326,7 @@
         )
         depth = lax.axis_size("dp") // 4
         results = write(
-            *woven(depth, tokens, cotangent, segment_ids, padding, gains, biases, owns)
+            *woven(depth, tokens, cotangent, segment_ids, padding, *gains, *biases, *owns)
         )
         (
             out, grad_out, gain_one, query, key, value, slot, out_t, gain_two, up, bias_one, down_t,

time: 109 us -> 101 us (0.927)
  Pallas kernels: 108 us -> 100 us
    pallas_call x1, Pallas kernels: 105 us -> 97 us  [woven(): pl.pallas_call(functools.partial(woven_kernel, length, depth), out_shape=...]
where the time goes in v5:
time: 101 us
  Pallas kernels  100 us (99%)
    pallas_call x1, Pallas kernels, woven(): pl.pallas_call(functools.partial(woven_kernel, length, depth), out_shape=...  97 us
    pallas_call x1, Pallas kernels, write(): pl.pallas_call(write_kernel, out_shape=(shape(out.shape, BF16), shape(out...  3.22 us

profile of v5, /device:TPU:1, one launch (start us, length us, event | category | flops | bytes accessed | tf_op | source)
XLA Modules:
  0.0 101.1 jit_solution(9224942883137864783)
XLA Ops:
  0.7 97.0 %woven.1 = (bf16[1024,512]{1,0:T(8,128)(2,1)}, bf16[1024,512]{1,0:T(8,128)(2,1)}, f32[2,16,1024]{2,1,0:T(8,128)}, f32[2,16,2304]{2,1,0:T(8,128)}, f32[8,512]{1,0:T(8,128)}) custom-call(bf16[1024,512]{1,0:T(8,128)(2,1)} %refs_0_.1, bf16[1024,512]{1,0:T(8,128)(2,1)} %refs_1_.1, s32[2,1024]{1,0:T(2,128)} %refs_2_.1, s32[2,1024]{1,0:T(2,128)} %refs_3_.1, ...), custom_call_target="tpu_custom_call" | custom-call | tf_op jit(solution)/shard_map/woven/pallas_call | solution.py:1269
  97.7 3.2 %write.1 = (bf16[1024,512]{1,0:T(8,128)(2,1)}, bf16[1024,512]{1,0:T(8,128)(2,1)}, f32[1,512]{1,0:T(1,128)}, f32[32,256]{1,0:T(8,128)}, f32[32,256]{1,0:T(8,128)}...) custom-call(bf16[1024,512]{1,0:T(8,128)(2,1)} %get-tuple-element.31., ...), custom_call_target="tpu_custom_call" | custom-call | tf_op jit(solution)/shard_map/write/pallas_call | solution.py:1235

commit v6 on v5

--- a/solution.py
+++ b/solution.py
@@ -111,10 +111,11 @@
         keepc[pl.ds(c * CHUNK, CHUNK), :] = 1.0 - pad.T
 
 
-def normalise(r, tok, gain, n1):
+def normalise(r, tok, cot, gain, n1, small):
     rows = pl.ds(pl.multiple_of(r * TILE, TILE), TILE)
     xhat, _ = standardise(tok[rows, :].astype(F32))
     n1[rows, :] = (xhat * gain[...]).astype(BF16)
+    small[2:3, :] += jnp.sum(cot[rows, :].astype(F32), axis=0, keepdims=True)
 
 
 def project_qk(g, r, wa, n1, q, k):
@@ -292,13 +293,14 @@
     return j // 2 % 2, (j // 4 * 2 + j % 2) * 256
 
 
-def feed_in(r, tok, gain, wb, mixed, n2, gh):
+def feed_in(r, tok, gain, wb, mixed, n2, gh, scales):
     rows = pl.ds(pl.multiple_of(r * TILE, TILE), TILE)
     hidden = tok[rows, :].astype(F32)
     for g in range(2):
         hidden += dot_rt(mixed[g, rows, :], flat(wb[g, ..., 0:256]))
-    gh[rows, :] = hidden
-    hat, _ = standardise(hidden)
+    hat, scale = standardise(hidden)
+    gh[rows, :] = hat
+    scales[rows, :] = scale
     n2[rows, :] = (hat * gain[...]).astype(BF16)
 
 
@@ -328,44 +330,53 @@
         lin[g, rows, column : column + 256] = slope.astype(BF16)
 
 
-def feed_down(r, cot, gain, wb, keepc, lin, gh, gm, small, between):
+def feed_grad(part, r, cot, wb, lin, small):
     rows = pl.ds(pl.multiple_of(r * TILE, TILE), TILE)
     grad = cot[rows, :]
-    hidden = gh[rows, :]
-    back = jnp.zeros((TILE, 512), F32)
 
     def grad_of(j):
-        g, column = divmod(j * 256, 1024)
+        g, column = units(j)
         down = flat(wb[g, ..., 1280 + column : 1536 + column])
         return dot(grad, down) * lin[g, rows, column : column + 256].astype(F32)
 
-    after = grad_of(0)
-    for j in range(8):
+    after = grad_of(4 * part)
+    for j in range(4 * part, 4 * part + 4):
         grad_low = after.astype(BF16)
-        if j < 7:
+        if j < 4 * part + 3:
             after = grad_of(j + 1)
-        g, column = divmod(j * 256, 1024)
+        g, column = units(j)
         lin[g, rows, column : column + 256] = grad_low
-        row, column = 4 + j // 2, j % 2 * 256
-        small[row : row + 1, column : column + 256] += jnp.sum(
+        row, here = 4 + 2 * g + column // 512, column % 512
+        small[row : row + 1, here : here + 256] += jnp.sum(
             grad_low.astype(F32), axis=0, keepdims=True
         )
-    between()
-    for g in range(2):
-        back += dot_rt(lin[g, rows, :], flat(wb[g, ..., 256:1280]))
-    hat, scale = standardise(hidden)
-    scaled = back * gain[...]
-    inner = scaled - jnp.mean(scaled, axis=-1, keepdims=True)
-    inner -= hat * jnp.mean(scaled * hat, axis=-1, keepdims=True)
-    grad_f32 = grad.astype(F32)
-    grad_hidden = grad_f32 + scale * inner
-    gh[rows, :] = grad_hidden
-    low = grad_hidden.astype(BF16)
-    small[0:1, :] += jnp.sum(back * hat, axis=0, keepdims=True)
-    small[2:3, :] += jnp.sum(grad_f32, axis=0, keepdims=True)
-    keep = twice(keepc[rows, :])
-    for g in range(2):
-        gm[g, rows, :] = (dot(low, flat(wb[g, ..., 0:256])) * keep).astype(BF16)
+
+
+def feed_back(r, cot, gain, wb, keepc, lin, gh, scales, gm, small):
+    half = TILE // 2
+    parts = [pl.ds(pl.multiple_of(r * TILE + n * half, half), half) for n in range(2)]
+    backs = [
+        dot_rt(lin[0, part, :], flat(wb[0, ..., 256:1280]))
+        + dot_rt(lin[1, part, :], flat(wb[1, ..., 256:1280]))
+        for part in parts
+    ]
+    hats = [gh[part, :] for part in parts]
+    keeps = [twice(keepc[part, :]) for part in parts]
+    hidden = []
+    for part, back, hat in zip(parts, backs, hats):
+        scaled = back * gain[...]
+        inner = scaled - jnp.mean(scaled, axis=-1, keepdims=True)
+        inner -= hat * jnp.mean(scaled * hat, axis=-1, keepdims=True)
+        hidden.append(cot[part, :].astype(F32) + scales[part, :] * inner)
+    mixed_grads = [
+        [(dot(rows.astype(BF16), flat(wb[g, ..., 0:256])) * keep).astype(BF16) for g in range(2)]
+        for rows, keep in zip(hidden, keeps)
+    ]
+    for n, part in enumerate(parts):
+        gh[part, :] = hidden[n]
+        for g in range(2):
+            gm[g, part, :] = mixed_grads[n][g]
+        small[0:1, :] += jnp.sum(backs[n] * hats[n], axis=0, keepdims=True)
 
 
 def emit(r, tok, down_bias, wb, mixed, act):
@@ -382,7 +393,8 @@
 def transpose_into(source, target, length):
     for r in range(length // 256):
         here = slice(r * 256, (r + 1) * 256)
-        target[:, here] = source[here, :].astype(BF16).T
+        turned = source[here, :].astype(BF16).T
+        target[..., here] = turned.reshape(target.shape[:-1] + (256,))
 
 
 def weight_grads(left_t, target, jobs):
@@ -390,7 +402,7 @@
 
     def product(job):
         _, right, at, _, columns = job
-        return dot(left_t[...], right[:, at : at + columns]).astype(BF16)
+        return dot(flat(left_t[...]), right[:, at : at + columns]).astype(BF16)
 
     after = product(jobs[0])
     for n, (g, _, _, to, columns) in enumerate(jobs):
@@ -416,11 +428,13 @@
         pass
 
     before = enter = normalised = weights_a = projected = mixing = nothing
-    weights_up = feeding = weights_down = grads_down = feeding_down = fed = grads_up = nothing
+    weights_up = feeding = weights_down = grads_down = feeding_down = grads_up = nothing
     mixing_back = mixed_back = grads_a = finishing = finished = gained = after = nothing
 
 
 LAYER_INPUTS = 6
+UP_PIECES = [(0, 768), (768, 1280)]
+DOWN_PIECES = [(1280, 1792), (1792, 2304)]
 
 
 def layer_body(
@@ -457,12 +471,13 @@
     wv_all,
     pt_all,
     mt_all,
-    n2,
     act,
     lin,
     gh,
+    scales,
     gm,
     flip,
+    n1_flip,
 ):
     runs, tiles = length // (UNROLL * CHUNK), length // TILE
 
@@ -478,10 +493,11 @@
 
     @pl.loop(0, tiles)
     def _(r):
-        normalise(r, tok, gain_one, n1)
+        normalise(r, tok, cot, gain_one, n1, small)
 
     comm.normalised()
     transpose_into(cot, flip, length)
+    transpose_into(n1, n1_flip, length)
 
     @pl.loop(0, 2)
     def _(g):
@@ -513,39 +529,40 @@
     @pl.loop(0, tiles)
     def _(r):
         comm.feeding(0, r)
-        feed_in(r, tok, gain_two, wb, mixed, n2, gh)
-        feed_up(0, r, up_bias, wb, n2, act, lin)
-
+        feed_in(r, tok, gain_two, wb, mixed, n1, gh, scales)
+        feed_up(0, r, up_bias, wb, n1, act, lin)
+
+    transpose_into(n1, ga.at[0], length)
     comm.weights_up(1)
 
     @pl.loop(0, tiles)
     def _(r):
         comm.feeding(1, r)
-        feed_up(1, r, up_bias, wb, n2, act, lin)
+        feed_up(1, r, up_bias, wb, n1, act, lin)
 
     for part in range(2):
         at = part * 512
         weight_grads(flip, gw, [(g, act.at[g], at, 1280 + at, 512) for g in range(2)])
         comm.grads_down(part)
-    comm.weights_down()
+
+    for part in range(2):
+        comm.weights_down(part)
+
+        @pl.loop(0, tiles)
+        def _(r):
+            feed_grad(part, r, cot, wb, lin, small)
 
     @pl.loop(0, tiles)
     def _(r):
-        comm.feeding_down(r, 0)
-        feed_down(
-            r, cot, gain_two, wb, keepc, lin, gh, gm, small,
-            functools.partial(comm.feeding_down, r, 1),
-        )
-
-    comm.fed()
-    transpose_into(n2, flip, length)
-    weight_grads(flip, gw, [(g, lin.at[g], 512, 768, 512) for g in range(2)])
+        comm.feeding_down(r)
+        feed_back(r, cot, gain_two, wb, keepc, lin, gh, scales, gm, small)
+
+    weight_grads(ga.at[0], gw, [(g, lin.at[g], 512, 768, 512) for g in range(2)])
     comm.grads_up(0)
-    weight_grads(flip, gw, [(g, lin.at[g], 0, 256, 512) for g in range(2)])
+    weight_grads(ga.at[0], gw, [(g, lin.at[g], 0, 256, 512) for g in range(2)])
     transpose_into(gh, flip, length)
     weight_grads(flip, gw, [(g, mixed.at[g], 0, 0, GROUP) for g in range(2)])
     comm.grads_up(1)
-    transpose_into(n1, flip, length)
 
     @pl.loop(0, 2)
     def _(g):
@@ -562,7 +579,7 @@
 
         comm.mixed_back(g)
         for part in range(2):
-            weight_grads(flip, ga, [(g, lin.at[g], part * 512, part * 512, 512)])
+            weight_grads(n1_flip, ga, [(g, lin.at[g], part * 512, part * 512, 512)])
             comm.grads_a(g, part)
 
     @pl.loop(0, length // LAST)
@@ -604,11 +621,12 @@
         vmem((2, chunks, HEAD_DIM, GROUP), BF16),
         vmem((2, length, 4 * CHUNK), BF16),
         vmem((2, length, 4 * CHUNK), BF16),
-        vmem((length, width), BF16),
         vmem((2, length, 1024), BF16),
         vmem((2, length, 1024), BF16),
         vmem((length, width), F32),
+        vmem((length, 1), F32),
         vmem((2, length, GROUP), BF16),
+        vmem((width, length), BF16),
         vmem((width, length), BF16),
     ]
 
@@ -963,14 +981,13 @@
         wa, wb, ga, gw = full
         own_a, own_b = own
         ranges = [(own_a, wa, 0, 0, 512), (own_a, wa, 0, 512, 1024), (own_a, wa, 1, 0, 1024)]
-        ranges += [(own_b, wb, None, 768 * n, 768 * n + 768) for n in range(3)]
+        ranges += [(own_b, wb, None, *part) for part in UP_PIECES + DOWN_PIECES]
         gather = [
             Gather(place, part, whole, g, slice(first, last), sems)
             for (part, whole, g, first, last), sems in zip(ranges, gathers)
         ]
         self.a0, self.a1, self.b = gather[:2], gather[2], gather[3:]
-        ranges = [(gw, None, 1280, 1792), (gw, None, 1792, 2304)]
-        ranges += [(gw, None, 768, 1280), (gw, None, 0, 768)]
+        ranges = [(gw, None, *part) for part in DOWN_PIECES + UP_PIECES[::-1]]
         ranges += [(ga, 0, 0, 1024), (ga, 1, 0, 512), (ga, 1, 512, 1024)]
         scatter = [
             Scatter(place, part, g, slice(first, last), *buffers)
@@ -1050,96 +1067,89 @@
                 },
                 {
                     (0,): (b[1].first, two.fourth, two.last),
-                    (1,): (b[0].third,),
+                    (1,): (b[0].third, b[3].first),
                 },
             )[part],
         )
 
     def projected(self, g):
-        self.table((g,), {(0,): (self.a1.third, self.b[0].second)})
+        b = self.b
+        self.table((g,), {(0,): (self.a1.third, b[0].second), (1,): (b[2].second,)})
 
     def mixing(self, g, i):
-        one, two, three = self.b
+        b = self.b
         steps = {
-            (0, 1): (two.second, self.a0[0].left, self.a0[1].left, three.first),
-            (1, 1): (three.second, one.fourth, two.third),
+            (0, 1): (b[1].second, self.a0[0].left, self.a0[1].left, b[2].first),
+            (1, 1): (b[1].third, b[0].fourth),
         }
         self.table((g, i), steps)
 
     def weights_up(self, part):
-        one, two, three = self.b
+        b = self.b
         if part == 0:
-            one.last()
+            b[3].second()
+            b[0].last()
         else:
-            three.third()
-            two.fourth()
-            two.last()
+            b[1].last()
 
     def feeding(self, part, r):
-        pass
+        b = self.b
+        steps = {(0, 1): (b[2].third, b[1].fourth), (1, 1): (b[3].third, b[2].fourth)}
+        self.table((part, r), steps)
 
     def grads_down(self, part):
-        if part == 0:
-            self.b[2].fourth()
+        if part == 1:
+            self.b[3].fourth()
+        else:
             self.a1.left()
             self.b[0].left()
             self.b[1].left()
         self.down_grad[part].first()
 
-    def weights_down(self):
-        self.b[2].last()
-        self.b[2].left()
-
-    def feeding_down(self, r, part):
+    def weights_down(self, part):
+        self.b[2 + part].last()
+        self.b[2 + part].left()
+        if part == 1:
+            self.down_grad[0].second()
+
+    def feeding_down(self, r):
         one, two = self.down_grad
-        if part == 0:
-            self.table((r,), {(1,): (two.second,)})
-        else:
-            self.table((r,), {(0,): (one.second,)})
-
-    def fed(self):
-        pass
+        self.table((r,), {(0,): (two.second,)})
 
     def grads_up(self, part):
-        one, two = self.down_grad
         self.up_grad[part].first()
-        if part == 0:
-            one.third()
-        else:
-            two.third()
-            self.up_grad[0].second()
+        self.down_grad[part].third()
 
     def mixing_back(self, g, i, part):
         up, rest = self.up_grad
         one, two = self.down_grad
         steps = {
-            (0, 0, 1): (one.fourth,),
-            (0, 1, 0): (rest.second,),
-            (0, 1, 1): (two.fourth, up.third),
-            (1, 0, 1): (rest.third,),
-            (1, 1, 0): (self.a0_grad.second, self.down_last, up.fourth),
+            (0, 0, 1): (up.second, one.fourth),
+            (0, 1, 0): (rest.second, two.fourth),
+            (1, 1, 0): (self.a0_grad.second, self.down_last),
+            (1, 1, 1): (rest.third,),
         }
         self.table((g, i, part), steps)
 
     def mixed_back(self, g):
-        self.table((g,), {(1,): (self.up_grad[1].fourth,)})
+        self.table((g,), {(1,): (self.up_grad[0].fourth,)})
 
     def grads_a(self, g, part):
         one, two = self.a1_grad
         if part == 0:
             self.table((g,), {(1,): (one.first,)})
         else:
-            self.table((g,), {(0,): (self.a0_grad.first,), (1,): (two.first, self.a0_grad.third)})
+            self.table((g,), {(0,): (self.a0_grad.first, self.up_grad[0].third), (1,): (two.first,)})
 
     def finishing(self, which, r):
         one, two = self.a1_grad
         steps = {
             (0, 1): (one.second,),
-            (0, 2): (two.second,),
-            (0, 3): (self.a0_grad.fourth,),
+            (0, 2): (self.a0_grad.third, two.second),
+            (0, 3): (self.up_grad[1].fourth,),
             (1, 1): (one.third,),
-            (1, 2): (two.third,),
-            (1, 3): (one.fourth,),
+            (1, 2): (self.a0_grad.fourth,),
+            (1, 3): (two.third,),
         }
         self.table((which, r), steps)
 
@@ -1159,6 +1169,7 @@
         up, rest = self.up_grad
         da, dw = self.near["da"], self.near["dw"]
         self.gains.second()
+        one.fourth()
         two.fourth()
         up.last(dw.at[:, :, 768:1280])
         rest.last(dw.at[:, :, 0:768])
@@ -1191,10 +1202,9 @@
     near.update(zip(("da", "dw", "total", "seg_row", "pad_row", "sems"), take(6)))
     own, full = take(2), take(4)
     small, parts, sums, gain_sems = take(4)
-    gathers = take(6)
+    gathers = take(7)
     scatters = [take(4) for _ in range(7)]
-    scatter_sems = gathers[:5] + take(2)
-    scatters = [buffers + [sems] for buffers, sems in zip(scatters, scatter_sems)]
+    scatters = [buffers + [sems] for buffers, sems in zip(scatters, gathers)]
     place = Place(depth)
     gains = Reduce(place, small, parts, sums, gain_sems)
     comm = Woven(place, far, near, own, full, gathers, scatters, gains)
@@ -1288,9 +1298,8 @@
             vmem((depth, 8, width), F32),
             dma((2, Reduce.COPIES)),
         ]
-        + [dma((2, Gather.COPIES))] * 6
+        + [dma((2, Gather.COPIES))] * 7
         + scatters
-        + [dma((2, Scatter.COPIES))] * 2
         + layer_scratch(length, width),
         compiler_params=pltpu.CompilerParams(
             collective_id=0, has_side_effects=True, vmem_limit_bytes=63 * 1024 * 1024

time: 101 us -> 97.5 us (0.965)
  Pallas kernels: 100 us -> 96.5 us
    pallas_call x1, Pallas kernels: 97 us -> 93.3 us  [woven(): pl.pallas_call(functools.partial(woven_kernel, length, depth), out_shape=...]
where the time goes in v6:
time: 97.5 us; the launch traced here: 97.3 us
  Pallas kernels  96.5 us (99%)
    pallas_call x1, Pallas kernels, woven(): pl.pallas_call(functools.partial(woven_kernel, length, depth), out_shape=...  93.3 us
    pallas_call x1, Pallas kernels, write(): pl.pallas_call(write_kernel, out_shape=(shape(out.shape, BF16), shape(out...  3.22 us

profile of v6, /device:TPU:1, one launch (start us, length us, event | category | flops | bytes accessed | tf_op | source)
XLA Modules:
  0.0 97.3 jit_solution(2433951224451037352)
XLA Ops:
  0.7 93.3 %woven.1 = (bf16[1024,512]{1,0:T(8,128)(2,1)}, bf16[1024,512]{1,0:T(8,128)(2,1)}, f32[2,16,1024]{2,1,0:T(8,128)}, f32[2,16,2304]{2,1,0:T(8,128)}, f32[8,512]{1,0:T(8,128)}) custom-call(bf16[1024,512]{1,0:T(8,128)(2,1)} %refs_0_.1, bf16[1024,512]{1,0:T(8,128)(2,1)} %refs_1_.1, s32[2,1024]{1,0:T(2,128)} %refs_2_.1, s32[2,1024]{1,0:T(2,128)} %refs_3_.1, ...), custom_call_target="tpu_custom_call" | custom-call | tf_op jit(solution)/shard_map/woven/pallas_call | solution.py:1279
  93.9 3.2 %write.1 = (bf16[1024,512]{1,0:T(8,128)(2,1)}, bf16[1024,512]{1,0:T(8,128)(2,1)}, f32[1,512]{1,0:T(1,128)}, f32[32,256]{1,0:T(8,128)}, f32[32,256]{1,0:T(8,128)}...) custom-call(bf16[1024,512]{1,0:T(8,128)(2,1)} %get-tuple-element.31., ...), custom_call_target="tpu_custom_call" | custom-call | tf_op jit(solution)/shard_map/write/pallas_call | solution.py:1245

commit v7 on v6

--- a/solution.py
+++ b/solution.py
@@ -203,7 +203,7 @@
         pt_all[g, r, :] = flip_pairs(pairs[n])
         mt_all[g, r, :] = flip_pairs(mixing[n])
         inv[g, r, :] = inverse[n]
-        score[g, r, :] = scores[n]
+        score[g, r, :] = scores[n].astype(BF16)
         probs[g, r, :] = chances[n]
         mixed[g, r, :] = (out[n] * keep[n]).astype(BF16)
     kw[...] = state_k[-1]
@@ -251,7 +251,9 @@
     weighted = [d_chance[n] * chances[n] for n in run]
     d_score = [weighted[n] - chances[n] * head_sum(weighted[n]) for n in run]
     d_pw = [(d_score[n] * inverse[n] * (HEAD_DIM**-0.5)).astype(BF16) for n in run]
-    d_total = [(weighted[n] + d_score[n] * scores[n]) * inverse[n] for n in run]
+    d_total = [
+        (weighted[n] + d_score[n] * scores[n].astype(F32)) * inverse[n] for n in run
+    ]
     d_pws = [head_stack(d_pw[n]) for n in run]
     d_pairs = [head_pairs(dot_rt(d_pws[n], wc[n]), causal[n]) for n in run]
     for n in run:
@@ -428,13 +430,14 @@
         pass
 
     before = enter = normalised = weights_a = projected = mixing = nothing
-    weights_up = feeding = weights_down = grads_down = feeding_down = grads_up = nothing
-    mixing_back = mixed_back = grads_a = finishing = finished = gained = after = nothing
+    weights_up = feeding = fed_up = weights_down = grads_down = fed_grad = feeding_down = grads_up = nothing
+    mixing_back = mixed_back = grads_a = finishing = finished = gained = grads_last = after = nothing
 
 
 LAYER_INPUTS = 6
 UP_PIECES = [(0, 768), (768, 1280)]
 DOWN_PIECES = [(1280, 1792), (1792, 2304)]
+GRAD_PIECES = DOWN_PIECES + [(256, 768), (768, 1280), (0, 256)]
 
 
 def layer_body(
@@ -540,6 +543,7 @@
         comm.feeding(1, r)
         feed_up(1, r, up_bias, wb, n1, act, lin)
 
+    comm.fed_up()
     for part in range(2):
         at = part * 512
         weight_grads(flip, gw, [(g, act.at[g], at, 1280 + at, 512) for g in range(2)])
@@ -552,17 +556,19 @@
         def _(r):
             feed_grad(part, r, cot, wb, lin, small)
 
+        comm.fed_grad(part)
+        at = part * 512
+        weight_grads(ga.at[0], gw, [(g, lin.at[g], at, 256 + at, 512) for g in range(2)])
+        comm.grads_up(part)
+
     @pl.loop(0, tiles)
     def _(r):
         comm.feeding_down(r)
         feed_back(r, cot, gain_two, wb, keepc, lin, gh, scales, gm, small)
 
-    weight_grads(ga.at[0], gw, [(g, lin.at[g], 512, 768, 512) for g in range(2)])
-    comm.grads_up(0)
-    weight_grads(ga.at[0], gw, [(g, lin.at[g], 0, 256, 512) for g in range(2)])
     transpose_into(gh, flip, length)
     weight_grads(flip, gw, [(g, mixed.at[g], 0, 0, GROUP) for g in range(2)])
-    comm.grads_up(1)
+    comm.grads_up(2)
 
     @pl.loop(0, 2)
     def _(g):
@@ -578,9 +584,14 @@
             )
 
         comm.mixed_back(g)
-        for part in range(2):
-            weight_grads(n1_flip, ga, [(g, lin.at[g], part * 512, part * 512, 512)])
-            comm.grads_a(g, part)
+
+        weight_grads(n1_flip, ga, [(g, lin.at[g], 0, 0, 512), (g, lin.at[g], 512, 512, 256)])
+
+        @pl.when(g == 0)
+        def _():
+            weight_grads(n1_flip, ga, [(0, lin.at[0], 768, 768, 256)])
+
+        comm.grads_a(g)
 
     @pl.loop(0, length // LAST)
     def _(r):
@@ -589,6 +600,8 @@
         comm.finished(0, r)
 
     comm.gained()
+    weight_grads(n1_flip, ga, [(1, lin.at[1], 768, 768, 256)])
+    comm.grads_last()
 
     @pl.loop(0, length // LAST)
     def _(r):
@@ -612,7 +625,7 @@
         vmem((2, length, GROUP), BF16),
         vmem((2, length, GROUP), F32),
         vmem((2, length, GROUP), F32),
-        vmem((2, length, GROUP), F32),
+        vmem((2, length, GROUP), BF16),
         vmem((2, length, GROUP), BF16),
         vmem((HEAD_DIM, GROUP), F32),
         vmem((HEAD_DIM, GROUP), F32),
@@ -679,6 +692,7 @@
         self.chips_z = [chip(level, y, x) for level in self.levels]
         self.to_near = {"dp": chip(z, *self.near)}
         self.to_next = {"dp": chip(z, *self.next)}
+        self.to_far = {"dp": chip(z, *self.far)}
         self.to_pair = {"tensor": self.other}
         self.spot = (y * 2 + x) * 2 + t
         flip = lambda value, bit: value + bit * (1 - 2 * value)
@@ -879,9 +893,13 @@
 
     def fourth(self):
         p = self.p
+        self.landed(self.next_in, 3)
+        self.add((p.y, p.x), self.next_in[...])
+        self.up_the_levels()
+
+    def up_the_levels(self):
+        p = self.p
         here = (p.y, p.x)
-        self.landed(self.next_in, 3)
-        self.add(here, self.next_in[...])
         for s in range(1, p.depth):
             for core in range(2) if self.group is None else (self.group,):
                 self.start(
@@ -924,6 +942,27 @@
         self.sent(self.last_in.at[0], (10,), self.pairs)
 
 
+class ShortScatter(Scatter):
+    def second(self):
+        p = self.p
+        self.landed(self.pair_in, 0)
+        for spot, target, device, number in (
+            (p.far, self.near_in.at[0], p.to_far, 1),
+            (p.near, self.near_in.at[1], p.to_near, 2),
+            (p.next, self.next_in, p.to_next, 3),
+        ):
+            self.add(spot, self.pair_in[:, :, spot[0], spot[1]])
+            self.start(lambda spot=spot: self.block(spot, p.t), target, device, number)
+        self.add((p.y, p.x), self.pair_in[:, :, p.y, p.x])
+
+    def fourth(self):
+        p = self.p
+        for part, number in ((self.next_in, 3), (self.near_in.at[1], 2), (self.near_in.at[0], 1)):
+            self.landed(part, number)
+            self.add((p.y, p.x), part[...])
+        self.up_the_levels()
+
+
 def scatter_scratch(groups, depth, columns):
     vmem = pltpu.VMEM
     return [
@@ -987,14 +1026,15 @@
             for (part, whole, g, first, last), sems in zip(ranges, gathers)
         ]
         self.a0, self.a1, self.b = gather[:2], gather[2], gather[3:]
-        ranges = [(gw, None, *part) for part in DOWN_PIECES + UP_PIECES[::-1]]
-        ranges += [(ga, 0, 0, 1024), (ga, 1, 0, 512), (ga, 1, 512, 1024)]
+        ranges = [(gw, None, *part) for part in GRAD_PIECES]
+        ranges += [(ga, 0, 0, 1024), (ga, 1, 0, 768), (ga, 1, 768, 1024)]
+        kinds = [Scatter] * 5 + [ShortScatter] * 3
         scatter = [
-            Scatter(place, part, g, slice(first, last), *buffers)
-            for (part, g, first, last), buffers in zip(ranges, scatters)
+            kind(place, part, g, slice(first, last), *buffers)
+            for kind, (part, g, first, last), buffers in zip(kinds, ranges, scatters)
         ]
-        self.down_grad, self.up_grad = scatter[:2], scatter[2:4]
-        self.a0_grad, self.a1_grad = scatter[4], scatter[5:]
+        self.down_grad, self.up_grad, self.out_grad = scatter[:2], scatter[2:4], scatter[4]
+        self.a0_grad, self.a1_grad = scatter[5], scatter[6:]
         self.gains = gains
         self.everything = scatter + [gains]
 
@@ -1094,13 +1134,14 @@
 
     def feeding(self, part, r):
         b = self.b
-        steps = {(0, 1): (b[2].third, b[1].fourth), (1, 1): (b[3].third, b[2].fourth)}
+        steps = {(0, 1): (b[2].third, b[1].fourth), (1, 1): (b[3].third,)}
         self.table((part, r), steps)
 
+    def fed_up(self):
+        self.b[2].fourth()
+
     def grads_down(self, part):
-        if part == 1:
-            self.b[3].fourth()
-        else:
+        if part == 0:
             self.a1.left()
             self.b[0].left()
             self.b[1].left()
@@ -1110,53 +1151,60 @@
         self.b[2 + part].last()
         self.b[2 + part].left()
         if part == 1:
+            self.down_grad[1].second()
+
+    def fed_grad(self, part):
+        if part == 0:
+            self.b[3].fourth()
             self.down_grad[0].second()
 
+    def grads_up(self, part):
+        if part < 2:
+            self.up_grad[part].first()
+        if part == 1:
+            self.up_grad[0].second()
+        if part == 2:
+            self.out_grad.first()
+            self.down_grad[1].third()
+            self.up_grad[1].second()
+
     def feeding_down(self, r):
+        self.table((r,), {(1,): (self.down_grad[0].third,)})
+
+    def mixing_back(self, g, i, part):
         one, two = self.down_grad
-        self.table((r,), {(0,): (two.second,)})
-
-    def grads_up(self, part):
-        self.up_grad[part].first()
-        self.down_grad[part].third()
-
-    def mixing_back(self, g, i, part):
         up, rest = self.up_grad
-        one, two = self.down_grad
         steps = {
-            (0, 0, 1): (up.second, one.fourth),
-            (0, 1, 0): (rest.second, two.fourth),
-            (1, 1, 0): (self.a0_grad.second, self.down_last),
-            (1, 1, 1): (rest.third,),
+            (0, 1, 0): (one.fourth, self.out_grad.second),
+            (0, 1, 1): (up.third,),
+            (1, 0, 1): (self.a0_grad.second, self.down_last, up.fourth),
+            (1, 1, 0): (self.out_grad.third,),
         }
         self.table((g, i, part), steps)
 
     def mixed_back(self, g):
-        self.table((g,), {(1,): (self.up_grad[0].fourth,)})
-
-    def grads_a(self, g, part):
+        self.table((g,), {(0,): (self.down_grad[1].fourth,)})
+
+    def grads_a(self, g):
         one, two = self.a1_grad
-        if part == 0:
-            self.table((g,), {(1,): (one.first,)})
-        else:
-            self.table((g,), {(0,): (self.a0_grad.first, self.up_grad[0].third), (1,): (two.first,)})
+        self.table((g,), {(0,): (self.a0_grad.first, self.up_grad[1].third), (1,): (one.first,)})
+
+    def grads_last(self):
+        self.a1_grad[1].first()
 
     def finishing(self, which, r):
         one, two = self.a1_grad
         steps = {
             (0, 1): (one.second,),
-            (0, 2): (self.a0_grad.third, two.second),
-            (0, 3): (self.up_grad[1].fourth,),
-            (1, 1): (one.third,),
-            (1, 2): (self.a0_grad.fourth,),
-            (1, 3): (two.third,),
+            (0, 2): (self.up_grad[1].fourth,),
+            (1, 0): (self.out_grad.fourth, self.a0_grad.fourth),
+            (1, 1): (two.second,),
+            (1, 3): (one.fourth,),
         }
         self.table((which, r), steps)
 
     def down_last(self):
-        dw = self.near["dw"]
-        self.down_grad[0].last(dw.at[:, :, 1280:1792])
-        self.down_grad[1].last(dw.at[:, :, 1792:2304])
+        self.down_grad[0].last(self.near["dw"].at[:, :, 1280:1792])
 
     def finished(self, which, r):
         self.put_rows(which, r).start()
@@ -1166,19 +1214,19 @@
 
     def after(self):
         one, two = self.a1_grad
-        up, rest = self.up_grad
         da, dw = self.near["da"], self.near["dw"]
         self.gains.second()
-        one.fourth()
         two.fourth()
-        up.last(dw.at[:, :, 768:1280])
-        rest.last(dw.at[:, :, 0:768])
+        self.down_grad[1].last(dw.at[:, :, 1792:2304])
+        self.up_grad[0].last(dw.at[:, :, 256:768])
+        self.up_grad[1].last(dw.at[:, :, 768:1280])
+        self.out_grad.last(dw.at[:, :, 0:256])
         self.put("dw", 15).start()
         self.near["total"][...] = self.gains.last()
         self.put("total", 16).start()
         self.a0_grad.last(da)
-        one.last(da.at[:, :, 0:512])
-        two.last(da.at[:, :, 512:1024])
+        one.last(da.at[:, :, 0:768])
+        two.last(da.at[:, :, 768:1024])
         self.put("da", 17).start()
         self.everything_left()
 
@@ -1203,8 +1251,8 @@
     own, full = take(2), take(4)
     small, parts, sums, gain_sems = take(4)
     gathers = take(7)
-    scatters = [take(4) for _ in range(7)]
-    scatters = [buffers + [sems] for buffers, sems in zip(scatters, gathers)]
+    scatters = [take(4) for _ in range(8)]
+    scatters = [buffers + [sems] for buffers, sems in zip(scatters, gathers + take(1))]
     place = Place(depth)
     gains = Reduce(place, small, parts, sums, gain_sems)
     comm = Woven(place, far, near, own, full, gathers, scatters, gains)
@@ -1274,7 +1322,7 @@
     full = lambda columns: vmem((2, depth, 2, 2, 2, 16, columns), BF16)
     da, dw, total = shape((2, 16, 1024), F32), shape((2, 16, 2304), F32), shape((8, width), F32)
     scatters = []
-    for groups, columns in ((2, 512), (2, 512), (2, 512), (2, 768), (1, 1024), (1, 512), (1, 512)):
+    for groups, columns in [(2, 512)] * 4 + [(2, 256), (1, 1024), (1, 768), (1, 256)]:
         scatters += scatter_scratch(groups, depth, columns)
     return pl.pallas_call(
         functools.partial(woven_kernel, length, depth),
@@ -1300,6 +1348,7 @@
         ]
         + [dma((2, Gather.COPIES))] * 7
         + scatters
+        + [dma((2, Scatter.COPIES))]
         + layer_scratch(length, width),
         compiler_params=pltpu.CompilerParams(
             collective_id=0, has_side_effects=True, vmem_limit_bytes=63 * 1024 * 1024

time: 97.5 us -> 95.8 us (0.983)
  Pallas kernels: 96.5 us -> 94.8 us
    pallas_call x1, Pallas kernels: 93.3 us -> 91.6 us  [woven(): pl.pallas_call(functools.partial(woven_kernel, length, depth), out_shape=...]
where the time goes in v7:
time: 95.8 us; the launch traced here: 95.6 us
  Pallas kernels  94.8 us (99%)
    pallas_call x1, Pallas kernels, woven(): pl.pallas_call(functools.partial(woven_kernel, length, depth), out_shape=...  91.6 us
    pallas_call x1, Pallas kernels, write(): pl.pallas_call(write_kernel, out_shape=(shape(out.shape, BF16), shape(out...  3.22 us

profile of v7, /device:TPU:1, one launch (start us, length us, event | category | flops | bytes accessed | tf_op | source)
XLA Modules:
  0.0 95.6 jit_solution(4375142342462026308)
XLA Ops:
  0.7 91.6 %woven.1 = (bf16[1024,512]{1,0:T(8,128)(2,1)}, bf16[1024,512]{1,0:T(8,128)(2,1)}, f32[2,16,1024]{2,1,0:T(8,128)}, f32[2,16,2304]{2,1,0:T(8,128)}, f32[8,512]{1,0:T(8,128)}) custom-call(bf16[1024,512]{1,0:T(8,128)(2,1)} %refs_0_.1, bf16[1024,512]{1,0:T(8,128)(2,1)} %refs_1_.1, s32[2,1024]{1,0:T(2,128)} %refs_2_.1, s32[2,1024]{1,0:T(2,128)} %refs_3_.1, ...), custom_call_target="tpu_custom_call" | custom-call | tf_op jit(solution)/shard_map/woven/pallas_call | solution.py:1327
  92.3 3.2 %write.1 = (bf16[1024,512]{1,0:T(8,128)(2,1)}, bf16[1024,512]{1,0:T(8,128)(2,1)}, f32[1,512]{1,0:T(1,128)}, f32[32,256]{1,0:T(8,128)}, f32[32,256]{1,0:T(8,128)}...) custom-call(bf16[1024,512]{1,0:T(8,128)(2,1)} %get-tuple-element.31., ...), custom_call_target="tpu_custom_call" | custom-call | tf_op jit(solution)/shard_map/write/pallas_call | solution.py:1293

commit v8 on v7

--- a/solution.py
+++ b/solution.py
@@ -213,7 +213,7 @@
 
 def mix_backward(
     g, i, segc, keepc, q, k, v, w, probs, inv, score, gm, rg, uq, zgrad, kw_all, wv_all, pt_all,
-    mt_all, gy, between,
+    mt_all, gy,
 ):
     run = range(UNROLL)
     chunks = [UNROLL * i + UNROLL - 1 - n for n in run]
@@ -262,7 +262,6 @@
         added = jnp.sum(d_total[n] * back[n], axis=0, keepdims=True)
         state_z.append(state_z[n] * carry[n] + added)
     uq_low = [head_stack(state_k[n].astype(BF16)) for n in run]
-    between()
     dw = []
     for n in run:
         z_high = d_total[n].astype(BF16)
@@ -576,11 +575,10 @@
 
         @pl.loop(0, runs)
         def _(i):
-            comm.mixing_back(g, i, 0)
+            comm.mixing_back(g, i)
             mix_backward(
                 g, runs - 1 - i, segc, keepc, q, k, v, w, probs, inv, score, gm, state_v, state_k,
                 state_z, kw_all, wv_all, pt_all, mt_all, lin,
-                functools.partial(comm.mixing_back, g, i, 1),
             )
 
         comm.mixed_back(g)
@@ -728,8 +726,8 @@
         return pltpu.make_async_remote_copy(
             src_ref=source,
             dst_ref=target,
-            send_sem=self.sems.at[0, out_sem],
-            recv_sem=self.sems.at[1, in_sem],
+            send_sem=self.sems[0].at[out_sem],
+            recv_sem=self.sems[1].at[in_sem],
             device_id=device,
             device_id_type=MESH,
         )
@@ -756,7 +754,7 @@
 
 
 class Gather(Copies):
-    COPIES = 14
+    SENDS, COPIES = 11, 14
 
     def __init__(self, place, own, full, group, columns, sems):
         super().__init__(sems)
@@ -772,9 +770,9 @@
     def block(self, spot, half):
         return self.at(self.groups, slice(None), spot, half)
 
-    def forward(self, spot, device, number):
+    def forward(self, spot, device, number, in_sem=None):
         block = lambda: self.block(spot, self.p.t)
-        self.start(block, block(), device, number)
+        self.start(block, block(), device, number, in_sem)
 
     def first(self):
         p = self.p
@@ -815,16 +813,17 @@
 
     def third(self):
         p = self.p
+        self.sent(self.own.at[0, :, self.columns], range(7), self.mine)
         self.landed(self.block(p.near, p.t), 7)
-        self.forward(p.near, p.to_next, 10)
-        self.forward(p.near, p.to_pair, 11)
+        self.forward(p.near, p.to_next, 0, 10)
+        self.forward(p.near, p.to_pair, 1, 11)
         self.landed(self.block(p.next, p.t), 8)
-        self.forward(p.next, p.to_pair, 12)
+        self.forward(p.next, p.to_pair, 2, 12)
 
     def fourth(self):
         p = self.p
         self.landed(self.block(p.far, p.t), 10)
-        self.forward(p.far, p.to_pair, 13)
+        self.forward(p.far, p.to_pair, 3, 13)
 
     def last(self):
         p = self.p
@@ -833,8 +832,7 @@
 
     def left(self):
         p = self.p
-        self.sent(self.own.at[0, :, self.columns], range(7), self.mine)
-        self.sent(self.block((p.y, p.x), p.t), range(7, 14))
+        self.sent(self.block((p.y, p.x), p.t), (0, 1, 2, 3, 7, 8, 9))
 
 
 class Scatter(Copies):
@@ -974,7 +972,7 @@
 
 
 class Reduce(Copies):
-    COPIES = 12
+    COPIES = 10
 
     def __init__(self, place, own, parts, sums, sems):
         super().__init__(sems)
@@ -1171,19 +1169,17 @@
     def feeding_down(self, r):
         self.table((r,), {(1,): (self.down_grad[0].third,)})
 
-    def mixing_back(self, g, i, part):
+    def mixing_back(self, g, i):
         one, two = self.down_grad
         up, rest = self.up_grad
         steps = {
-            (0, 1, 0): (one.fourth, self.out_grad.second),
-            (0, 1, 1): (up.third,),
-            (1, 0, 1): (self.a0_grad.second, self.down_last, up.fourth),
-            (1, 1, 0): (self.out_grad.third,),
+            (0, 1): (one.fourth, self.out_grad.second),
+            (1, 1): (self.a0_grad.second, self.out_grad.third, self.down_last, up.fourth),
         }
-        self.table((g, i, part), steps)
+        self.table((g, i), steps)
 
     def mixed_back(self, g):
-        self.table((g,), {(0,): (self.down_grad[1].fourth,)})
+        self.table((g,), {(0,): (self.up_grad[0].third, self.down_grad[1].fourth)})
 
     def grads_a(self, g):
         one, two = self.a1_grad
@@ -1249,10 +1245,11 @@
     near = dict(enumerate(take(15)))
     near.update(zip(("da", "dw", "total", "seg_row", "pad_row", "sems"), take(6)))
     own, full = take(2), take(4)
-    small, parts, sums, gain_sems = take(4)
-    gathers = take(7)
+    small, parts, sums = take(3)
+    gain_sems = take(2)
+    gathers = [take(2) for _ in range(7)]
     scatters = [take(4) for _ in range(8)]
-    scatters = [buffers + [sems] for buffers, sems in zip(scatters, gathers + take(1))]
+    scatters = [buffers + [sems] for buffers, sems in zip(scatters, gathers + [take(2)])]
     place = Place(depth)
     gains = Reduce(place, small, parts, sums, gain_sems)
     comm = Woven(place, far, near, own, full, gathers, scatters, gains)
@@ -1269,46 +1266,38 @@
     ) = refs
     out[...] = out_in[...]
     grad_out[...] = grad_in[...]
-    rows = lambda part: part.reshape(-1, part.shape[-1])
-    query[...] = rows(da[:, :, 0:256])
-    key[...] = rows(da[:, :, 256:512])
-    value[...] = rows(da[:, :, 512:768])
-    slot[...] = rows(da[:, :, 768:1024])
-    out_t[...] = rows(dw[:, :, 0:256])
-    up[...] = rows(dw[:, :, 256:1280])
-    down_t[...] = rows(dw[:, :, 1280:2304])
-    feed_gain[...] = small[0:1, :]
-    mixer_gain[...] = small[1:2, :]
-    down_bias[...] = small[2:3, :]
-    for row in range(4):
-        up_bias[:, row * 512 : (row + 1) * 512] = small[4 + row : 5 + row, :]
+
+    @pl.when(pl.program_id(0) == 0)
+    def _():
+        rows = lambda part: part.reshape(-1, part.shape[-1])
+        query[...] = rows(da[:, :, 0:256])
+        key[...] = rows(da[:, :, 256:512])
+        value[...] = rows(da[:, :, 512:768])
+        slot[...] = rows(da[:, :, 768:1024])
+        out_t[...] = rows(dw[:, :, 0:256])
+        up[...] = rows(dw[:, :, 256:1280])
+        down_t[...] = rows(dw[:, :, 1280:2304])
+        feed_gain[...] = small[0:1, :]
+        mixer_gain[...] = small[1:2, :]
+        down_bias[...] = small[2:3, :]
+        for row in range(4):
+            up_bias[:, row * 512 : (row + 1) * 512] = small[4 + row : 5 + row, :]
 
 
 def write(out, grad_out, da, dw, small):
     shape = jax.ShapeDtypeStruct
-    space = pl.BlockSpec(memory_space=pltpu.VMEM)
-    width = out.shape[1]
+    length, width = out.shape
     square, wide = shape((32, 256), F32), shape((32, 1024), F32)
-    row = shape((1, width), F32)
+    row, big = shape((1, width), F32), shape(out.shape, BF16)
+    outputs = (big, big, row) + (square,) * 5 + (row, wide, shape((1, 4 * width), F32), wide, row)
+    half = pl.BlockSpec((length // 2, width), lambda i: (i, 0))
+    whole = lambda array: pl.BlockSpec(array.shape, lambda i: (0,) * len(array.shape))
     return pl.pallas_call(
         write_kernel,
-        out_shape=(
-            shape(out.shape, BF16),
-            shape(out.shape, BF16),
-            row,
-            square,
-            square,
-            square,
-            square,
-            square,
-            row,
-            wide,
-            shape((1, 4 * width), F32),
-            wide,
-            row,
-        ),
-        in_specs=[space] * 5,
-        out_specs=(space,) * 13,
+        grid=(2,),
+        out_shape=outputs,
+        in_specs=[half, half, whole(da), whole(dw), whole(small)],
+        out_specs=(half, half) + tuple(whole(array) for array in outputs[2:]),
         name="write",
     )(out, grad_out, da, dw, small)
 
@@ -1344,11 +1333,12 @@
             vmem((8, width), F32),
             vmem((8, 8, width), F32),
             vmem((depth, 8, width), F32),
-            dma((2, Reduce.COPIES)),
+            dma((Reduce.COPIES,)),
+            dma((Reduce.COPIES,)),
         ]
-        + [dma((2, Gather.COPIES))] * 7
+        + [dma((Gather.SENDS,)), dma((Gather.COPIES,))] * 7
         + scatters
-        + [dma((2, Scatter.COPIES))]
+        + [dma((Scatter.COPIES,))] * 2
         + layer_scratch(length, width),
         compiler_params=pltpu.CompilerParams(
             collective_id=0, has_side_effects=True, vmem_limit_bytes=63 * 1024 * 1024

time: 95.8 us -> 94.6 us (0.987)
  Pallas kernels: 94.8 us -> 93.6 us
where the time goes in v8:
time: 94.6 us; the launch traced here: 94.4 us
  Pallas kernels  93.6 us (99%)
    pallas_call x1, Pallas kernels, woven(): pl.pallas_call(functools.partial(woven_kernel, length, depth), out_shape=...  90.7 us
    pallas_call x1, Pallas kernels, write(): pl.pallas_call(write_kernel, grid=(2,), out_shape=outputs, in_specs=[half...  2.93 us

profile of v8, /device:TPU:1, one launch (start us, length us, event | category | flops | bytes accessed | tf_op | source)
XLA Modules:
  0.0 94.4 jit_solution(7552032386097323988)
XLA Ops:
  0.7 90.7 %woven.1 = (bf16[1024,512]{1,0:T(8,128)(2,1)}, bf16[1024,512]{1,0:T(8,128)(2,1)}, f32[2,16,1024]{2,1,0:T(8,128)}, f32[2,16,2304]{2,1,0:T(8,128)}, f32[8,512]{1,0:T(8,128)}) custom-call(bf16[1024,512]{1,0:T(8,128)(2,1)} %refs_0_.1, bf16[1024,512]{1,0:T(8,128)(2,1)} %refs_1_.1, s32[2,1024]{1,0:T(2,128)} %refs_2_.1, s32[2,1024]{1,0:T(2,128)} %refs_3_.1, ...), custom_call_target="tpu_custom_call" | custom-call | tf_op jit(solution)/shard_map/woven/pallas_call | solution.py:1316
  91.3 2.9 %write.1 = (bf16[1024,512]{1,0:T(8,128)(2,1)}, bf16[1024,512]{1,0:T(8,128)(2,1)}, f32[1,512]{1,0:T(1,128)}, f32[32,256]{1,0:T(8,128)}, f32[32,256]{1,0:T(8,128)}...) custom-call(bf16[1024,512]{1,0:T(8,128)(2,1)} %get-tuple-element.31., ...), custom_call_target="tpu_custom_call" | custom-call | tf_op jit(solution)/shard_map/write/pallas_call | solution.py:1295

commit v9 on v8

--- a/solution.py
+++ b/solution.py
@@ -15,7 +15,7 @@
 GROUP = 256
 TILE = 512
 WIDE = 512
-LAST = 256
+LAST = 512
 
 F32 = jnp.float32
 BF16 = jnp.bfloat16
@@ -1026,7 +1026,7 @@
         self.a0, self.a1, self.b = gather[:2], gather[2], gather[3:]
         ranges = [(gw, None, *part) for part in GRAD_PIECES]
         ranges += [(ga, 0, 0, 1024), (ga, 1, 0, 768), (ga, 1, 768, 1024)]
-        kinds = [Scatter] * 5 + [ShortScatter] * 3
+        kinds = [Scatter] * 4 + [ShortScatter] * 4
         scatter = [
             kind(place, part, g, slice(first, last), *buffers)
             for kind, (part, g, first, last), buffers in zip(kinds, ranges, scatters)
@@ -1059,7 +1059,7 @@
         return pltpu.make_async_copy(
             self.near[source].at[rows],
             self.far[target].at[rows],
-            self.near["sems"].at[18 + 4 * which + r],
+            self.near["sems"].at[18 + 2 * which + r],
         )
 
     def before(self):
@@ -1105,20 +1105,20 @@
                 },
                 {
                     (0,): (b[1].first, two.fourth, two.last),
-                    (1,): (b[0].third, b[3].first),
+                    (1,): (b[3].first,),
                 },
             )[part],
         )
 
     def projected(self, g):
         b = self.b
-        self.table((g,), {(0,): (self.a1.third, b[0].second), (1,): (b[2].second,)})
+        self.table((g,), {(0,): (self.a1.third, b[0].second), (1,): (b[0].third,)})
 
     def mixing(self, g, i):
         b = self.b
         steps = {
             (0, 1): (b[1].second, self.a0[0].left, self.a0[1].left, b[2].first),
-            (1, 1): (b[1].third, b[0].fourth),
+            (1, 1): (b[2].second, b[1].third, b[0].fourth),
         }
         self.table((g, i), steps)
 
@@ -1174,7 +1174,7 @@
         up, rest = self.up_grad
         steps = {
             (0, 1): (one.fourth, self.out_grad.second),
-            (1, 1): (self.a0_grad.second, self.out_grad.third, self.down_last, up.fourth),
+            (1, 1): (self.a0_grad.second, self.down_last, up.fourth, self.out_grad.fourth),
         }
         self.table((g, i), steps)
 
@@ -1191,11 +1191,9 @@
     def finishing(self, which, r):
         one, two = self.a1_grad
         steps = {
-            (0, 1): (one.second,),
-            (0, 2): (self.up_grad[1].fourth,),
-            (1, 0): (self.out_grad.fourth, self.a0_grad.fourth),
+            (0, 1): (one.second, self.up_grad[1].fourth),
+            (1, 0): (self.a0_grad.fourth,),
             (1, 1): (two.second,),
-            (1, 3): (one.fourth,),
         }
         self.table((which, r), steps)
 
@@ -1211,6 +1209,7 @@
     def after(self):
         one, two = self.a1_grad
         da, dw = self.near["da"], self.near["dw"]
+        one.fourth()
         self.gains.second()
         two.fourth()
         self.down_grad[1].last(dw.at[:, :, 1792:2304])
@@ -1229,7 +1228,7 @@
     def everything_left(self):
         for copies in self.everything:
             copies.left()
-        for r in range(4):
+        for r in range(2):
             self.put_rows(0, r).wait()
             self.put_rows(1, r).wait()
         self.put("dw", 15).wait()
@@ -1323,7 +1322,7 @@
         + [
             vmem((1, length), jnp.int32),
             vmem((1, length), jnp.int32),
-            dma((26,)),
+            dma((22,)),
             vmem((2, 16, 1024), BF16),
             vmem((2, 16, 2304), BF16),
             full(1024),

time: 94.6 us -> 95.2 us (level)
  no operation moved by 1% of the time
where the time goes in v9:
time: 95.2 us; the launch traced here: 95 us
  Pallas kernels  94.2 us (99%)
    pallas_call x1, Pallas kernels, woven(): pl.pallas_call(functools.partial(woven_kernel, length, depth), out_shape=...  91.2 us
    pallas_call x1, Pallas kernels, write(): pl.pallas_call(write_kernel, grid=(2,), out_shape=outputs, in_specs=[half...  2.93 us

profile of v9, /device:TPU:1, one launch (start us, length us, event | category | flops | bytes accessed | tf_op | source)
XLA Modules:
  0.0 95.0 jit_solution(7174301077278713436)
XLA Ops:
  0.7 91.2 %woven.1 = (bf16[1024,512]{1,0:T(8,128)(2,1)}, bf16[1024,512]{1,0:T(8,128)(2,1)}, f32[2,16,1024]{2,1,0:T(8,128)}, f32[2,16,2304]{2,1,0:T(8,128)}, f32[8,512]{1,0:T(8,128)}) custom-call(bf16[1024,512]{1,0:T(8,128)(2,1)} %refs_0_.1, bf16[1024,512]{1,0:T(8,128)(2,1)} %refs_1_.1, s32[2,1024]{1,0:T(2,128)} %refs_2_.1, s32[2,1024]{1,0:T(2,128)} %refs_3_.1, ...), custom_call_target="tpu_custom_call" | custom-call | tf_op jit(solution)/shard_map/woven/pallas_call | solution.py:1315
  91.9 2.9 %write.1 = (bf16[1024,512]{1,0:T(8,128)(2,1)}, bf16[1024,512]{1,0:T(8,128)(2,1)}, f32[1,512]{1,0:T(1,128)}, f32[32,256]{1,0:T(8,128)}, f32[32,256]{1,0:T(8,128)}...) custom-call(bf16[1024,512]{1,0:T(8,128)(2,1)} %get-tuple-element.31., ...), custom_call_target="tpu_custom_call" | custom-call | tf_op jit(solution)/shard_map/write/pallas_call | solution.py:1294

commit v10 on v9

--- a/solution.py
+++ b/solution.py
@@ -1026,7 +1026,7 @@
         self.a0, self.a1, self.b = gather[:2], gather[2], gather[3:]
         ranges = [(gw, None, *part) for part in GRAD_PIECES]
         ranges += [(ga, 0, 0, 1024), (ga, 1, 0, 768), (ga, 1, 768, 1024)]
-        kinds = [Scatter] * 4 + [ShortScatter] * 4
+        kinds = [Scatter] * 5 + [ShortScatter] * 3
         scatter = [
             kind(place, part, g, slice(first, last), *buffers)
             for kind, (part, g, first, last), buffers in zip(kinds, ranges, scatters)
@@ -1105,20 +1105,20 @@
                 },
                 {
                     (0,): (b[1].first, two.fourth, two.last),
-                    (1,): (b[3].first,),
+                    (1,): (b[0].third, b[3].first),
                 },
             )[part],
         )
 
     def projected(self, g):
         b = self.b
-        self.table((g,), {(0,): (self.a1.third, b[0].second), (1,): (b[0].third,)})
+        self.table((g,), {(0,): (self.a1.third, b[0].second), (1,): (b[2].second,)})
 
     def mixing(self, g, i):
         b = self.b
         steps = {
             (0, 1): (b[1].second, self.a0[0].left, self.a0[1].left, b[2].first),
-            (1, 1): (b[2].second, b[1].third, b[0].fourth),
+            (1, 1): (b[1].third, b[0].fourth),
         }
         self.table((g, i), steps)
 
@@ -1174,7 +1174,7 @@
         up, rest = self.up_grad
         steps = {
             (0, 1): (one.fourth, self.out_grad.second),
-            (1, 1): (self.a0_grad.second, self.down_last, up.fourth, self.out_grad.fourth),
+            (1, 1): (self.a0_grad.second, self.out_grad.third, self.down_last, up.fourth),
         }
         self.table((g, i), steps)
 
@@ -1192,7 +1192,7 @@
         one, two = self.a1_grad
         steps = {
             (0, 1): (one.second, self.up_grad[1].fourth),
-            (1, 0): (self.a0_grad.fourth,),
+            (1, 0): (self.out_grad.fourth, self.a0_grad.fourth),
             (1, 1): (two.second,),
         }
         self.table((which, r), steps)

time: 95.2 us -> 94.8 us (level)
  no operation moved by 1% of the time
where the time goes in v10:
time: 94.8 us; the launch traced here: 94.6 us
  Pallas kernels  93.8 us (99%)
    pallas_call x1, Pallas kernels, woven(): pl.pallas_call(functools.partial(woven_kernel, length, depth), out_shape=...  90.9 us
    pallas_call x1, Pallas kernels, write(): pl.pallas_call(write_kernel, grid=(2,), out_shape=outputs, in_specs=[half...  2.93 us

profile of v10, /device:TPU:1, one launch (start us, length us, event | category | flops | bytes accessed | tf_op | source)
XLA Modules:
  0.0 94.6 jit_solution(4151447667755626678)
XLA Ops:
  0.7 90.9 %woven.1 = (bf16[1024,512]{1,0:T(8,128)(2,1)}, bf16[1024,512]{1,0:T(8,128)(2,1)}, f32[2,16,1024]{2,1,0:T(8,128)}, f32[2,16,2304]{2,1,0:T(8,128)}, f32[8,512]{1,0:T(8,128)}) custom-call(bf16[1024,512]{1,0:T(8,128)(2,1)} %refs_0_.1, bf16[1024,512]{1,0:T(8,128)(2,1)} %refs_1_.1, s32[2,1024]{1,0:T(2,128)} %refs_2_.1, s32[2,1024]{1,0:T(2,128)} %refs_3_.1, ...), custom_call_target="tpu_custom_call" | custom-call | tf_op jit(solution)/shard_map/woven/pallas_call | solution.py:1315
  91.5 2.9 %write.1 = (bf16[1024,512]{1,0:T(8,128)(2,1)}, bf16[1024,512]{1,0:T(8,128)(2,1)}, f32[1,512]{1,0:T(1,128)}, f32[32,256]{1,0:T(8,128)}, f32[32,256]{1,0:T(8,128)}...) custom-call(bf16[1024,512]{1,0:T(8,128)(2,1)} %get-tuple-element.31., ...), custom_call_target="tpu_custom_call" | custom-call | tf_op jit(solution)/shard_map/write/pallas_call | solution.py:1294
